TPU v7x, 32 devices: a whole 2x2x4 slice. The times are simulated.
32 devices in a mesh: grp: 4 (over y, x), mem: 8 (over z, core).
Axes of the slice: x: 2, y: 2, z: 4, core: 2. Of those that a mesh axis runs over, the one named last changes fastest.
Arguments:
- activations: bfloat16 [1024, 32, 4096], P(('grp', 'mem')), may hold values from -6 to 6
- out_grads: bfloat16 [1024, 32, 4096], P(('grp', 'mem')), may hold values from -6 to 6
- proj_in: bfloat16 [4096, 64], replicated, may hold values from -1 to 1
- proj_out: bfloat16 [4096, 64], replicated, may hold values from -1 to 1
- basis_in: float32 [64, 64], replicated, may hold values from -1 to 1
- basis_out: float32 [64, 64], replicated, may hold values from -1 to 1
- eigen: float32 [64, 64], replicated, may hold values from 0.05 to 12
- doc_ids: int32 [1024], P(('grp', 'mem')), may hold values from 0 to 255
Outputs:
- scores: float32 [1024, 1024], P(('grp', 'mem'))
All inputs are finite; a program needn't handle non-finite values.
Results may differ from a plain program's by a relative error of at most 0.0077.
Values may be sent and summed in bfloat16 or wider, within the bound.
No kernel may reach another device: no remote copies, remote signals or barrier semaphores. Data moves between devices by JAX's collectives and lax.ppermute only.
A program may use at most 192 MiB of HBM per device.

v0:
```python
import functools
import jax
import jax.numpy as jnp
from jax import lax
from jax.experimental import pallas as pl
from jax.experimental.pallas import tpu as pltpu
from jax.sharding import PartitionSpec as P

damping = 0.1
parts = 2
batch = 8
id_rows = 16
cores = 2


def dot_nn(a, b):
    return lax.dot_general(a, b, (((1,), (0,)), ((), ())), preferred_element_type=jnp.float32)


def dot_nt(a, b):
    return lax.dot_general(a, b, (((1,), (1,)), ((), ())), preferred_element_type=jnp.float32)


def split_two(value):
    high = value.astype(jnp.bfloat16)
    low = (value - high.astype(jnp.float32)).astype(jnp.bfloat16)
    return high, low


def feature_kernel(
    tokens, slices, act_hbm, grad_hbm, pin_hbm, pout_hbm, bin_hbm, bout_hbm, eigen_hbm, ids_hbm, *refs
):
    out_refs = refs[:slices]
    (act, grad, pin, pout, bin_ref, bout_ref, eigen_ref, ids_ref, act_proj, grad_proj, gt_ref, feat,
     act_sem, grad_sem, w_sem, s_sem) = refs[slices:]
    rows = act.shape[0]
    rank = bin_ref.shape[0]
    half = rank // 2
    step_rows = batch * tokens
    steps = rows // step_rows
    examples = feat.shape[1]

    part_rows = step_rows // parts

    def part_copies(step, part):
        rng = pl.ds(pl.multiple_of(step * step_rows + part * part_rows, part_rows), part_rows)
        return (
            pltpu.make_async_copy(act_hbm.at[rng], act.at[rng], act_sem.at[step, part]),
            pltpu.make_async_copy(grad_hbm.at[rng], grad.at[rng], grad_sem.at[step, part]),
        )

    weights = [
        pltpu.make_async_copy(pin_hbm, pin, w_sem.at[0]),
        pltpu.make_async_copy(pout_hbm, pout, w_sem.at[1]),
    ]
    def start_step(step):
        for part in range(parts):
            for priority, copy in enumerate(part_copies(step, part)):
                copy.start(priority=priority)

    small = [
        pltpu.make_async_copy(source, target, s_sem.at[index])
        for index, (source, target) in enumerate((
            (bin_hbm, bin_ref), (bout_hbm, bout_ref), (eigen_hbm, eigen_ref), (ids_hbm, ids_ref)))
    ]
    for copy in weights:
        copy.start()
    start_step(0)
    for copy in small:
        copy.start()
    for step in range(1, steps):
        start_step(step)
    for copy in small:
        copy.wait()

    bin_hi, bin_lo = split_two(jnp.concatenate([bin_ref[...], bin_ref[...]], axis=1))
    bout_hi, bout_lo = split_two(bout_ref[...].T)
    inverse = 1.0 / jnp.sqrt(eigen_ref[...] + damping)
    inverse = jnp.concatenate([inverse[:half], inverse[half:]], axis=1)
    own_token = (
        lax.broadcasted_iota(jnp.int32, (batch, step_rows), 1) // tokens
        == lax.broadcasted_iota(jnp.int32, (batch, step_rows), 0)
    )
    first_lanes = lax.broadcasted_iota(jnp.int32, (batch, 2 * rank), 1) < rank
    ids = jnp.concatenate([ids_ref[...]] * (2 * rank // examples), axis=1)
    place = lax.broadcasted_iota(jnp.int32, (id_rows, 2 * rank), 0) % 4
    digits = (jnp.broadcast_to(ids, (id_rows, 2 * rank)) >> (place * 8)) & 255
    digits = digits.astype(jnp.float32).astype(jnp.bfloat16)
    for copy in weights:
        copy.wait()

    def project(step):
        acts, grads = [], []
        for part in range(parts):
            for copy in part_copies(step, part):
                copy.wait()
            rng = pl.ds(pl.multiple_of(step * step_rows + part * part_rows, part_rows), part_rows)
            acts.append(dot_nt(act[rng], pin[...]).astype(jnp.bfloat16))
            grads.append(dot_nt(pout[...], grad[rng]).astype(jnp.bfloat16))
        return jnp.concatenate(acts, axis=0), jnp.concatenate(grads, axis=1)

    def rotate(step, act_part, grad_part):
        act_hi, act_lo = split_two(dot_nn(act_part, bin_hi) + dot_nn(act_part, bin_lo))
        grad_hi, grad_lo = split_two(dot_nn(bout_hi, grad_part) + dot_nn(bout_lo, grad_part))
        gt_ref[0] = grad_hi.astype(jnp.float32)
        gt_ref[1] = grad_lo.astype(jnp.float32)
        spread_hi, spread_lo = [
            jnp.concatenate([
                jnp.where(own_token, jnp.broadcast_to(gt_ref[part, pl.ds(u, 1)], (batch, step_rows)), 0.0)
                for u in range(rank)
            ], axis=0).astype(jnp.bfloat16)
            for part in range(2)
        ]
        wide = dot_nn(spread_hi, jnp.concatenate([act_hi, act_lo], axis=1))
        rotated = wide[:, :2 * rank] + wide[:, 2 * rank:] + dot_nn(spread_lo, act_hi)
        start = pl.multiple_of(step * batch, batch)
        for u in range(half):
            value = jnp.where(
                first_lanes,
                rotated[u * batch:(u + 1) * batch],
                rotated[(u + half) * batch:(u + half + 1) * batch],
            ) * inverse[u:u + 1]
            feat[u, pl.ds(start, batch)] = value

    act_proj[...], grad_proj[...] = project(0)

    def body(step, carry):
        act_part, grad_part = act_proj[...], grad_proj[...]
        act_next, grad_next = project(step)
        rotate(step - 1, act_part, grad_part)
        act_proj[...] = act_next
        grad_proj[...] = grad_next
        return carry

    lax.fori_loop(1, steps, body, 0)
    rotate(steps - 1, act_proj[...], grad_proj[...])
    depth = half // slices
    me = lax.axis_index("mem") // cores
    for index in range(slices):
        start = (me ^ index) * depth
        piece = feat[pl.ds(start, depth)].astype(jnp.bfloat16)
        out_refs[index][pl.ds(0, depth * examples)] = piece.reshape(depth * examples, 2 * rank)
        out_refs[index][pl.ds(depth * examples, id_rows)] = digits


def features(slices, activations, out_grads, proj_in, proj_out, basis_in, basis_out, eigen, doc_ids):
    examples, tokens, width = activations.shape
    rank = proj_in.shape[1]
    rows = examples * tokens
    steps = examples // batch
    half = rank // 2
    hbm = pl.BlockSpec(memory_space=pl.ANY)
    vmem = pl.BlockSpec(memory_space=pltpu.VMEM)
    return pl.pallas_call(
        functools.partial(feature_kernel, tokens, slices),
        out_shape=[
            jax.ShapeDtypeStruct((half // slices * examples + id_rows, 2 * rank), jnp.bfloat16)
        ] * slices,
        in_specs=[hbm] * 8,
        out_specs=[vmem] * slices,
        scratch_shapes=[
            pltpu.VMEM((rows, width), jnp.bfloat16),
            pltpu.VMEM((rows, width), jnp.bfloat16),
            pltpu.VMEM((rank, width), jnp.bfloat16),
            pltpu.VMEM((rank, width), jnp.bfloat16),
            pltpu.VMEM((rank, rank), jnp.float32),
            pltpu.VMEM((rank, rank), jnp.float32),
            pltpu.VMEM((rank, rank), jnp.float32),
            pltpu.VMEM((1, examples), jnp.int32),
            pltpu.VMEM((batch * tokens, rank), jnp.bfloat16),
            pltpu.VMEM((rank, batch * tokens), jnp.bfloat16),
            pltpu.VMEM((2, rank, batch * tokens), jnp.float32),
            pltpu.VMEM((half, examples, 2 * rank), jnp.float32),
            pltpu.SemaphoreType.DMA((steps, parts)),
            pltpu.SemaphoreType.DMA((steps, parts)),
            pltpu.SemaphoreType.DMA((2,)),
            pltpu.SemaphoreType.DMA((4,)),
        ],
        compiler_params=pltpu.CompilerParams(vmem_limit_bytes=60 * 2**20),
        cost_estimate=pl.CostEstimate(
            flops=4 * rows * width * rank, bytes_accessed=4 * rows * width, transcendentals=0),
        name="features",
    )(
        activations.reshape(rows, width), out_grads.reshape(rows, width),
        proj_in.T, proj_out.T, basis_in, basis_out, eigen, doc_ids.reshape(1, examples),
    )


def slice_order(slices):
    return list(range(slices))


def product_kernel(slices, pieces, examples, row_groups, column_groups, *refs):
    runs = slices // pieces
    slabs = row_groups - 1 + 2 * column_groups
    ins, outs = refs[:runs * slabs], refs[runs * slabs:runs * slabs + slices]
    column_stack, row_stack, masked = refs[runs * slabs + slices:]
    piece_rows, lanes = ins[0].shape
    piece_rows = piece_rows // pieces
    depth = (piece_rows - id_rows) // examples
    mem = lax.axis_index("mem")
    pair, core = mem // cores, mem % cores

    def place(stack, digits, row, ref, piece):
        start = pl.multiple_of(row * examples, examples)
        for part in range(depth):
            stack[pl.ds(start, examples), pl.ds(part * lanes, lanes)] = (
                ref[pl.ds(piece * piece_rows + part * examples, examples)])
        some = ref[pl.ds((piece + 1) * piece_rows - id_rows, id_rows)].astype(jnp.float32)
        some = jnp.concatenate([some] * (digits.shape[1] // lanes), axis=1)
        block = lax.broadcasted_iota(jnp.int32, digits.shape, 1) // examples
        return jnp.where(block == row, some, digits)

    column_digits = jnp.zeros((id_rows, column_stack.shape[0]), jnp.float32)
    row_digits = jnp.zeros((id_rows, row_stack.shape[0]), jnp.float32)
    for run in range(runs):
        part = ins[run * slabs:(run + 1) * slabs]
        columns, others = part[:column_groups], part[column_groups:2 * column_groups]
        rows = (columns[0],) + tuple(part[2 * column_groups:])
        for piece in range(pieces):
            place_of = pair ^ slice_order(slices)[run * pieces + piece]
            for group in range(column_groups):
                for ref, side in ((columns[group], core), (others[group], core ^ 1)):
                    column = (group * slices + place_of) * cores + side
                    column_digits = place(column_stack, column_digits, column, ref, piece)
            for group in range(row_groups):
                row = place_of * row_groups + group
                row_digits = place(row_stack, row_digits, row, rows[group], piece)

    def halves(digits):
        return (digits[0:1] + digits[1:2] * 256.0, digits[2:3] + digits[3:4] * 256.0)

    column_low, column_high = halves(column_digits)
    row_low, row_high = halves(row_digits)
    result = dot_nt(row_stack[...], column_stack[...])
    for start in range(0, row_stack.shape[0], 128):
        low, high = (
            jnp.broadcast_to(row[:, start:start + 128], (128, 128)).T[:, 0:1] for row in (row_low, row_high))
        value = result[start:start + 128]
        value = jnp.where((low == column_low) & (high == column_high), 0.0, value)
        masked[pl.ds(start, 128)] = value.astype(jnp.bfloat16)
    count = row_groups * examples
    for index in range(slices):
        start = pl.multiple_of((pair ^ index) * count, count)
        outs[index][...] = masked[pl.ds(start, count)]


def products(slabs, slices, pieces, examples, row_groups, column_groups):
    piece_rows, lanes = slabs[0].shape
    depth = (piece_rows // pieces - id_rows) // examples
    vmem = pl.BlockSpec(memory_space=pltpu.VMEM)
    rows, cols = row_groups * slices * examples, column_groups * slices * cores * examples
    return pl.pallas_call(
        functools.partial(product_kernel, slices, pieces, examples, row_groups, column_groups),
        out_shape=[jax.ShapeDtypeStruct((row_groups * examples, cols), jnp.bfloat16)] * slices,
        in_specs=[vmem] * len(slabs),
        out_specs=[vmem] * slices,
        scratch_shapes=[
            pltpu.VMEM((cols, depth * lanes), jnp.bfloat16),
            pltpu.VMEM((rows, depth * lanes), jnp.bfloat16),
            pltpu.VMEM((rows, cols), jnp.bfloat16),
        ],
        compiler_params=pltpu.CompilerParams(vmem_limit_bytes=40 * 2**20),
        cost_estimate=pl.CostEstimate(
            flops=2 * rows * cols * depth * lanes, bytes_accessed=4 * rows * cols, transcendentals=0),
        name="products",
    )(*slabs)


def total_kernel(slices, *refs):
    parts, outs = refs[:slices], refs[slices:]
    examples = outs[0].shape[0]
    for group, out in enumerate(outs):
        rng = pl.ds(group * examples, examples)
        out[...] = sum(part[rng].astype(jnp.float32) for part in parts).astype(out.dtype)


def totals(parts, examples):
    rows, cols = parts[0].shape
    groups = rows // examples
    vmem = pl.BlockSpec(memory_space=pltpu.VMEM)
    return pl.pallas_call(
        functools.partial(total_kernel, len(parts)),
        out_shape=[
            jax.ShapeDtypeStruct((examples, cols), jnp.bfloat16 if group else jnp.float32)
            for group in range(groups)
        ],
        in_specs=[vmem] * len(parts),
        out_specs=[vmem] * groups,
        compiler_params=pltpu.CompilerParams(vmem_limit_bytes=40 * 2**20),
        cost_estimate=pl.CostEstimate(
            flops=rows * cols * len(parts), bytes_accessed=8 * rows * cols, transcendentals=0),
        name="totals",
    )(*parts)


def finish_kernel(factor, column_groups, *refs):
    parts, out_ref = refs[:-1], refs[-1]
    cols = parts[0].shape[1]
    width = cols // column_groups
    grp = lax.axis_index("grp")
    for row_step, part in enumerate(parts):
        value = part[...].astype(jnp.float32) * factor
        for column_step in range(column_groups):
            start = (grp ^ row_step ^ (column_step * len(parts))) * width
            out_ref[:, pl.ds(pl.multiple_of(start, width), width)] = (
                value[:, column_step * width:(column_step + 1) * width])


def finish(parts, column_groups, factor):
    examples, cols = parts[0].shape
    vmem = pl.BlockSpec(memory_space=pltpu.VMEM)
    return pl.pallas_call(
        functools.partial(finish_kernel, factor, column_groups),
        out_shape=jax.ShapeDtypeStruct((examples, len(parts) * cols), jnp.float32),
        in_specs=[vmem] * len(parts),
        out_specs=vmem,
        compiler_params=pltpu.CompilerParams(vmem_limit_bytes=40 * 2**20),
        cost_estimate=pl.CostEstimate(
            flops=8 * examples * cols, bytes_accessed=16 * examples * cols, transcendentals=0),
        name="finish",
    )(*parts)


def swap(value, axis, size, distance):
    if distance == 0:
        return value
    return lax.ppermute(value, axis, [(place, place ^ distance) for place in range(size)])


def on_device(members, groups, activations, out_grads, proj_in, proj_out, basis_in, basis_out, eigen, doc_ids):
    examples, tokens, width = activations.shape
    rank = proj_in.shape[1]
    factor = 1.0 / (tokens * rank)
    slices = members // cores
    runs = 2
    pieces = slices // runs
    row_groups = 1 << ((groups.bit_length() - 1) // 2)
    column_groups = groups // row_groups
    feat = features(slices, activations, out_grads, proj_in, proj_out, basis_in, basis_out, eigen, doc_ids)
    got = [swap(feat[index], "mem", members, cores * index) for index in slice_order(slices)]
    slabs = []
    for run in range(runs):
        slab = jnp.concatenate(got[run * pieces:(run + 1) * pieces], axis=0)
        if run:
            slab, slabs[column_groups] = lax.optimization_barrier((slab, slabs[column_groups]))
        columns = [swap(slab, "grp", groups, row_groups * step) for step in range(column_groups)]
        rows = [swap(slab, "grp", groups, step) for step in range(1, row_groups)]
        held = lax.optimization_barrier((*columns[1:], *rows))[:column_groups - 1]
        others = [swap(column, "mem", members, 1) for column in (slab, *held)]
        slabs += columns + others + rows
    partial = products(slabs, slices, pieces, examples, row_groups, column_groups)
    parts = [swap(partial[index], "mem", members, cores * index) for index in slice_order(slices)]
    sums = totals(parts, examples)
    sums = [swap(value, "grp", groups, step) for step, value in enumerate(sums)]
    return finish(sums, column_groups, factor)


def solution(mesh):
    return jax.shard_map(
        functools.partial(on_device, mesh.shape["mem"], mesh.shape["grp"]),
        mesh=mesh,
        in_specs=(
            P(("grp", "mem"), None, None),
            P(("grp", "mem"), None, None),
            P(),
            P(),
            P(),
            P(),
            P(),
            P(("grp", "mem")),
        ),
        out_specs=P(("grp", "mem"), None),
        check_vma=False,
    )
```

profile of v0, /device:TPU:0, one launch (start us, length us, event | category | flops | bytes accessed | tf_op | source)
XLA Modules:
  0.0 47.2 jit_solution(8266376250762966085)
XLA Ops:
  0.0 12.4 %features.1 = (bf16[272,128]{1,0:T(8,128)(2,1)}, bf16[272,128]{1,0:T(8,128)(2,1)}, bf16[272,128]{1,0:T(8,128)(2,1)}, bf16[272,128]{1,0:T(8,128)(2,1)}) custom-call(bf16[1024,4096]{1,0:T(8,128)(2,1)} %bitcast.5, bf16[1024,4096]{1,0:T(8,128)(2,1)} %bitcast.6, bf16[64,4096]{1,0:T(8,128)(2,1)} %bitcast.7, bf16[64,4096]{1,0:T(8,128)(2,1)} %bitcast.8, ...), custom_call_target="tpu_custom_call" | custom-call | flops 1073741824 | bytes 16777216 | tf_op jit(solution)/shard_map/features/pallas_call | solution.py:154
  12.4 3.1 %collective-permute-start = (bf16[272,128]{1,0:T(8,128)(2,1)}, bf16[272,128]{1,0:T(8,128)(2,1)S(1)}, u32[]{:S(2)}, u32[]{:S(2)}) collective-permute-start(bf16[272,128]{1,0:T(8,128)(2,1)} %get-tuple-element.20), channel_id=1, source_target_pairs={{0,2},{1,3},{2,0},{3,1},{4,6},{5,7},{6,4},{7,5},{8,10},{9,11},{10,... | collective-permute-start | bytes 208904 | tf_op jit(solution)/shard_map/ppermute | solution.py:328
  15.5 2.6 %collective-permute-start.2 = (bf16[272,128]{1,0:T(8,128)(2,1)}, bf16[272,128]{1,0:T(8,128)(2,1)S(1)}, u32[]{:S(2)}, u32[]{:S(2)}) collective-permute-start(bf16[272,128]{1,0:T(8,128)(2,1)} %get-tuple-element.21), channel_id=1, source_target_pairs={{0,4},{1,5},{2,6},{3,7},{4,0},{5,1},{6,2},{7,3},{8,12},{9,13},{10,... | collective-permute-start | bytes 208904 | tf_op jit(solution)/shard_map/ppermute | solution.py:328
  18.1 0.9 %constant_dynamic-update-slice_fusion.1 = bf16[544,128]{1,0:T(8,128)(2,1)S(1)} fusion(bf16[272,128]{1,0:T(8,128)(2,1)} %get-tuple-element.19), kind=kLoop, calls=%fused_computation.2 | loop fusion | bytes 139264
  19.0 0.1 collective-permute-start.4
  19.1 1.8 %collective-permute-start.5 = (bf16[544,128]{1,0:T(8,128)(2,1)S(1)}, bf16[544,128]{1,0:T(8,128)(2,1)S(1)}, u32[]{:S(2)}, u32[]{:S(2)}) collective-permute-start(bf16[544,128]{1,0:T(8,128)(2,1)S(1)} %constant_dynamic-update-slice_fusion.refs_0_), channel_id=1, source_target_pairs={{0,8},{8,0},{16,24},{24,16},{1,9},{9,1},{17,25},{25,17},{2,10},{10... | collective-permute-start | bytes 417800 | tf_op jit(solution)/shard_map/ppermute | solution.py:328
  20.9 1.5 %collective-permute-start.1 = (bf16[544,128]{1,0:T(8,128)(2,1)S(1)}, bf16[544,128]{1,0:T(8,128)(2,1)S(1)}, u32[]{:S(2)}, u32[]{:S(2)}) collective-permute-start(bf16[544,128]{1,0:T(8,128)(2,1)S(1)} %constant_dynamic-update-slice_fusion.refs_0_), channel_id=1, source_target_pairs={{0,16},{8,24},{16,0},{24,8},{1,17},{9,25},{17,1},{25,9},{2,18},{10... | collective-permute-start | bytes 417800 | tf_op jit(solution)/shard_map/ppermute | solution.py:328
  22.4 0.8 %collective-permute-done.2 = bf16[272,128]{1,0:T(8,128)(2,1)S(1)} collective-permute-done((bf16[272,128]{1,0:T(8,128)(2,1)}, bf16[272,128]{1,0:T(8,128)(2,1)S(1)}, u32[]{:S(2)}, u32[]{:S(2)}) %collective-permute-start.2) | collective-permute-done | bytes 69664 | tf_op jit(solution)/shard_map/ppermute | solution.py:328
  23.2 1.3 %collective-permute-done.3 = bf16[272,128]{1,0:T(8,128)(2,1)S(1)} collective-permute-done((bf16[272,128]{1,0:T(8,128)(2,1)}, bf16[272,128]{1,0:T(8,128)(2,1)S(1)}, u32[]{:S(2)}, u32[]{:S(2)}) %collective-permute-start.3) | collective-permute-done | bytes 69664 | tf_op jit(solution)/shard_map/ppermute | solution.py:328
  24.5 1.6 %collective-permute-start.9 = (bf16[544,128]{1,0:T(8,128)(2,1)S(1)}, bf16[544,128]{1,0:T(8,128)(2,1)S(1)}, u32[]{:S(2)}, u32[]{:S(2)}) collective-permute-start(bf16[544,128]{1,0:T(8,128)(2,1)S(1)} %pad_maximum_fusion.refs_5_), channel_id=1, source_target_pairs={{0,8},{8,0},{16,24},{24,16},{1,9},{9,1},{17,25},{25,17},{2,10},{10... | collective-permute-start | bytes 417800 | tf_op jit(solution)/shard_map/ppermute | solution.py:328
  26.1 1.5 %collective-permute-start.7 = (bf16[544,128]{1,0:T(8,128)(2,1)S(1)}, bf16[544,128]{1,0:T(8,128)(2,1)S(1)}, u32[]{:S(2)}, u32[]{:S(2)}) collective-permute-start(bf16[544,128]{1,0:T(8,128)(2,1)S(1)} %pad_maximum_fusion.refs_5_), channel_id=1, source_target_pairs={{0,16},{8,24},{16,0},{24,8},{1,17},{9,25},{17,1},{25,9},{2,18},{10... | collective-permute-start | bytes 417800 | tf_op jit(solution)/shard_map/ppermute | solution.py:328
  27.6 0.5 %collective-permute-start.6 = (bf16[544,128]{1,0:T(8,128)(2,1)S(1)}, bf16[544,128]{1,0:T(8,128)(2,1)S(1)}, u32[]{:S(2)}, u32[]{:S(2)}) collective-permute-start(bf16[544,128]{1,0:T(8,128)(2,1)S(1)} %collective-permute-done.1.refs_1_), channel_id=1, source_target_pairs={{0,1},{1,0},{2,3},{3,2},{4,5},{5,4},{6,7},{7,6},{8,9},{9,8},{10,11... | collective-permute-start | bytes 417800 | tf_op jit(solution)/shard_map/ppermute | solution.py:328
  28.1 1.5 %collective-permute-done.9.refs_9_ = bf16[544,128]{1,0:T(8,128)(2,1)S(1)} collective-permute-done((bf16[544,128]{1,0:T(8,128)(2,1)S(1)}, bf16[544,128]{1,0:T(8,128)(2,1)S(1)}, u32[]{:S(2)}, u32[]{:S(2)}) %collective-permute-start.9) | collective-permute-done | bytes 139296 | tf_op jit(solution)/shard_map/ppermute | solution.py:328
  29.6 1.5 %collective-permute-done.7.refs_6_ = bf16[544,128]{1,0:T(8,128)(2,1)S(1)} collective-permute-done((bf16[544,128]{1,0:T(8,128)(2,1)S(1)}, bf16[544,128]{1,0:T(8,128)(2,1)S(1)}, u32[]{:S(2)}, u32[]{:S(2)}) %collective-permute-start.7) | collective-permute-done | bytes 139296 | tf_op jit(solution)/shard_map/ppermute | solution.py:328
  31.2 1.3 %collective-permute-done.10.refs_8_ = bf16[544,128]{1,0:T(8,128)(2,1)S(1)} collective-permute-done((bf16[544,128]{1,0:T(8,128)(2,1)S(1)}, bf16[544,128]{1,0:T(8,128)(2,1)S(1)}, u32[]{:S(2)}, u32[]{:S(2)}) %collective-permute-start.10) | collective-permute-done | bytes 139296 | tf_op jit(solution)/shard_map/ppermute | solution.py:328
  32.5 0.7 %products.1 = (bf16[64,512]{1,0:T(8,128)(2,1)S(1)}, bf16[64,512]{1,0:T(8,128)(2,1)S(1)}, bf16[64,512]{1,0:T(8,128)(2,1)S(1)}, bf16[64,512]{1,0:T(8,128)(2,1)S(1)}) custom-call(bf16[544,128]{1,0:T(8,128)(2,1)S(1)} %constant_dynamic-update-slice_fusion.refs_0_, bf16[544,128]{1,0:T(8,128)(2,1)S(1)} %collective-permute-done.1.refs_1_, ...), custom_call_target="tpu_custom_call" | custom-call | flops 268435456 | bytes 524288 | tf_op jit(solution)/shard_map/products/pallas_call | solution.py:253
  33.3 0.8 %collective-permute-start.11 = (bf16[64,512]{1,0:T(8,128)(2,1)S(1)}, bf16[64,512]{1,0:T(8,128)(2,1)S(1)}, u32[]{:S(2)}, u32[]{:S(2)}) collective-permute-start(bf16[64,512]{1,0:T(8,128)(2,1)S(1)} %get-tuple-element.28), channel_id=1, source_target_pairs={{0,2},{1,3},{2,0},{3,1},{4,6},{5,7},{6,4},{7,5},{8,10},{9,11},{10,... | collective-permute-start | bytes 196616 | tf_op jit(solution)/shard_map/ppermute | solution.py:328
  34.1 1.8 %collective-permute-start.12 = (bf16[64,512]{1,0:T(8,128)(2,1)S(1)}, bf16[64,512]{1,0:T(8,128)(2,1)S(1)}, u32[]{:S(2)}, u32[]{:S(2)}) collective-permute-start(bf16[64,512]{1,0:T(8,128)(2,1)S(1)} %get-tuple-element.29), channel_id=1, source_target_pairs={{0,4},{1,5},{2,6},{3,7},{4,0},{5,1},{6,2},{7,3},{8,12},{9,13},{10,... | collective-permute-start | bytes 196616 | tf_op jit(solution)/shard_map/ppermute | solution.py:328
  35.9 1.8 %collective-permute-start.13 = (bf16[64,512]{1,0:T(8,128)(2,1)S(1)}, bf16[64,512]{1,0:T(8,128)(2,1)S(1)}, u32[]{:S(2)}, u32[]{:S(2)}) collective-permute-start(bf16[64,512]{1,0:T(8,128)(2,1)S(1)} %get-tuple-element.30), channel_id=1, source_target_pairs={{0,6},{1,7},{2,4},{3,5},{4,2},{5,3},{6,0},{7,1},{8,14},{9,15},{10,... | collective-permute-start | bytes 196616 | tf_op jit(solution)/shard_map/ppermute | solution.py:328
  37.7 0.6 %collective-permute-done.11.refs_1_ = bf16[64,512]{1,0:T(8,128)(2,1)S(1)} collective-permute-done((bf16[64,512]{1,0:T(8,128)(2,1)S(1)}, bf16[64,512]{1,0:T(8,128)(2,1)S(1)}, u32[]{:S(2)}, u32[]{:S(2)}) %collective-permute-start.11) | collective-permute-done | bytes 65568 | tf_op jit(solution)/shard_map/ppermute | solution.py:328
  38.3 4.2 %collective-permute-done.12.refs_2_ = bf16[64,512]{1,0:T(8,128)(2,1)S(1)} collective-permute-done((bf16[64,512]{1,0:T(8,128)(2,1)S(1)}, bf16[64,512]{1,0:T(8,128)(2,1)S(1)}, u32[]{:S(2)}, u32[]{:S(2)}) %collective-permute-start.12) | collective-permute-done | bytes 65568 | tf_op jit(solution)/shard_map/ppermute | solution.py:328
  42.5 0.6 %collective-permute-start.14 = (bf16[32,512]{1,0:T(8,128)(2,1)S(1)}, bf16[32,512]{1,0:T(8,128)(2,1)S(1)}, u32[]{:S(2)}, u32[]{:S(2)}) collective-permute-start(bf16[32,512]{1,0:T(8,128)(2,1)S(1)} %get-tuple-element.32), channel_id=1, source_target_pairs={{0,8},{8,0},{16,24},{24,16},{1,9},{9,1},{17,25},{25,17},{2,10},{10... | collective-permute-start | bytes 98312 | tf_op jit(solution)/shard_map/ppermute | solution.py:328
  43.1 3.4 %collective-permute-done.14.refs_1_ = bf16[32,512]{1,0:T(8,128)(2,1)S(1)} collective-permute-done((bf16[32,512]{1,0:T(8,128)(2,1)S(1)}, bf16[32,512]{1,0:T(8,128)(2,1)S(1)}, u32[]{:S(2)}, u32[]{:S(2)}) %collective-permute-start.14) | collective-permute-done | bytes 32800 | tf_op jit(solution)/shard_map/ppermute | solution.py:328
  46.5 0.7 %finish.1 = f32[32,1024]{1,0:T(8,128)} custom-call(f32[32,512]{1,0:T(8,128)S(1)} %get-tuple-element.31.refs_0_, bf16[32,512]{1,0:T(8,128)(2,1)S(1)} %collective-permute-done.14.refs_1_), custom_call_target="tpu_custom_call" | custom-call | flops 131072 | bytes 262144 | tf_op jit(solution)/shard_map/finish/pallas_call | solution.py:313
  (13 shorter events, 0.1 us)
Async XLA Ops:
  12.4 6.5 %collective-permute-start = (bf16[272,128]{1,0:T(8,128)(2,1)}, bf16[272,128]{1,0:T(8,128)(2,1)S(1)}, u32[]{:S(2)}, u32[]{:S(2)}) collective-permute-start(bf16[272,128]{1,0:T(8,128)(2,1)} %get-tuple-element.20), channel_id=1, source_target_pairs={{0,2},{1,3},{2,0},{3,1},{4,6},{5,7},{6,4},{7,5},{8,10},{9,11},{10,... | collective-permute-start | bytes 208904 | tf_op jit(solution)/shard_map/ppermute | solution.py:328
  15.5 7.7 %collective-permute-start.2 = (bf16[272,128]{1,0:T(8,128)(2,1)}, bf16[272,128]{1,0:T(8,128)(2,1)S(1)}, u32[]{:S(2)}, u32[]{:S(2)}) collective-permute-start(bf16[272,128]{1,0:T(8,128)(2,1)} %get-tuple-element.21), channel_id=1, source_target_pairs={{0,4},{1,5},{2,6},{3,7},{4,0},{5,1},{6,2},{7,3},{8,12},{9,13},{10,... | collective-permute-start | bytes 208904 | tf_op jit(solution)/shard_map/ppermute | solution.py:328
  18.1 6.4 %collective-permute-start.3 = (bf16[272,128]{1,0:T(8,128)(2,1)}, bf16[272,128]{1,0:T(8,128)(2,1)S(1)}, u32[]{:S(2)}, u32[]{:S(2)}) collective-permute-start(bf16[272,128]{1,0:T(8,128)(2,1)} %get-tuple-element.22), channel_id=1, source_target_pairs={{0,6},{1,7},{2,4},{3,5},{4,2},{5,3},{6,0},{7,1},{8,14},{9,15},{10,... | collective-permute-start | bytes 208904 | tf_op jit(solution)/shard_map/ppermute | solution.py:328
  19.0 5.5 %collective-permute-start.4 = (bf16[544,128]{1,0:T(8,128)(2,1)S(1)}, bf16[544,128]{1,0:T(8,128)(2,1)S(1)}, u32[]{:S(2)}, u32[]{:S(2)}) collective-permute-start(bf16[544,128]{1,0:T(8,128)(2,1)S(1)} %constant_dynamic-update-slice_fusion.refs_0_), channel_id=1, source_target_pairs={{0,1},{1,0},{2,3},{3,2},{4,5},{5,4},{6,7},{7,6},{8,9},{9,8},{10,11... | collective-permute-start | bytes 417800 | tf_op jit(solution)/shard_map/ppermute | solution.py:328
  19.1 8.6 %collective-permute-start.5 = (bf16[544,128]{1,0:T(8,128)(2,1)S(1)}, bf16[544,128]{1,0:T(8,128)(2,1)S(1)}, u32[]{:S(2)}, u32[]{:S(2)}) collective-permute-start(bf16[544,128]{1,0:T(8,128)(2,1)S(1)} %constant_dynamic-update-slice_fusion.refs_0_), channel_id=1, source_target_pairs={{0,8},{8,0},{16,24},{24,16},{1,9},{9,1},{17,25},{25,17},{2,10},{10... | collective-permute-start | bytes 417800 | tf_op jit(solution)/shard_map/ppermute | solution.py:328
  20.9 6.8 %collective-permute-start.1 = (bf16[544,128]{1,0:T(8,128)(2,1)S(1)}, bf16[544,128]{1,0:T(8,128)(2,1)S(1)}, u32[]{:S(2)}, u32[]{:S(2)}) collective-permute-start(bf16[544,128]{1,0:T(8,128)(2,1)S(1)} %constant_dynamic-update-slice_fusion.refs_0_), channel_id=1, source_target_pairs={{0,16},{8,24},{16,0},{24,8},{1,17},{9,25},{17,1},{25,9},{2,18},{10... | collective-permute-start | bytes 417800 | tf_op jit(solution)/shard_map/ppermute | solution.py:328
  24.5 5.1 %collective-permute-start.9 = (bf16[544,128]{1,0:T(8,128)(2,1)S(1)}, bf16[544,128]{1,0:T(8,128)(2,1)S(1)}, u32[]{:S(2)}, u32[]{:S(2)}) collective-permute-start(bf16[544,128]{1,0:T(8,128)(2,1)S(1)} %pad_maximum_fusion.refs_5_), channel_id=1, source_target_pairs={{0,8},{8,0},{16,24},{24,16},{1,9},{9,1},{17,25},{25,17},{2,10},{10... | collective-permute-start | bytes 417800 | tf_op jit(solution)/shard_map/ppermute | solution.py:328
  26.1 5.1 %collective-permute-start.7 = (bf16[544,128]{1,0:T(8,128)(2,1)S(1)}, bf16[544,128]{1,0:T(8,128)(2,1)S(1)}, u32[]{:S(2)}, u32[]{:S(2)}) collective-permute-start(bf16[544,128]{1,0:T(8,128)(2,1)S(1)} %pad_maximum_fusion.refs_5_), channel_id=1, source_target_pairs={{0,16},{8,24},{16,0},{24,8},{1,17},{9,25},{17,1},{25,9},{2,18},{10... | collective-permute-start | bytes 417800 | tf_op jit(solution)/shard_map/ppermute | solution.py:328
  27.6 3.5 %collective-permute-start.8 = (bf16[544,128]{1,0:T(8,128)(2,1)S(1)}, bf16[544,128]{1,0:T(8,128)(2,1)S(1)}, u32[]{:S(2)}, u32[]{:S(2)}) collective-permute-start(bf16[544,128]{1,0:T(8,128)(2,1)S(1)} %pad_maximum_fusion.refs_5_), channel_id=1, source_target_pairs={{0,1},{1,0},{2,3},{3,2},{4,5},{5,4},{6,7},{7,6},{8,9},{9,8},{10,11... | collective-permute-start | bytes 417800 | tf_op jit(solution)/shard_map/ppermute | solution.py:328
  27.6 3.5 %collective-permute-start.6 = (bf16[544,128]{1,0:T(8,128)(2,1)S(1)}, bf16[544,128]{1,0:T(8,128)(2,1)S(1)}, u32[]{:S(2)}, u32[]{:S(2)}) collective-permute-start(bf16[544,128]{1,0:T(8,128)(2,1)S(1)} %collective-permute-done.1.refs_1_), channel_id=1, source_target_pairs={{0,1},{1,0},{2,3},{3,2},{4,5},{5,4},{6,7},{7,6},{8,9},{9,8},{10,11... | collective-permute-start | bytes 417800 | tf_op jit(solution)/shard_map/ppermute | solution.py:328
  31.2 1.4 %collective-permute-start.10 = (bf16[544,128]{1,0:T(8,128)(2,1)S(1)}, bf16[544,128]{1,0:T(8,128)(2,1)S(1)}, u32[]{:S(2)}, u32[]{:S(2)}) collective-permute-start(bf16[544,128]{1,0:T(8,128)(2,1)S(1)} %collective-permute-done.7.refs_6_), channel_id=1, source_target_pairs={{0,1},{1,0},{2,3},{3,2},{4,5},{5,4},{6,7},{7,6},{8,9},{9,8},{10,11... | collective-permute-start | bytes 417800 | tf_op jit(solution)/shard_map/ppermute | solution.py:328
  33.3 5.0 %collective-permute-start.11 = (bf16[64,512]{1,0:T(8,128)(2,1)S(1)}, bf16[64,512]{1,0:T(8,128)(2,1)S(1)}, u32[]{:S(2)}, u32[]{:S(2)}) collective-permute-start(bf16[64,512]{1,0:T(8,128)(2,1)S(1)} %get-tuple-element.28), channel_id=1, source_target_pairs={{0,2},{1,3},{2,0},{3,1},{4,6},{5,7},{6,4},{7,5},{8,10},{9,11},{10,... | collective-permute-start | bytes 196616 | tf_op jit(solution)/shard_map/ppermute | solution.py:328
  34.1 8.4 %collective-permute-start.12 = (bf16[64,512]{1,0:T(8,128)(2,1)S(1)}, bf16[64,512]{1,0:T(8,128)(2,1)S(1)}, u32[]{:S(2)}, u32[]{:S(2)}) collective-permute-start(bf16[64,512]{1,0:T(8,128)(2,1)S(1)} %get-tuple-element.29), channel_id=1, source_target_pairs={{0,4},{1,5},{2,6},{3,7},{4,0},{5,1},{6,2},{7,3},{8,12},{9,13},{10,... | collective-permute-start | bytes 196616 | tf_op jit(solution)/shard_map/ppermute | solution.py:328
  35.9 6.5 %collective-permute-start.13 = (bf16[64,512]{1,0:T(8,128)(2,1)S(1)}, bf16[64,512]{1,0:T(8,128)(2,1)S(1)}, u32[]{:S(2)}, u32[]{:S(2)}) collective-permute-start(bf16[64,512]{1,0:T(8,128)(2,1)S(1)} %get-tuple-element.30), channel_id=1, source_target_pairs={{0,6},{1,7},{2,4},{3,5},{4,2},{5,3},{6,0},{7,1},{8,14},{9,15},{10,... | collective-permute-start | bytes 196616 | tf_op jit(solution)/shard_map/ppermute | solution.py:328
  42.5 4.0 %collective-permute-start.14 = (bf16[32,512]{1,0:T(8,128)(2,1)S(1)}, bf16[32,512]{1,0:T(8,128)(2,1)S(1)}, u32[]{:S(2)}, u32[]{:S(2)}) collective-permute-start(bf16[32,512]{1,0:T(8,128)(2,1)S(1)} %get-tuple-element.32), channel_id=1, source_target_pairs={{0,8},{8,0},{16,24},{24,16},{1,9},{9,1},{17,25},{25,17},{2,10},{10... | collective-permute-start | bytes 98312 | tf_op jit(solution)/shard_map/ppermute | solution.py:328
where the time goes:
time: 47.3 us; the launch traced here: 47.2 us
  starting transfers between devices  17.7 us (37%)
  waiting for transfers between devices  14.6 us (31%)
  Pallas kernels  13.9 us (29%)
  local copies, waits for them, and re-layouts  0.9 us (2%)
    ppermute x15, starting transfers between devices, swap(): lax.ppermute(value, axis, [(place, place ^ distance) for place in range(s...  17.7 us
    ppermute x15, waiting for transfers between devices, swap(): lax.ppermute(value, axis, [(place, place ^ distance) for place in range(s...  14.6 us
    pallas_call x1, Pallas kernels, features(): pl.pallas_call(functools.partial(feature_kernel, tokens, slices), out_sha...  12.4 us
  transfers between devices with their start and end apart: 15, of which 8 were waited for; matrix products, arithmetic and copies ran while one was open for 2% of the time, Pallas kernels for 0%

commit v1 on v0

--- a/solution.py
+++ b/solution.py
@@ -7,7 +7,6 @@
 from jax.sharding import PartitionSpec as P
 
 damping = 0.1
-parts = 2
 batch = 8
 id_rows = 16
 cores = 2
@@ -33,20 +32,18 @@
     out_refs = refs[:slices]
     (act, grad, pin, pout, bin_ref, bout_ref, eigen_ref, ids_ref, act_proj, grad_proj, gt_ref, feat,
      act_sem, grad_sem, w_sem, s_sem) = refs[slices:]
-    rows = act.shape[0]
+    rows, width = act.shape
     rank = bin_ref.shape[0]
     half = rank // 2
     step_rows = batch * tokens
     steps = rows // step_rows
     examples = feat.shape[1]
 
-    part_rows = step_rows // parts
-
-    def part_copies(step, part):
-        rng = pl.ds(pl.multiple_of(step * step_rows + part * part_rows, part_rows), part_rows)
+    def step_copies(step):
+        rng = pl.ds(pl.multiple_of(step * step_rows, step_rows), step_rows)
         return (
-            pltpu.make_async_copy(act_hbm.at[rng], act.at[rng], act_sem.at[step, part]),
-            pltpu.make_async_copy(grad_hbm.at[rng], grad.at[rng], grad_sem.at[step, part]),
+            pltpu.make_async_copy(act_hbm.at[rng], act.at[rng], act_sem.at[step]),
+            pltpu.make_async_copy(grad_hbm.at[rng], grad.at[rng], grad_sem.at[step]),
         )
 
     weights = [
@@ -54,9 +51,8 @@
         pltpu.make_async_copy(pout_hbm, pout, w_sem.at[1]),
     ]
     def start_step(step):
-        for part in range(parts):
-            for priority, copy in enumerate(part_copies(step, part)):
-                copy.start(priority=priority)
+        for priority, copy in enumerate(step_copies(step)):
+            copy.start(priority=priority)
 
     small = [
         pltpu.make_async_copy(source, target, s_sem.at[index])
@@ -90,14 +86,16 @@
         copy.wait()
 
     def project(step):
-        acts, grads = [], []
-        for part in range(parts):
-            for copy in part_copies(step, part):
-                copy.wait()
-            rng = pl.ds(pl.multiple_of(step * step_rows + part * part_rows, part_rows), part_rows)
-            acts.append(dot_nt(act[rng], pin[...]).astype(jnp.bfloat16))
-            grads.append(dot_nt(pout[...], grad[rng]).astype(jnp.bfloat16))
-        return jnp.concatenate(acts, axis=0), jnp.concatenate(grads, axis=1)
+        for copy in step_copies(step):
+            copy.wait()
+        rng = pl.ds(pl.multiple_of(step * step_rows, step_rows), step_rows)
+        first, second = pl.ds(0, width // 2), pl.ds(width // 2, width // 2)
+        return (
+            (dot_nt(act[rng, first], pin[:, first]) + dot_nt(act[rng, second], pin[:, second])
+             ).astype(jnp.bfloat16),
+            (dot_nt(pout[:, first], grad[rng, first]) + dot_nt(pout[:, second], grad[rng, second])
+             ).astype(jnp.bfloat16),
+        )
 
     def rotate(step, act_part, grad_part):
         act_hi, act_lo = split_two(dot_nn(act_part, bin_hi) + dot_nn(act_part, bin_lo))
@@ -171,8 +169,8 @@
             pltpu.VMEM((rank, batch * tokens), jnp.bfloat16),
             pltpu.VMEM((2, rank, batch * tokens), jnp.float32),
             pltpu.VMEM((half, examples, 2 * rank), jnp.float32),
-            pltpu.SemaphoreType.DMA((steps, parts)),
-            pltpu.SemaphoreType.DMA((steps, parts)),
+            pltpu.SemaphoreType.DMA((steps,)),
+            pltpu.SemaphoreType.DMA((steps,)),
             pltpu.SemaphoreType.DMA((2,)),
             pltpu.SemaphoreType.DMA((4,)),
         ],
@@ -346,11 +344,14 @@
             slab, slabs[column_groups] = lax.optimization_barrier((slab, slabs[column_groups]))
         columns = [swap(slab, "grp", groups, row_groups * step) for step in range(column_groups)]
         rows = [swap(slab, "grp", groups, step) for step in range(1, row_groups)]
-        held = lax.optimization_barrier((*columns[1:], *rows))[:column_groups - 1]
+        held = columns[1:]
+        if run + 1 < runs:
+            held = lax.optimization_barrier((*held, *rows))[:column_groups - 1]
         others = [swap(column, "mem", members, 1) for column in (slab, *held)]
         slabs += columns + others + rows
     partial = products(slabs, slices, pieces, examples, row_groups, column_groups)
-    parts = [swap(partial[index], "mem", members, cores * index) for index in slice_order(slices)]
+    parts = [partial[0]] + [
+        swap(partial[index], "mem", members, cores * index) for index in reversed(range(1, slices))]
     sums = totals(parts, examples)
     sums = [swap(value, "grp", groups, step) for step, value in enumerate(sums)]
     return finish(sums, column_groups, factor)

time: 47.3 us -> 45.3 us (0.958)
  waiting for transfers between devices: 14.6 us -> 12.8 us
  Pallas kernels: 13.9 us -> 13.2 us
  starting transfers between devices: 17.7 us -> 18.2 us
    ppermute x15, waiting for transfers between devices: 14.6 us -> 12.8 us  [swap(): lax.ppermute(value, axis, [(place, place ^ distance) for place in range(s...]
    pallas_call x1, Pallas kernels: 12.4 us -> 11.8 us  [features(): pl.pallas_call(functools.partial(feature_kernel, tokens, slices), out_sha...]
    ppermute x15, starting transfers between devices: 17.7 us -> 18.2 us  [swap(): lax.ppermute(value, axis, [(place, place ^ distance) for place in range(s...]
where the time goes in v1:
time: 45.3 us; the launch traced here: 45.2 us
  starting transfers between devices  18.2 us (40%)
  Pallas kernels  13.2 us (29%)
  waiting for transfers between devices  12.8 us (28%)
  local copies, waits for them, and re-layouts  0.9 us (2%)
    ppermute x15, starting transfers between devices, swap(): lax.ppermute(value, axis, [(place, place ^ distance) for place in range(s...  18.2 us
    ppermute x15, waiting for transfers between devices, swap(): lax.ppermute(value, axis, [(place, place ^ distance) for place in range(s...  12.8 us
    pallas_call x1, Pallas kernels, features(): pl.pallas_call(functools.partial(feature_kernel, tokens, slices), out_sha...  11.8 us
  transfers between devices with their start and end apart: 15, of which 8 were waited for; matrix products, arithmetic and copies ran while one was open for 2% of the time, Pallas kernels for 0%

profile of v1, /device:TPU:0, one launch (start us, length us, event | category | flops | bytes accessed | tf_op | source)
XLA Modules:
  0.0 45.2 jit_solution(14208319075866077764)
XLA Ops:
  0.0 11.8 %features.1 = (bf16[272,128]{1,0:T(8,128)(2,1)}, bf16[272,128]{1,0:T(8,128)(2,1)}, bf16[272,128]{1,0:T(8,128)(2,1)}, bf16[272,128]{1,0:T(8,128)(2,1)}) custom-call(bf16[1024,4096]{1,0:T(8,128)(2,1)} %bitcast.5, bf16[1024,4096]{1,0:T(8,128)(2,1)} %bitcast.6, bf16[64,4096]{1,0:T(8,128)(2,1)} %bitcast.7, bf16[64,4096]{1,0:T(8,128)(2,1)} %bitcast.8, ...), custom_call_target="tpu_custom_call" | custom-call | flops 1073741824 | bytes 16777216 | tf_op jit(solution)/shard_map/features/pallas_call | solution.py:152
  11.8 3.1 %collective-permute-start = (bf16[272,128]{1,0:T(8,128)(2,1)}, bf16[272,128]{1,0:T(8,128)(2,1)S(1)}, u32[]{:S(2)}, u32[]{:S(2)}) collective-permute-start(bf16[272,128]{1,0:T(8,128)(2,1)} %get-tuple-element.19), channel_id=1, source_target_pairs={{0,2},{1,3},{2,0},{3,1},{4,6},{5,7},{6,4},{7,5},{8,10},{9,11},{10,... | collective-permute-start | bytes 208904 | tf_op jit(solution)/shard_map/ppermute | solution.py:326
  14.9 2.6 %collective-permute-start.2 = (bf16[272,128]{1,0:T(8,128)(2,1)}, bf16[272,128]{1,0:T(8,128)(2,1)S(1)}, u32[]{:S(2)}, u32[]{:S(2)}) collective-permute-start(bf16[272,128]{1,0:T(8,128)(2,1)} %get-tuple-element.20), channel_id=1, source_target_pairs={{0,4},{1,5},{2,6},{3,7},{4,0},{5,1},{6,2},{7,3},{8,12},{9,13},{10,... | collective-permute-start | bytes 208904 | tf_op jit(solution)/shard_map/ppermute | solution.py:326
  17.5 0.0 collective-permute-start.3
  17.5 0.9 %constant_dynamic-update-slice_fusion.1 = bf16[544,128]{1,0:T(8,128)(2,1)S(1)} fusion(bf16[272,128]{1,0:T(8,128)(2,1)} %get-tuple-element.18), kind=kLoop, calls=%fused_computation.2 | loop fusion | bytes 139264
  18.4 0.1 collective-permute-start.4
  18.5 1.8 %collective-permute-start.5 = (bf16[544,128]{1,0:T(8,128)(2,1)S(1)}, bf16[544,128]{1,0:T(8,128)(2,1)S(1)}, u32[]{:S(2)}, u32[]{:S(2)}) collective-permute-start(bf16[544,128]{1,0:T(8,128)(2,1)S(1)} %constant_dynamic-update-slice_fusion.refs_0_), channel_id=1, source_target_pairs={{0,8},{8,0},{16,24},{24,16},{1,9},{9,1},{17,25},{25,17},{2,10},{10... | collective-permute-start | bytes 417800 | tf_op jit(solution)/shard_map/ppermute | solution.py:326
  20.2 1.5 %collective-permute-start.1 = (bf16[544,128]{1,0:T(8,128)(2,1)S(1)}, bf16[544,128]{1,0:T(8,128)(2,1)S(1)}, u32[]{:S(2)}, u32[]{:S(2)}) collective-permute-start(bf16[544,128]{1,0:T(8,128)(2,1)S(1)} %constant_dynamic-update-slice_fusion.refs_0_), channel_id=1, source_target_pairs={{0,16},{8,24},{16,0},{24,8},{1,17},{9,25},{17,1},{25,9},{2,18},{10... | collective-permute-start | bytes 417800 | tf_op jit(solution)/shard_map/ppermute | solution.py:326
  21.8 0.9 %collective-permute-done.2 = bf16[272,128]{1,0:T(8,128)(2,1)S(1)} collective-permute-done((bf16[272,128]{1,0:T(8,128)(2,1)}, bf16[272,128]{1,0:T(8,128)(2,1)S(1)}, u32[]{:S(2)}, u32[]{:S(2)}) %collective-permute-start.2) | collective-permute-done | bytes 69664 | tf_op jit(solution)/shard_map/ppermute | solution.py:326
  22.6 1.3 %collective-permute-done.3 = bf16[272,128]{1,0:T(8,128)(2,1)S(1)} collective-permute-done((bf16[272,128]{1,0:T(8,128)(2,1)}, bf16[272,128]{1,0:T(8,128)(2,1)S(1)}, u32[]{:S(2)}, u32[]{:S(2)}) %collective-permute-start.3) | collective-permute-done | bytes 69664 | tf_op jit(solution)/shard_map/ppermute | solution.py:326
  23.9 1.6 %collective-permute-start.7 = (bf16[544,128]{1,0:T(8,128)(2,1)S(1)}, bf16[544,128]{1,0:T(8,128)(2,1)S(1)}, u32[]{:S(2)}, u32[]{:S(2)}) collective-permute-start(bf16[544,128]{1,0:T(8,128)(2,1)S(1)} %pad_maximum_fusion.refs_5_), channel_id=1, source_target_pairs={{0,16},{8,24},{16,0},{24,8},{1,17},{9,25},{17,1},{25,9},{2,18},{10... | collective-permute-start | bytes 417800 | tf_op jit(solution)/shard_map/ppermute | solution.py:326
  25.5 1.5 %collective-permute-start.10 = (bf16[544,128]{1,0:T(8,128)(2,1)S(1)}, bf16[544,128]{1,0:T(8,128)(2,1)S(1)}, u32[]{:S(2)}, u32[]{:S(2)}) collective-permute-start(bf16[544,128]{1,0:T(8,128)(2,1)S(1)} %pad_maximum_fusion.refs_5_), channel_id=1, source_target_pairs={{0,8},{8,0},{16,24},{24,16},{1,9},{9,1},{17,25},{25,17},{2,10},{10... | collective-permute-start | bytes 417800 | tf_op jit(solution)/shard_map/ppermute | solution.py:326
  27.0 0.5 %collective-permute-start.6 = (bf16[544,128]{1,0:T(8,128)(2,1)S(1)}, bf16[544,128]{1,0:T(8,128)(2,1)S(1)}, u32[]{:S(2)}, u32[]{:S(2)}) collective-permute-start(bf16[544,128]{1,0:T(8,128)(2,1)S(1)} %collective-permute-done.1.refs_1_), channel_id=1, source_target_pairs={{0,1},{1,0},{2,3},{3,2},{4,5},{5,4},{6,7},{7,6},{8,9},{9,8},{10,11... | collective-permute-start | bytes 417800 | tf_op jit(solution)/shard_map/ppermute | solution.py:326
  27.5 1.5 %collective-permute-done.7.refs_6_ = bf16[544,128]{1,0:T(8,128)(2,1)S(1)} collective-permute-done((bf16[544,128]{1,0:T(8,128)(2,1)S(1)}, bf16[544,128]{1,0:T(8,128)(2,1)S(1)}, u32[]{:S(2)}, u32[]{:S(2)}) %collective-permute-start.7) | collective-permute-done | bytes 139296 | tf_op jit(solution)/shard_map/ppermute | solution.py:326
  29.0 1.5 %collective-permute-done.10.refs_9_ = bf16[544,128]{1,0:T(8,128)(2,1)S(1)} collective-permute-done((bf16[544,128]{1,0:T(8,128)(2,1)S(1)}, bf16[544,128]{1,0:T(8,128)(2,1)S(1)}, u32[]{:S(2)}, u32[]{:S(2)}) %collective-permute-start.10) | collective-permute-done | bytes 139296 | tf_op jit(solution)/shard_map/ppermute | solution.py:326
  30.6 0.7 %products.1 = (bf16[64,512]{1,0:T(8,128)(2,1)S(1)}, bf16[64,512]{1,0:T(8,128)(2,1)S(1)}, bf16[64,512]{1,0:T(8,128)(2,1)S(1)}, bf16[64,512]{1,0:T(8,128)(2,1)S(1)}) custom-call(bf16[544,128]{1,0:T(8,128)(2,1)S(1)} %constant_dynamic-update-slice_fusion.refs_0_, bf16[544,128]{1,0:T(8,128)(2,1)S(1)} %collective-permute-done.1.refs_1_, ...), custom_call_target="tpu_custom_call" | custom-call | flops 268435456 | bytes 524288 | tf_op jit(solution)/shard_map/products/pallas_call | solution.py:251
  31.3 3.4 %collective-permute-start.11 = (bf16[64,512]{1,0:T(8,128)(2,1)S(1)}, bf16[64,512]{1,0:T(8,128)(2,1)S(1)}, u32[]{:S(2)}, u32[]{:S(2)}) collective-permute-start(bf16[64,512]{1,0:T(8,128)(2,1)S(1)} %get-tuple-element.26), channel_id=1, source_target_pairs={{0,6},{1,7},{2,4},{3,5},{4,2},{5,3},{6,0},{7,1},{8,14},{9,15},{10,... | collective-permute-start | bytes 196616 | tf_op jit(solution)/shard_map/ppermute | solution.py:326
  34.7 1.0 %collective-permute-start.13 = (bf16[64,512]{1,0:T(8,128)(2,1)S(1)}, bf16[64,512]{1,0:T(8,128)(2,1)S(1)}, u32[]{:S(2)}, u32[]{:S(2)}) collective-permute-start(bf16[64,512]{1,0:T(8,128)(2,1)S(1)} %get-tuple-element.28), channel_id=1, source_target_pairs={{0,2},{1,3},{2,0},{3,1},{4,6},{5,7},{6,4},{7,5},{8,10},{9,11},{10,... | collective-permute-start | bytes 196616 | tf_op jit(solution)/shard_map/ppermute | solution.py:326
  35.8 2.4 %collective-permute-done.11.refs_1_ = bf16[64,512]{1,0:T(8,128)(2,1)S(1)} collective-permute-done((bf16[64,512]{1,0:T(8,128)(2,1)S(1)}, bf16[64,512]{1,0:T(8,128)(2,1)S(1)}, u32[]{:S(2)}, u32[]{:S(2)}) %collective-permute-start.11) | collective-permute-done | bytes 65568 | tf_op jit(solution)/shard_map/ppermute | solution.py:326
  38.2 2.1 %collective-permute-done.12.refs_2_ = bf16[64,512]{1,0:T(8,128)(2,1)S(1)} collective-permute-done((bf16[64,512]{1,0:T(8,128)(2,1)S(1)}, bf16[64,512]{1,0:T(8,128)(2,1)S(1)}, u32[]{:S(2)}, u32[]{:S(2)}) %collective-permute-start.12) | collective-permute-done | bytes 65568 | tf_op jit(solution)/shard_map/ppermute | solution.py:326
  40.3 0.2 collective-permute-done.13.refs_3_
  40.5 1.1 %collective-permute-start.14 = (bf16[32,512]{1,0:T(8,128)(2,1)S(1)}, bf16[32,512]{1,0:T(8,128)(2,1)S(1)}, u32[]{:S(2)}, u32[]{:S(2)}) collective-permute-start(bf16[32,512]{1,0:T(8,128)(2,1)S(1)} %get-tuple-element.30), channel_id=1, source_target_pairs={{0,8},{8,0},{16,24},{24,16},{1,9},{9,1},{17,25},{25,17},{2,10},{10... | collective-permute-start | bytes 98312 | tf_op jit(solution)/shard_map/ppermute | solution.py:326
  41.6 2.9 %collective-permute-done.14.refs_1_ = bf16[32,512]{1,0:T(8,128)(2,1)S(1)} collective-permute-done((bf16[32,512]{1,0:T(8,128)(2,1)S(1)}, bf16[32,512]{1,0:T(8,128)(2,1)S(1)}, u32[]{:S(2)}, u32[]{:S(2)}) %collective-permute-start.14) | collective-permute-done | bytes 32800 | tf_op jit(solution)/shard_map/ppermute | solution.py:326
  44.5 0.7 %finish.1 = f32[32,1024]{1,0:T(8,128)} custom-call(f32[32,512]{1,0:T(8,128)S(1)} %get-tuple-element.29.refs_0_, bf16[32,512]{1,0:T(8,128)(2,1)S(1)} %collective-permute-done.14.refs_1_), custom_call_target="tpu_custom_call" | custom-call | flops 131072 | bytes 262144 | tf_op jit(solution)/shard_map/finish/pallas_call | solution.py:311
  (13 shorter events, 0.1 us)
Async XLA Ops:
  11.8 6.6 %collective-permute-start = (bf16[272,128]{1,0:T(8,128)(2,1)}, bf16[272,128]{1,0:T(8,128)(2,1)S(1)}, u32[]{:S(2)}, u32[]{:S(2)}) collective-permute-start(bf16[272,128]{1,0:T(8,128)(2,1)} %get-tuple-element.19), channel_id=1, source_target_pairs={{0,2},{1,3},{2,0},{3,1},{4,6},{5,7},{6,4},{7,5},{8,10},{9,11},{10,... | collective-permute-start | bytes 208904 | tf_op jit(solution)/shard_map/ppermute | solution.py:326
  14.9 7.7 %collective-permute-start.2 = (bf16[272,128]{1,0:T(8,128)(2,1)}, bf16[272,128]{1,0:T(8,128)(2,1)S(1)}, u32[]{:S(2)}, u32[]{:S(2)}) collective-permute-start(bf16[272,128]{1,0:T(8,128)(2,1)} %get-tuple-element.20), channel_id=1, source_target_pairs={{0,4},{1,5},{2,6},{3,7},{4,0},{5,1},{6,2},{7,3},{8,12},{9,13},{10,... | collective-permute-start | bytes 208904 | tf_op jit(solution)/shard_map/ppermute | solution.py:326
  17.5 6.4 %collective-permute-start.3 = (bf16[272,128]{1,0:T(8,128)(2,1)}, bf16[272,128]{1,0:T(8,128)(2,1)S(1)}, u32[]{:S(2)}, u32[]{:S(2)}) collective-permute-start(bf16[272,128]{1,0:T(8,128)(2,1)} %get-tuple-element.21), channel_id=1, source_target_pairs={{0,6},{1,7},{2,4},{3,5},{4,2},{5,3},{6,0},{7,1},{8,14},{9,15},{10,... | collective-permute-start | bytes 208904 | tf_op jit(solution)/shard_map/ppermute | solution.py:326
  18.4 5.5 %collective-permute-start.4 = (bf16[544,128]{1,0:T(8,128)(2,1)S(1)}, bf16[544,128]{1,0:T(8,128)(2,1)S(1)}, u32[]{:S(2)}, u32[]{:S(2)}) collective-permute-start(bf16[544,128]{1,0:T(8,128)(2,1)S(1)} %constant_dynamic-update-slice_fusion.refs_0_), channel_id=1, source_target_pairs={{0,1},{1,0},{2,3},{3,2},{4,5},{5,4},{6,7},{7,6},{8,9},{9,8},{10,11... | collective-permute-start | bytes 417800 | tf_op jit(solution)/shard_map/ppermute | solution.py:326
  18.5 8.5 %collective-permute-start.5 = (bf16[544,128]{1,0:T(8,128)(2,1)S(1)}, bf16[544,128]{1,0:T(8,128)(2,1)S(1)}, u32[]{:S(2)}, u32[]{:S(2)}) collective-permute-start(bf16[544,128]{1,0:T(8,128)(2,1)S(1)} %constant_dynamic-update-slice_fusion.refs_0_), channel_id=1, source_target_pairs={{0,8},{8,0},{16,24},{24,16},{1,9},{9,1},{17,25},{25,17},{2,10},{10... | collective-permute-start | bytes 417800 | tf_op jit(solution)/shard_map/ppermute | solution.py:326
  20.2 6.8 %collective-permute-start.1 = (bf16[544,128]{1,0:T(8,128)(2,1)S(1)}, bf16[544,128]{1,0:T(8,128)(2,1)S(1)}, u32[]{:S(2)}, u32[]{:S(2)}) collective-permute-start(bf16[544,128]{1,0:T(8,128)(2,1)S(1)} %constant_dynamic-update-slice_fusion.refs_0_), channel_id=1, source_target_pairs={{0,16},{8,24},{16,0},{24,8},{1,17},{9,25},{17,1},{25,9},{2,18},{10... | collective-permute-start | bytes 417800 | tf_op jit(solution)/shard_map/ppermute | solution.py:326
  23.9 5.1 %collective-permute-start.7 = (bf16[544,128]{1,0:T(8,128)(2,1)S(1)}, bf16[544,128]{1,0:T(8,128)(2,1)S(1)}, u32[]{:S(2)}, u32[]{:S(2)}) collective-permute-start(bf16[544,128]{1,0:T(8,128)(2,1)S(1)} %pad_maximum_fusion.refs_5_), channel_id=1, source_target_pairs={{0,16},{8,24},{16,0},{24,8},{1,17},{9,25},{17,1},{25,9},{2,18},{10... | collective-permute-start | bytes 417800 | tf_op jit(solution)/shard_map/ppermute | solution.py:326
  25.5 5.1 %collective-permute-start.10 = (bf16[544,128]{1,0:T(8,128)(2,1)S(1)}, bf16[544,128]{1,0:T(8,128)(2,1)S(1)}, u32[]{:S(2)}, u32[]{:S(2)}) collective-permute-start(bf16[544,128]{1,0:T(8,128)(2,1)S(1)} %pad_maximum_fusion.refs_5_), channel_id=1, source_target_pairs={{0,8},{8,0},{16,24},{24,16},{1,9},{9,1},{17,25},{25,17},{2,10},{10... | collective-permute-start | bytes 417800 | tf_op jit(solution)/shard_map/ppermute | solution.py:326
  27.0 3.6 %collective-permute-start.8 = (bf16[544,128]{1,0:T(8,128)(2,1)S(1)}, bf16[544,128]{1,0:T(8,128)(2,1)S(1)}, u32[]{:S(2)}, u32[]{:S(2)}) collective-permute-start(bf16[544,128]{1,0:T(8,128)(2,1)S(1)} %pad_maximum_fusion.refs_5_), channel_id=1, source_target_pairs={{0,1},{1,0},{2,3},{3,2},{4,5},{5,4},{6,7},{7,6},{8,9},{9,8},{10,11... | collective-permute-start | bytes 417800 | tf_op jit(solution)/shard_map/ppermute | solution.py:326
  27.0 3.6 %collective-permute-start.6 = (bf16[544,128]{1,0:T(8,128)(2,1)S(1)}, bf16[544,128]{1,0:T(8,128)(2,1)S(1)}, u32[]{:S(2)}, u32[]{:S(2)}) collective-permute-start(bf16[544,128]{1,0:T(8,128)(2,1)S(1)} %collective-permute-done.1.refs_1_), channel_id=1, source_target_pairs={{0,1},{1,0},{2,3},{3,2},{4,5},{5,4},{6,7},{7,6},{8,9},{9,8},{10,11... | collective-permute-start | bytes 417800 | tf_op jit(solution)/shard_map/ppermute | solution.py:326
  29.0 1.5 %collective-permute-start.9 = (bf16[544,128]{1,0:T(8,128)(2,1)S(1)}, bf16[544,128]{1,0:T(8,128)(2,1)S(1)}, u32[]{:S(2)}, u32[]{:S(2)}) collective-permute-start(bf16[544,128]{1,0:T(8,128)(2,1)S(1)} %collective-permute-done.7.refs_6_), channel_id=1, source_target_pairs={{0,1},{1,0},{2,3},{3,2},{4,5},{5,4},{6,7},{7,6},{8,9},{9,8},{10,11... | collective-permute-start | bytes 417800 | tf_op jit(solution)/shard_map/ppermute | solution.py:326
  31.3 6.9 %collective-permute-start.11 = (bf16[64,512]{1,0:T(8,128)(2,1)S(1)}, bf16[64,512]{1,0:T(8,128)(2,1)S(1)}, u32[]{:S(2)}, u32[]{:S(2)}) collective-permute-start(bf16[64,512]{1,0:T(8,128)(2,1)S(1)} %get-tuple-element.26), channel_id=1, source_target_pairs={{0,6},{1,7},{2,4},{3,5},{4,2},{5,3},{6,0},{7,1},{8,14},{9,15},{10,... | collective-permute-start | bytes 196616 | tf_op jit(solution)/shard_map/ppermute | solution.py:326
  34.7 5.6 %collective-permute-start.12 = (bf16[64,512]{1,0:T(8,128)(2,1)S(1)}, bf16[64,512]{1,0:T(8,128)(2,1)S(1)}, u32[]{:S(2)}, u32[]{:S(2)}) collective-permute-start(bf16[64,512]{1,0:T(8,128)(2,1)S(1)} %get-tuple-element.27), channel_id=1, source_target_pairs={{0,4},{1,5},{2,6},{3,7},{4,0},{5,1},{6,2},{7,3},{8,12},{9,13},{10,... | collective-permute-start | bytes 196616 | tf_op jit(solution)/shard_map/ppermute | solution.py:326
  34.7 5.7 %collective-permute-start.13 = (bf16[64,512]{1,0:T(8,128)(2,1)S(1)}, bf16[64,512]{1,0:T(8,128)(2,1)S(1)}, u32[]{:S(2)}, u32[]{:S(2)}) collective-permute-start(bf16[64,512]{1,0:T(8,128)(2,1)S(1)} %get-tuple-element.28), channel_id=1, source_target_pairs={{0,2},{1,3},{2,0},{3,1},{4,6},{5,7},{6,4},{7,5},{8,10},{9,11},{10,... | collective-permute-start | bytes 196616 | tf_op jit(solution)/shard_map/ppermute | solution.py:326
  40.5 4.0 %collective-permute-start.14 = (bf16[32,512]{1,0:T(8,128)(2,1)S(1)}, bf16[32,512]{1,0:T(8,128)(2,1)S(1)}, u32[]{:S(2)}, u32[]{:S(2)}) collective-permute-start(bf16[32,512]{1,0:T(8,128)(2,1)S(1)} %get-tuple-element.30), channel_id=1, source_target_pairs={{0,8},{8,0},{16,24},{24,16},{1,9},{9,1},{17,25},{25,17},{2,10},{10... | collective-permute-start | bytes 98312 | tf_op jit(solution)/shard_map/ppermute | solution.py:326

commit v2 on v1

--- a/solution.py
+++ b/solution.py
@@ -185,7 +185,7 @@
 
 
 def slice_order(slices):
-    return list(range(slices))
+    return [0, 1] + list(range(slices - 1, 1, -1))
 
 
 def product_kernel(slices, pieces, examples, row_groups, column_groups, *refs):

time: 45.3 us -> 45.7 us (level)
  no operation moved by 1% of the time
where the time goes in v2:
time: 45.7 us; the launch traced here: 45.5 us
  starting transfers between devices  18.4 us (40%)
  Pallas kernels  13.2 us (29%)
  waiting for transfers between devices  12.9 us (28%)
  local copies, waits for them, and re-layouts  0.9 us (2%)
    ppermute x15, starting transfers between devices, swap(): lax.ppermute(value, axis, [(place, place ^ distance) for place in range(s...  18.4 us
    ppermute x15, waiting for transfers between devices, swap(): lax.ppermute(value, axis, [(place, place ^ distance) for place in range(s...  12.9 us
    pallas_call x1, Pallas kernels, features(): pl.pallas_call(functools.partial(feature_kernel, tokens, slices), out_sha...  11.8 us
  transfers between devices with their start and end apart: 15, of which 8 were waited for; matrix products, arithmetic and copies ran while one was open for 2% of the time, Pallas kernels for 0%

profile of v2, /device:TPU:0, one launch (start us, length us, event | category | flops | bytes accessed | tf_op | source)
XLA Modules:
  0.0 45.5 jit_solution(8708265399769544314)
XLA Ops:
  0.0 11.8 %features.1 = (bf16[272,128]{1,0:T(8,128)(2,1)}, bf16[272,128]{1,0:T(8,128)(2,1)}, bf16[272,128]{1,0:T(8,128)(2,1)}, bf16[272,128]{1,0:T(8,128)(2,1)}) custom-call(bf16[1024,4096]{1,0:T(8,128)(2,1)} %bitcast.5, bf16[1024,4096]{1,0:T(8,128)(2,1)} %bitcast.6, bf16[64,4096]{1,0:T(8,128)(2,1)} %bitcast.7, bf16[64,4096]{1,0:T(8,128)(2,1)} %bitcast.8, ...), custom_call_target="tpu_custom_call" | custom-call | flops 1073741824 | bytes 16777216 | tf_op jit(solution)/shard_map/features/pallas_call | solution.py:152
  11.8 3.1 %collective-permute-start = (bf16[272,128]{1,0:T(8,128)(2,1)}, bf16[272,128]{1,0:T(8,128)(2,1)S(1)}, u32[]{:S(2)}, u32[]{:S(2)}) collective-permute-start(bf16[272,128]{1,0:T(8,128)(2,1)} %get-tuple-element.19), channel_id=1, source_target_pairs={{0,2},{1,3},{2,0},{3,1},{4,6},{5,7},{6,4},{7,5},{8,10},{9,11},{10,... | collective-permute-start | bytes 208904 | tf_op jit(solution)/shard_map/ppermute | solution.py:326
  14.9 2.5 %collective-permute-start.2 = (bf16[272,128]{1,0:T(8,128)(2,1)}, bf16[272,128]{1,0:T(8,128)(2,1)S(1)}, u32[]{:S(2)}, u32[]{:S(2)}) collective-permute-start(bf16[272,128]{1,0:T(8,128)(2,1)} %get-tuple-element.20), channel_id=1, source_target_pairs={{0,6},{1,7},{2,4},{3,5},{4,2},{5,3},{6,0},{7,1},{8,14},{9,15},{10,... | collective-permute-start | bytes 208904 | tf_op jit(solution)/shard_map/ppermute | solution.py:326
  17.4 0.1 collective-permute-start.3
  17.5 0.9 %constant_dynamic-update-slice_fusion.1 = bf16[544,128]{1,0:T(8,128)(2,1)S(1)} fusion(bf16[272,128]{1,0:T(8,128)(2,1)} %get-tuple-element.18), kind=kLoop, calls=%fused_computation.2 | loop fusion | bytes 139264
  18.4 0.1 collective-permute-start.4
  18.5 1.6 %collective-permute-start.5 = (bf16[544,128]{1,0:T(8,128)(2,1)S(1)}, bf16[544,128]{1,0:T(8,128)(2,1)S(1)}, u32[]{:S(2)}, u32[]{:S(2)}) collective-permute-start(bf16[544,128]{1,0:T(8,128)(2,1)S(1)} %constant_dynamic-update-slice_fusion.refs_0_), channel_id=1, source_target_pairs={{0,8},{8,0},{16,24},{24,16},{1,9},{9,1},{17,25},{25,17},{2,10},{10... | collective-permute-start | bytes 417800 | tf_op jit(solution)/shard_map/ppermute | solution.py:326
  20.0 1.5 %collective-permute-start.1 = (bf16[544,128]{1,0:T(8,128)(2,1)S(1)}, bf16[544,128]{1,0:T(8,128)(2,1)S(1)}, u32[]{:S(2)}, u32[]{:S(2)}) collective-permute-start(bf16[544,128]{1,0:T(8,128)(2,1)S(1)} %constant_dynamic-update-slice_fusion.refs_0_), channel_id=1, source_target_pairs={{0,16},{8,24},{16,0},{24,8},{1,17},{9,25},{17,1},{25,9},{2,18},{10... | collective-permute-start | bytes 417800 | tf_op jit(solution)/shard_map/ppermute | solution.py:326
  21.5 0.6 %collective-permute-done.2 = bf16[272,128]{1,0:T(8,128)(2,1)S(1)} collective-permute-done((bf16[272,128]{1,0:T(8,128)(2,1)}, bf16[272,128]{1,0:T(8,128)(2,1)S(1)}, u32[]{:S(2)}, u32[]{:S(2)}) %collective-permute-start.2) | collective-permute-done | bytes 69664 | tf_op jit(solution)/shard_map/ppermute | solution.py:326
  22.1 2.2 %collective-permute-done.3 = bf16[272,128]{1,0:T(8,128)(2,1)S(1)} collective-permute-done((bf16[272,128]{1,0:T(8,128)(2,1)}, bf16[272,128]{1,0:T(8,128)(2,1)S(1)}, u32[]{:S(2)}, u32[]{:S(2)}) %collective-permute-start.3) | collective-permute-done | bytes 69664 | tf_op jit(solution)/shard_map/ppermute | solution.py:326
  24.3 1.6 %collective-permute-start.7 = (bf16[544,128]{1,0:T(8,128)(2,1)S(1)}, bf16[544,128]{1,0:T(8,128)(2,1)S(1)}, u32[]{:S(2)}, u32[]{:S(2)}) collective-permute-start(bf16[544,128]{1,0:T(8,128)(2,1)S(1)} %pad_maximum_fusion.refs_5_), channel_id=1, source_target_pairs={{0,16},{8,24},{16,0},{24,8},{1,17},{9,25},{17,1},{25,9},{2,18},{10... | collective-permute-start | bytes 417800 | tf_op jit(solution)/shard_map/ppermute | solution.py:326
  25.9 1.5 %collective-permute-start.10 = (bf16[544,128]{1,0:T(8,128)(2,1)S(1)}, bf16[544,128]{1,0:T(8,128)(2,1)S(1)}, u32[]{:S(2)}, u32[]{:S(2)}) collective-permute-start(bf16[544,128]{1,0:T(8,128)(2,1)S(1)} %pad_maximum_fusion.refs_5_), channel_id=1, source_target_pairs={{0,8},{8,0},{16,24},{24,16},{1,9},{9,1},{17,25},{25,17},{2,10},{10... | collective-permute-start | bytes 417800 | tf_op jit(solution)/shard_map/ppermute | solution.py:326
  27.4 0.5 %collective-permute-start.6 = (bf16[544,128]{1,0:T(8,128)(2,1)S(1)}, bf16[544,128]{1,0:T(8,128)(2,1)S(1)}, u32[]{:S(2)}, u32[]{:S(2)}) collective-permute-start(bf16[544,128]{1,0:T(8,128)(2,1)S(1)} %collective-permute-done.1.refs_1_), channel_id=1, source_target_pairs={{0,1},{1,0},{2,3},{3,2},{4,5},{5,4},{6,7},{7,6},{8,9},{9,8},{10,11... | collective-permute-start | bytes 417800 | tf_op jit(solution)/shard_map/ppermute | solution.py:326
  27.9 2.0 %collective-permute-done.7.refs_6_ = bf16[544,128]{1,0:T(8,128)(2,1)S(1)} collective-permute-done((bf16[544,128]{1,0:T(8,128)(2,1)S(1)}, bf16[544,128]{1,0:T(8,128)(2,1)S(1)}, u32[]{:S(2)}, u32[]{:S(2)}) %collective-permute-start.7) | collective-permute-done | bytes 139296 | tf_op jit(solution)/shard_map/ppermute | solution.py:326
  29.9 1.2 %collective-permute-done.10.refs_9_ = bf16[544,128]{1,0:T(8,128)(2,1)S(1)} collective-permute-done((bf16[544,128]{1,0:T(8,128)(2,1)S(1)}, bf16[544,128]{1,0:T(8,128)(2,1)S(1)}, u32[]{:S(2)}, u32[]{:S(2)}) %collective-permute-start.10) | collective-permute-done | bytes 139296 | tf_op jit(solution)/shard_map/ppermute | solution.py:326
  31.2 0.1 collective-permute-done.9.refs_8_
  31.3 0.7 %products.1 = (bf16[64,512]{1,0:T(8,128)(2,1)S(1)}, bf16[64,512]{1,0:T(8,128)(2,1)S(1)}, bf16[64,512]{1,0:T(8,128)(2,1)S(1)}, bf16[64,512]{1,0:T(8,128)(2,1)S(1)}) custom-call(bf16[544,128]{1,0:T(8,128)(2,1)S(1)} %constant_dynamic-update-slice_fusion.refs_0_, bf16[544,128]{1,0:T(8,128)(2,1)S(1)} %collective-permute-done.1.refs_1_, ...), custom_call_target="tpu_custom_call" | custom-call | flops 268435456 | bytes 524288 | tf_op jit(solution)/shard_map/products/pallas_call | solution.py:251
  32.0 2.2 %collective-permute-start.11 = (bf16[64,512]{1,0:T(8,128)(2,1)S(1)}, bf16[64,512]{1,0:T(8,128)(2,1)S(1)}, u32[]{:S(2)}, u32[]{:S(2)}) collective-permute-start(bf16[64,512]{1,0:T(8,128)(2,1)S(1)} %get-tuple-element.26), channel_id=1, source_target_pairs={{0,6},{1,7},{2,4},{3,5},{4,2},{5,3},{6,0},{7,1},{8,14},{9,15},{10,... | collective-permute-start | bytes 196616 | tf_op jit(solution)/shard_map/ppermute | solution.py:326
  34.2 2.2 %collective-permute-start.13 = (bf16[64,512]{1,0:T(8,128)(2,1)S(1)}, bf16[64,512]{1,0:T(8,128)(2,1)S(1)}, u32[]{:S(2)}, u32[]{:S(2)}) collective-permute-start(bf16[64,512]{1,0:T(8,128)(2,1)S(1)} %get-tuple-element.28), channel_id=1, source_target_pairs={{0,2},{1,3},{2,0},{3,1},{4,6},{5,7},{6,4},{7,5},{8,10},{9,11},{10,... | collective-permute-start | bytes 196616 | tf_op jit(solution)/shard_map/ppermute | solution.py:326
  36.5 2.4 %collective-permute-done.11.refs_1_ = bf16[64,512]{1,0:T(8,128)(2,1)S(1)} collective-permute-done((bf16[64,512]{1,0:T(8,128)(2,1)S(1)}, bf16[64,512]{1,0:T(8,128)(2,1)S(1)}, u32[]{:S(2)}, u32[]{:S(2)}) %collective-permute-start.11) | collective-permute-done | bytes 65568 | tf_op jit(solution)/shard_map/ppermute | solution.py:326
  38.8 2.0 %collective-permute-done.12.refs_2_ = bf16[64,512]{1,0:T(8,128)(2,1)S(1)} collective-permute-done((bf16[64,512]{1,0:T(8,128)(2,1)S(1)}, bf16[64,512]{1,0:T(8,128)(2,1)S(1)}, u32[]{:S(2)}, u32[]{:S(2)}) %collective-permute-start.12) | collective-permute-done | bytes 65568 | tf_op jit(solution)/shard_map/ppermute | solution.py:326
  40.9 1.6 %collective-permute-start.14 = (bf16[32,512]{1,0:T(8,128)(2,1)S(1)}, bf16[32,512]{1,0:T(8,128)(2,1)S(1)}, u32[]{:S(2)}, u32[]{:S(2)}) collective-permute-start(bf16[32,512]{1,0:T(8,128)(2,1)S(1)} %get-tuple-element.30), channel_id=1, source_target_pairs={{0,8},{8,0},{16,24},{24,16},{1,9},{9,1},{17,25},{25,17},{2,10},{10... | collective-permute-start | bytes 98312 | tf_op jit(solution)/shard_map/ppermute | solution.py:326
  42.4 2.4 %collective-permute-done.14.refs_1_ = bf16[32,512]{1,0:T(8,128)(2,1)S(1)} collective-permute-done((bf16[32,512]{1,0:T(8,128)(2,1)S(1)}, bf16[32,512]{1,0:T(8,128)(2,1)S(1)}, u32[]{:S(2)}, u32[]{:S(2)}) %collective-permute-start.14) | collective-permute-done | bytes 32800 | tf_op jit(solution)/shard_map/ppermute | solution.py:326
  44.9 0.7 %finish.1 = f32[32,1024]{1,0:T(8,128)} custom-call(f32[32,512]{1,0:T(8,128)S(1)} %get-tuple-element.29.refs_0_, bf16[32,512]{1,0:T(8,128)(2,1)S(1)} %collective-permute-done.14.refs_1_), custom_call_target="tpu_custom_call" | custom-call | flops 131072 | bytes 262144 | tf_op jit(solution)/shard_map/finish/pallas_call | solution.py:311
  (13 shorter events, 0.1 us)
Async XLA Ops:
  11.8 6.6 %collective-permute-start = (bf16[272,128]{1,0:T(8,128)(2,1)}, bf16[272,128]{1,0:T(8,128)(2,1)S(1)}, u32[]{:S(2)}, u32[]{:S(2)}) collective-permute-start(bf16[272,128]{1,0:T(8,128)(2,1)} %get-tuple-element.19), channel_id=1, source_target_pairs={{0,2},{1,3},{2,0},{3,1},{4,6},{5,7},{6,4},{7,5},{8,10},{9,11},{10,... | collective-permute-start | bytes 208904 | tf_op jit(solution)/shard_map/ppermute | solution.py:326
  14.9 7.2 %collective-permute-start.2 = (bf16[272,128]{1,0:T(8,128)(2,1)}, bf16[272,128]{1,0:T(8,128)(2,1)S(1)}, u32[]{:S(2)}, u32[]{:S(2)}) collective-permute-start(bf16[272,128]{1,0:T(8,128)(2,1)} %get-tuple-element.20), channel_id=1, source_target_pairs={{0,6},{1,7},{2,4},{3,5},{4,2},{5,3},{6,0},{7,1},{8,14},{9,15},{10,... | collective-permute-start | bytes 208904 | tf_op jit(solution)/shard_map/ppermute | solution.py:326
  17.4 7.0 %collective-permute-start.3 = (bf16[272,128]{1,0:T(8,128)(2,1)}, bf16[272,128]{1,0:T(8,128)(2,1)S(1)}, u32[]{:S(2)}, u32[]{:S(2)}) collective-permute-start(bf16[272,128]{1,0:T(8,128)(2,1)} %get-tuple-element.21), channel_id=1, source_target_pairs={{0,4},{1,5},{2,6},{3,7},{4,0},{5,1},{6,2},{7,3},{8,12},{9,13},{10,... | collective-permute-start | bytes 208904 | tf_op jit(solution)/shard_map/ppermute | solution.py:326
  18.4 6.0 %collective-permute-start.4 = (bf16[544,128]{1,0:T(8,128)(2,1)S(1)}, bf16[544,128]{1,0:T(8,128)(2,1)S(1)}, u32[]{:S(2)}, u32[]{:S(2)}) collective-permute-start(bf16[544,128]{1,0:T(8,128)(2,1)S(1)} %constant_dynamic-update-slice_fusion.refs_0_), channel_id=1, source_target_pairs={{0,1},{1,0},{2,3},{3,2},{4,5},{5,4},{6,7},{7,6},{8,9},{9,8},{10,11... | collective-permute-start | bytes 417800 | tf_op jit(solution)/shard_map/ppermute | solution.py:326
  18.5 9.0 %collective-permute-start.5 = (bf16[544,128]{1,0:T(8,128)(2,1)S(1)}, bf16[544,128]{1,0:T(8,128)(2,1)S(1)}, u32[]{:S(2)}, u32[]{:S(2)}) collective-permute-start(bf16[544,128]{1,0:T(8,128)(2,1)S(1)} %constant_dynamic-update-slice_fusion.refs_0_), channel_id=1, source_target_pairs={{0,8},{8,0},{16,24},{24,16},{1,9},{9,1},{17,25},{25,17},{2,10},{10... | collective-permute-start | bytes 417800 | tf_op jit(solution)/shard_map/ppermute | solution.py:326
  20.0 7.4 %collective-permute-start.1 = (bf16[544,128]{1,0:T(8,128)(2,1)S(1)}, bf16[544,128]{1,0:T(8,128)(2,1)S(1)}, u32[]{:S(2)}, u32[]{:S(2)}) collective-permute-start(bf16[544,128]{1,0:T(8,128)(2,1)S(1)} %constant_dynamic-update-slice_fusion.refs_0_), channel_id=1, source_target_pairs={{0,16},{8,24},{16,0},{24,8},{1,17},{9,25},{17,1},{25,9},{2,18},{10... | collective-permute-start | bytes 417800 | tf_op jit(solution)/shard_map/ppermute | solution.py:326
  24.3 5.6 %collective-permute-start.7 = (bf16[544,128]{1,0:T(8,128)(2,1)S(1)}, bf16[544,128]{1,0:T(8,128)(2,1)S(1)}, u32[]{:S(2)}, u32[]{:S(2)}) collective-permute-start(bf16[544,128]{1,0:T(8,128)(2,1)S(1)} %pad_maximum_fusion.refs_5_), channel_id=1, source_target_pairs={{0,16},{8,24},{16,0},{24,8},{1,17},{9,25},{17,1},{25,9},{2,18},{10... | collective-permute-start | bytes 417800 | tf_op jit(solution)/shard_map/ppermute | solution.py:326
  25.9 5.2 %collective-permute-start.10 = (bf16[544,128]{1,0:T(8,128)(2,1)S(1)}, bf16[544,128]{1,0:T(8,128)(2,1)S(1)}, u32[]{:S(2)}, u32[]{:S(2)}) collective-permute-start(bf16[544,128]{1,0:T(8,128)(2,1)S(1)} %pad_maximum_fusion.refs_5_), channel_id=1, source_target_pairs={{0,8},{8,0},{16,24},{24,16},{1,9},{9,1},{17,25},{25,17},{2,10},{10... | collective-permute-start | bytes 417800 | tf_op jit(solution)/shard_map/ppermute | solution.py:326
  27.4 3.7 %collective-permute-start.8 = (bf16[544,128]{1,0:T(8,128)(2,1)S(1)}, bf16[544,128]{1,0:T(8,128)(2,1)S(1)}, u32[]{:S(2)}, u32[]{:S(2)}) collective-permute-start(bf16[544,128]{1,0:T(8,128)(2,1)S(1)} %pad_maximum_fusion.refs_5_), channel_id=1, source_target_pairs={{0,1},{1,0},{2,3},{3,2},{4,5},{5,4},{6,7},{7,6},{8,9},{9,8},{10,11... | collective-permute-start | bytes 417800 | tf_op jit(solution)/shard_map/ppermute | solution.py:326
  27.4 3.7 %collective-permute-start.6 = (bf16[544,128]{1,0:T(8,128)(2,1)S(1)}, bf16[544,128]{1,0:T(8,128)(2,1)S(1)}, u32[]{:S(2)}, u32[]{:S(2)}) collective-permute-start(bf16[544,128]{1,0:T(8,128)(2,1)S(1)} %collective-permute-done.1.refs_1_), channel_id=1, source_target_pairs={{0,1},{1,0},{2,3},{3,2},{4,5},{5,4},{6,7},{7,6},{8,9},{9,8},{10,11... | collective-permute-start | bytes 417800 | tf_op jit(solution)/shard_map/ppermute | solution.py:326
  29.9 1.4 %collective-permute-start.9 = (bf16[544,128]{1,0:T(8,128)(2,1)S(1)}, bf16[544,128]{1,0:T(8,128)(2,1)S(1)}, u32[]{:S(2)}, u32[]{:S(2)}) collective-permute-start(bf16[544,128]{1,0:T(8,128)(2,1)S(1)} %collective-permute-done.7.refs_6_), channel_id=1, source_target_pairs={{0,1},{1,0},{2,3},{3,2},{4,5},{5,4},{6,7},{7,6},{8,9},{9,8},{10,11... | collective-permute-start | bytes 417800 | tf_op jit(solution)/shard_map/ppermute | solution.py:326
  32.0 6.8 %collective-permute-start.11 = (bf16[64,512]{1,0:T(8,128)(2,1)S(1)}, bf16[64,512]{1,0:T(8,128)(2,1)S(1)}, u32[]{:S(2)}, u32[]{:S(2)}) collective-permute-start(bf16[64,512]{1,0:T(8,128)(2,1)S(1)} %get-tuple-element.26), channel_id=1, source_target_pairs={{0,6},{1,7},{2,4},{3,5},{4,2},{5,3},{6,0},{7,1},{8,14},{9,15},{10,... | collective-permute-start | bytes 196616 | tf_op jit(solution)/shard_map/ppermute | solution.py:326
  34.2 6.6 %collective-permute-start.12 = (bf16[64,512]{1,0:T(8,128)(2,1)S(1)}, bf16[64,512]{1,0:T(8,128)(2,1)S(1)}, u32[]{:S(2)}, u32[]{:S(2)}) collective-permute-start(bf16[64,512]{1,0:T(8,128)(2,1)S(1)} %get-tuple-element.27), channel_id=1, source_target_pairs={{0,4},{1,5},{2,6},{3,7},{4,0},{5,1},{6,2},{7,3},{8,12},{9,13},{10,... | collective-permute-start | bytes 196616 | tf_op jit(solution)/shard_map/ppermute | solution.py:326
  34.2 6.6 %collective-permute-start.13 = (bf16[64,512]{1,0:T(8,128)(2,1)S(1)}, bf16[64,512]{1,0:T(8,128)(2,1)S(1)}, u32[]{:S(2)}, u32[]{:S(2)}) collective-permute-start(bf16[64,512]{1,0:T(8,128)(2,1)S(1)} %get-tuple-element.28), channel_id=1, source_target_pairs={{0,2},{1,3},{2,0},{3,1},{4,6},{5,7},{6,4},{7,5},{8,10},{9,11},{10,... | collective-permute-start | bytes 196616 | tf_op jit(solution)/shard_map/ppermute | solution.py:326
  40.9 4.0 %collective-permute-start.14 = (bf16[32,512]{1,0:T(8,128)(2,1)S(1)}, bf16[32,512]{1,0:T(8,128)(2,1)S(1)}, u32[]{:S(2)}, u32[]{:S(2)}) collective-permute-start(bf16[32,512]{1,0:T(8,128)(2,1)S(1)} %get-tuple-element.30), channel_id=1, source_target_pairs={{0,8},{8,0},{16,24},{24,16},{1,9},{9,1},{17,25},{25,17},{2,10},{10... | collective-permute-start | bytes 98312 | tf_op jit(solution)/shard_map/ppermute | solution.py:326

commit v3 on v1

--- a/solution.py
+++ b/solution.py
@@ -7,6 +7,7 @@
 from jax.sharding import PartitionSpec as P
 
 damping = 0.1
+halves = 2
 batch = 8
 id_rows = 16
 cores = 2
@@ -39,19 +40,21 @@
     steps = rows // step_rows
     examples = feat.shape[1]
 
-    def step_copies(step):
-        rng = pl.ds(pl.multiple_of(step * step_rows, step_rows), step_rows)
+    half_rows = rows // halves
+
+    def half_copies(index):
+        rng = pl.ds(index * half_rows, half_rows)
         return (
-            pltpu.make_async_copy(act_hbm.at[rng], act.at[rng], act_sem.at[step]),
-            pltpu.make_async_copy(grad_hbm.at[rng], grad.at[rng], grad_sem.at[step]),
+            pltpu.make_async_copy(act_hbm.at[rng], act.at[rng], act_sem.at[index]),
+            pltpu.make_async_copy(grad_hbm.at[rng], grad.at[rng], grad_sem.at[index]),
         )
 
     weights = [
         pltpu.make_async_copy(pin_hbm, pin, w_sem.at[0]),
         pltpu.make_async_copy(pout_hbm, pout, w_sem.at[1]),
     ]
-    def start_step(step):
-        for priority, copy in enumerate(step_copies(step)):
+    def start_half(index):
+        for priority, copy in enumerate(half_copies(index)):
             copy.start(priority=priority)
 
     small = [
@@ -61,11 +64,11 @@
     ]
     for copy in weights:
         copy.start()
-    start_step(0)
+    start_half(0)
     for copy in small:
         copy.start()
-    for step in range(1, steps):
-        start_step(step)
+    for index in range(1, halves):
+        start_half(index)
     for copy in small:
         copy.wait()
 
@@ -85,19 +88,17 @@
     for copy in weights:
         copy.wait()
 
-    def project(step):
-        for copy in step_copies(step):
-            copy.wait()
+    def project(index):
+        rng = pl.ds(index * half_rows, half_rows)
+        act_copy, grad_copy = half_copies(index)
+        act_copy.wait()
+        act_proj[rng] = dot_nt(pin[...], act[rng]).T.astype(jnp.bfloat16)
+        grad_copy.wait()
+        grad_proj[:, rng] = dot_nt(pout[...], grad[rng]).astype(jnp.bfloat16)
+
+    def rotate(step):
         rng = pl.ds(pl.multiple_of(step * step_rows, step_rows), step_rows)
-        first, second = pl.ds(0, width // 2), pl.ds(width // 2, width // 2)
-        return (
-            (dot_nt(act[rng, first], pin[:, first]) + dot_nt(act[rng, second], pin[:, second])
-             ).astype(jnp.bfloat16),
-            (dot_nt(pout[:, first], grad[rng, first]) + dot_nt(pout[:, second], grad[rng, second])
-             ).astype(jnp.bfloat16),
-        )
-
-    def rotate(step, act_part, grad_part):
+        act_part, grad_part = act_proj[rng], grad_proj[:, rng]
         act_hi, act_lo = split_two(dot_nn(act_part, bin_hi) + dot_nn(act_part, bin_lo))
         grad_hi, grad_lo = split_two(dot_nn(bout_hi, grad_part) + dot_nn(bout_lo, grad_part))
         gt_ref[0] = grad_hi.astype(jnp.float32)
@@ -120,18 +121,13 @@
             ) * inverse[u:u + 1]
             feat[u, pl.ds(start, batch)] = value
 
-    act_proj[...], grad_proj[...] = project(0)
-
-    def body(step, carry):
-        act_part, grad_part = act_proj[...], grad_proj[...]
-        act_next, grad_next = project(step)
-        rotate(step - 1, act_part, grad_part)
-        act_proj[...] = act_next
-        grad_proj[...] = grad_next
-        return carry
-
-    lax.fori_loop(1, steps, body, 0)
-    rotate(steps - 1, act_proj[...], grad_proj[...])
+    each = steps // halves
+    project(0)
+    for index in range(1, halves):
+        project(index)
+        for step in range((index - 1) * each, index * each):
+            rotate(step)
+    lax.fori_loop(steps - each, steps, lambda step, carry: (rotate(step), carry)[1], 0)
     depth = half // slices
     me = lax.axis_index("mem") // cores
     for index in range(slices):
@@ -145,7 +141,6 @@
     examples, tokens, width = activations.shape
     rank = proj_in.shape[1]
     rows = examples * tokens
-    steps = examples // batch
     half = rank // 2
     hbm = pl.BlockSpec(memory_space=pl.ANY)
     vmem = pl.BlockSpec(memory_space=pltpu.VMEM)
@@ -165,12 +160,12 @@
             pltpu.VMEM((rank, rank), jnp.float32),
             pltpu.VMEM((rank, rank), jnp.float32),
             pltpu.VMEM((1, examples), jnp.int32),
-            pltpu.VMEM((batch * tokens, rank), jnp.bfloat16),
-            pltpu.VMEM((rank, batch * tokens), jnp.bfloat16),
+            pltpu.VMEM((rows, rank), jnp.bfloat16),
+            pltpu.VMEM((rank, rows), jnp.bfloat16),
             pltpu.VMEM((2, rank, batch * tokens), jnp.float32),
             pltpu.VMEM((half, examples, 2 * rank), jnp.float32),
-            pltpu.SemaphoreType.DMA((steps,)),
-            pltpu.SemaphoreType.DMA((steps,)),
+            pltpu.SemaphoreType.DMA((halves,)),
+            pltpu.SemaphoreType.DMA((halves,)),
             pltpu.SemaphoreType.DMA((2,)),
             pltpu.SemaphoreType.DMA((4,)),
         ],

time: 45.3 us -> 45.2 us (level)
  no operation moved by 1% of the time
where the time goes in v3:
time: 45.2 us; the launch traced here: 45.1 us
  starting transfers between devices  18.2 us (40%)
  Pallas kernels  13.1 us (29%)
  waiting for transfers between devices  12.8 us (28%)
  local copies, waits for them, and re-layouts  0.9 us (2%)
    ppermute x15, starting transfers between devices, swap(): lax.ppermute(value, axis, [(place, place ^ distance) for place in range(s...  18.2 us
    ppermute x15, waiting for transfers between devices, swap(): lax.ppermute(value, axis, [(place, place ^ distance) for place in range(s...  12.8 us
    pallas_call x1, Pallas kernels, features(): pl.pallas_call(functools.partial(feature_kernel, tokens, slices), out_sha...  11.7 us
  transfers between devices with their start and end apart: 15, of which 8 were waited for; matrix products, arithmetic and copies ran while one was open for 2% of the time, Pallas kernels for 0%

profile of v3, /device:TPU:0, one launch (start us, length us, event | category | flops | bytes accessed | tf_op | source)
XLA Modules:
  0.0 45.1 jit_solution(1987461867534351943)
XLA Ops:
  0.0 11.7 %features.1 = (bf16[272,128]{1,0:T(8,128)(2,1)}, bf16[272,128]{1,0:T(8,128)(2,1)}, bf16[272,128]{1,0:T(8,128)(2,1)}, bf16[272,128]{1,0:T(8,128)(2,1)}) custom-call(bf16[1024,4096]{1,0:T(8,128)(2,1)} %bitcast.5, bf16[1024,4096]{1,0:T(8,128)(2,1)} %bitcast.6, bf16[64,4096]{1,0:T(8,128)(2,1)} %bitcast.7, bf16[64,4096]{1,0:T(8,128)(2,1)} %bitcast.8, ...), custom_call_target="tpu_custom_call" | custom-call | flops 1073741824 | bytes 16777216 | tf_op jit(solution)/shard_map/features/pallas_call | solution.py:147
  11.7 3.1 %collective-permute-start = (bf16[272,128]{1,0:T(8,128)(2,1)}, bf16[272,128]{1,0:T(8,128)(2,1)S(1)}, u32[]{:S(2)}, u32[]{:S(2)}) collective-permute-start(bf16[272,128]{1,0:T(8,128)(2,1)} %get-tuple-element.19), channel_id=1, source_target_pairs={{0,2},{1,3},{2,0},{3,1},{4,6},{5,7},{6,4},{7,5},{8,10},{9,11},{10,... | collective-permute-start | bytes 208904 | tf_op jit(solution)/shard_map/ppermute | solution.py:321
  14.8 2.6 %collective-permute-start.2 = (bf16[272,128]{1,0:T(8,128)(2,1)}, bf16[272,128]{1,0:T(8,128)(2,1)S(1)}, u32[]{:S(2)}, u32[]{:S(2)}) collective-permute-start(bf16[272,128]{1,0:T(8,128)(2,1)} %get-tuple-element.20), channel_id=1, source_target_pairs={{0,4},{1,5},{2,6},{3,7},{4,0},{5,1},{6,2},{7,3},{8,12},{9,13},{10,... | collective-permute-start | bytes 208904 | tf_op jit(solution)/shard_map/ppermute | solution.py:321
  17.4 0.0 collective-permute-start.3
  17.4 0.9 %constant_dynamic-update-slice_fusion.1 = bf16[544,128]{1,0:T(8,128)(2,1)S(1)} fusion(bf16[272,128]{1,0:T(8,128)(2,1)} %get-tuple-element.18), kind=kLoop, calls=%fused_computation.2 | loop fusion | bytes 139264
  18.3 0.1 collective-permute-start.4
  18.4 1.8 %collective-permute-start.5 = (bf16[544,128]{1,0:T(8,128)(2,1)S(1)}, bf16[544,128]{1,0:T(8,128)(2,1)S(1)}, u32[]{:S(2)}, u32[]{:S(2)}) collective-permute-start(bf16[544,128]{1,0:T(8,128)(2,1)S(1)} %constant_dynamic-update-slice_fusion.refs_0_), channel_id=1, source_target_pairs={{0,8},{8,0},{16,24},{24,16},{1,9},{9,1},{17,25},{25,17},{2,10},{10... | collective-permute-start | bytes 417800 | tf_op jit(solution)/shard_map/ppermute | solution.py:321
  20.2 1.5 %collective-permute-start.1 = (bf16[544,128]{1,0:T(8,128)(2,1)S(1)}, bf16[544,128]{1,0:T(8,128)(2,1)S(1)}, u32[]{:S(2)}, u32[]{:S(2)}) collective-permute-start(bf16[544,128]{1,0:T(8,128)(2,1)S(1)} %constant_dynamic-update-slice_fusion.refs_0_), channel_id=1, source_target_pairs={{0,16},{8,24},{16,0},{24,8},{1,17},{9,25},{17,1},{25,9},{2,18},{10... | collective-permute-start | bytes 417800 | tf_op jit(solution)/shard_map/ppermute | solution.py:321
  21.7 0.9 %collective-permute-done.2 = bf16[272,128]{1,0:T(8,128)(2,1)S(1)} collective-permute-done((bf16[272,128]{1,0:T(8,128)(2,1)}, bf16[272,128]{1,0:T(8,128)(2,1)S(1)}, u32[]{:S(2)}, u32[]{:S(2)}) %collective-permute-start.2) | collective-permute-done | bytes 69664 | tf_op jit(solution)/shard_map/ppermute | solution.py:321
  22.5 1.3 %collective-permute-done.3 = bf16[272,128]{1,0:T(8,128)(2,1)S(1)} collective-permute-done((bf16[272,128]{1,0:T(8,128)(2,1)}, bf16[272,128]{1,0:T(8,128)(2,1)S(1)}, u32[]{:S(2)}, u32[]{:S(2)}) %collective-permute-start.3) | collective-permute-done | bytes 69664 | tf_op jit(solution)/shard_map/ppermute | solution.py:321
  23.8 1.6 %collective-permute-start.7 = (bf16[544,128]{1,0:T(8,128)(2,1)S(1)}, bf16[544,128]{1,0:T(8,128)(2,1)S(1)}, u32[]{:S(2)}, u32[]{:S(2)}) collective-permute-start(bf16[544,128]{1,0:T(8,128)(2,1)S(1)} %pad_maximum_fusion.refs_5_), channel_id=1, source_target_pairs={{0,16},{8,24},{16,0},{24,8},{1,17},{9,25},{17,1},{25,9},{2,18},{10... | collective-permute-start | bytes 417800 | tf_op jit(solution)/shard_map/ppermute | solution.py:321
  25.4 1.5 %collective-permute-start.10 = (bf16[544,128]{1,0:T(8,128)(2,1)S(1)}, bf16[544,128]{1,0:T(8,128)(2,1)S(1)}, u32[]{:S(2)}, u32[]{:S(2)}) collective-permute-start(bf16[544,128]{1,0:T(8,128)(2,1)S(1)} %pad_maximum_fusion.refs_5_), channel_id=1, source_target_pairs={{0,8},{8,0},{16,24},{24,16},{1,9},{9,1},{17,25},{25,17},{2,10},{10... | collective-permute-start | bytes 417800 | tf_op jit(solution)/shard_map/ppermute | solution.py:321
  26.9 0.5 %collective-permute-start.6 = (bf16[544,128]{1,0:T(8,128)(2,1)S(1)}, bf16[544,128]{1,0:T(8,128)(2,1)S(1)}, u32[]{:S(2)}, u32[]{:S(2)}) collective-permute-start(bf16[544,128]{1,0:T(8,128)(2,1)S(1)} %collective-permute-done.1.refs_1_), channel_id=1, source_target_pairs={{0,1},{1,0},{2,3},{3,2},{4,5},{5,4},{6,7},{7,6},{8,9},{9,8},{10,11... | collective-permute-start | bytes 417800 | tf_op jit(solution)/shard_map/ppermute | solution.py:321
  27.4 1.5 %collective-permute-done.7.refs_6_ = bf16[544,128]{1,0:T(8,128)(2,1)S(1)} collective-permute-done((bf16[544,128]{1,0:T(8,128)(2,1)S(1)}, bf16[544,128]{1,0:T(8,128)(2,1)S(1)}, u32[]{:S(2)}, u32[]{:S(2)}) %collective-permute-start.7) | collective-permute-done | bytes 139296 | tf_op jit(solution)/shard_map/ppermute | solution.py:321
  29.0 1.5 %collective-permute-done.10.refs_9_ = bf16[544,128]{1,0:T(8,128)(2,1)S(1)} collective-permute-done((bf16[544,128]{1,0:T(8,128)(2,1)S(1)}, bf16[544,128]{1,0:T(8,128)(2,1)S(1)}, u32[]{:S(2)}, u32[]{:S(2)}) %collective-permute-start.10) | collective-permute-done | bytes 139296 | tf_op jit(solution)/shard_map/ppermute | solution.py:321
  30.5 0.7 %products.1 = (bf16[64,512]{1,0:T(8,128)(2,1)S(1)}, bf16[64,512]{1,0:T(8,128)(2,1)S(1)}, bf16[64,512]{1,0:T(8,128)(2,1)S(1)}, bf16[64,512]{1,0:T(8,128)(2,1)S(1)}) custom-call(bf16[544,128]{1,0:T(8,128)(2,1)S(1)} %constant_dynamic-update-slice_fusion.refs_0_, bf16[544,128]{1,0:T(8,128)(2,1)S(1)} %collective-permute-done.1.refs_1_, ...), custom_call_target="tpu_custom_call" | custom-call | flops 268435456 | bytes 524288 | tf_op jit(solution)/shard_map/products/pallas_call | solution.py:246
  31.2 3.4 %collective-permute-start.11 = (bf16[64,512]{1,0:T(8,128)(2,1)S(1)}, bf16[64,512]{1,0:T(8,128)(2,1)S(1)}, u32[]{:S(2)}, u32[]{:S(2)}) collective-permute-start(bf16[64,512]{1,0:T(8,128)(2,1)S(1)} %get-tuple-element.26), channel_id=1, source_target_pairs={{0,6},{1,7},{2,4},{3,5},{4,2},{5,3},{6,0},{7,1},{8,14},{9,15},{10,... | collective-permute-start | bytes 196616 | tf_op jit(solution)/shard_map/ppermute | solution.py:321
  34.7 1.0 %collective-permute-start.13 = (bf16[64,512]{1,0:T(8,128)(2,1)S(1)}, bf16[64,512]{1,0:T(8,128)(2,1)S(1)}, u32[]{:S(2)}, u32[]{:S(2)}) collective-permute-start(bf16[64,512]{1,0:T(8,128)(2,1)S(1)} %get-tuple-element.28), channel_id=1, source_target_pairs={{0,2},{1,3},{2,0},{3,1},{4,6},{5,7},{6,4},{7,5},{8,10},{9,11},{10,... | collective-permute-start | bytes 196616 | tf_op jit(solution)/shard_map/ppermute | solution.py:321
  35.7 2.4 %collective-permute-done.11.refs_1_ = bf16[64,512]{1,0:T(8,128)(2,1)S(1)} collective-permute-done((bf16[64,512]{1,0:T(8,128)(2,1)S(1)}, bf16[64,512]{1,0:T(8,128)(2,1)S(1)}, u32[]{:S(2)}, u32[]{:S(2)}) %collective-permute-start.11) | collective-permute-done | bytes 65568 | tf_op jit(solution)/shard_map/ppermute | solution.py:321
  38.1 2.1 %collective-permute-done.12.refs_2_ = bf16[64,512]{1,0:T(8,128)(2,1)S(1)} collective-permute-done((bf16[64,512]{1,0:T(8,128)(2,1)S(1)}, bf16[64,512]{1,0:T(8,128)(2,1)S(1)}, u32[]{:S(2)}, u32[]{:S(2)}) %collective-permute-start.12) | collective-permute-done | bytes 65568 | tf_op jit(solution)/shard_map/ppermute | solution.py:321
  40.2 0.2 collective-permute-done.13.refs_3_
  40.4 1.1 %collective-permute-start.14 = (bf16[32,512]{1,0:T(8,128)(2,1)S(1)}, bf16[32,512]{1,0:T(8,128)(2,1)S(1)}, u32[]{:S(2)}, u32[]{:S(2)}) collective-permute-start(bf16[32,512]{1,0:T(8,128)(2,1)S(1)} %get-tuple-element.30), channel_id=1, source_target_pairs={{0,8},{8,0},{16,24},{24,16},{1,9},{9,1},{17,25},{25,17},{2,10},{10... | collective-permute-start | bytes 98312 | tf_op jit(solution)/shard_map/ppermute | solution.py:321
  41.5 2.9 %collective-permute-done.14.refs_1_ = bf16[32,512]{1,0:T(8,128)(2,1)S(1)} collective-permute-done((bf16[32,512]{1,0:T(8,128)(2,1)S(1)}, bf16[32,512]{1,0:T(8,128)(2,1)S(1)}, u32[]{:S(2)}, u32[]{:S(2)}) %collective-permute-start.14) | collective-permute-done | bytes 32800 | tf_op jit(solution)/shard_map/ppermute | solution.py:321
  44.4 0.7 %finish.1 = f32[32,1024]{1,0:T(8,128)} custom-call(f32[32,512]{1,0:T(8,128)S(1)} %get-tuple-element.29.refs_0_, bf16[32,512]{1,0:T(8,128)(2,1)S(1)} %collective-permute-done.14.refs_1_), custom_call_target="tpu_custom_call" | custom-call | flops 131072 | bytes 262144 | tf_op jit(solution)/shard_map/finish/pallas_call | solution.py:306
  (13 shorter events, 0.1 us)
Async XLA Ops:
  11.7 6.6 %collective-permute-start = (bf16[272,128]{1,0:T(8,128)(2,1)}, bf16[272,128]{1,0:T(8,128)(2,1)S(1)}, u32[]{:S(2)}, u32[]{:S(2)}) collective-permute-start(bf16[272,128]{1,0:T(8,128)(2,1)} %get-tuple-element.19), channel_id=1, source_target_pairs={{0,2},{1,3},{2,0},{3,1},{4,6},{5,7},{6,4},{7,5},{8,10},{9,11},{10,... | collective-permute-start | bytes 208904 | tf_op jit(solution)/shard_map/ppermute | solution.py:321
  14.8 7.7 %collective-permute-start.2 = (bf16[272,128]{1,0:T(8,128)(2,1)}, bf16[272,128]{1,0:T(8,128)(2,1)S(1)}, u32[]{:S(2)}, u32[]{:S(2)}) collective-permute-start(bf16[272,128]{1,0:T(8,128)(2,1)} %get-tuple-element.20), channel_id=1, source_target_pairs={{0,4},{1,5},{2,6},{3,7},{4,0},{5,1},{6,2},{7,3},{8,12},{9,13},{10,... | collective-permute-start | bytes 208904 | tf_op jit(solution)/shard_map/ppermute | solution.py:321
  17.4 6.4 %collective-permute-start.3 = (bf16[272,128]{1,0:T(8,128)(2,1)}, bf16[272,128]{1,0:T(8,128)(2,1)S(1)}, u32[]{:S(2)}, u32[]{:S(2)}) collective-permute-start(bf16[272,128]{1,0:T(8,128)(2,1)} %get-tuple-element.21), channel_id=1, source_target_pairs={{0,6},{1,7},{2,4},{3,5},{4,2},{5,3},{6,0},{7,1},{8,14},{9,15},{10,... | collective-permute-start | bytes 208904 | tf_op jit(solution)/shard_map/ppermute | solution.py:321
  18.3 5.5 %collective-permute-start.4 = (bf16[544,128]{1,0:T(8,128)(2,1)S(1)}, bf16[544,128]{1,0:T(8,128)(2,1)S(1)}, u32[]{:S(2)}, u32[]{:S(2)}) collective-permute-start(bf16[544,128]{1,0:T(8,128)(2,1)S(1)} %constant_dynamic-update-slice_fusion.refs_0_), channel_id=1, source_target_pairs={{0,1},{1,0},{2,3},{3,2},{4,5},{5,4},{6,7},{7,6},{8,9},{9,8},{10,11... | collective-permute-start | bytes 417800 | tf_op jit(solution)/shard_map/ppermute | solution.py:321
  18.4 8.5 %collective-permute-start.5 = (bf16[544,128]{1,0:T(8,128)(2,1)S(1)}, bf16[544,128]{1,0:T(8,128)(2,1)S(1)}, u32[]{:S(2)}, u32[]{:S(2)}) collective-permute-start(bf16[544,128]{1,0:T(8,128)(2,1)S(1)} %constant_dynamic-update-slice_fusion.refs_0_), channel_id=1, source_target_pairs={{0,8},{8,0},{16,24},{24,16},{1,9},{9,1},{17,25},{25,17},{2,10},{10... | collective-permute-start | bytes 417800 | tf_op jit(solution)/shard_map/ppermute | solution.py:321
  20.2 6.8 %collective-permute-start.1 = (bf16[544,128]{1,0:T(8,128)(2,1)S(1)}, bf16[544,128]{1,0:T(8,128)(2,1)S(1)}, u32[]{:S(2)}, u32[]{:S(2)}) collective-permute-start(bf16[544,128]{1,0:T(8,128)(2,1)S(1)} %constant_dynamic-update-slice_fusion.refs_0_), channel_id=1, source_target_pairs={{0,16},{8,24},{16,0},{24,8},{1,17},{9,25},{17,1},{25,9},{2,18},{10... | collective-permute-start | bytes 417800 | tf_op jit(solution)/shard_map/ppermute | solution.py:321
  23.8 5.1 %collective-permute-start.7 = (bf16[544,128]{1,0:T(8,128)(2,1)S(1)}, bf16[544,128]{1,0:T(8,128)(2,1)S(1)}, u32[]{:S(2)}, u32[]{:S(2)}) collective-permute-start(bf16[544,128]{1,0:T(8,128)(2,1)S(1)} %pad_maximum_fusion.refs_5_), channel_id=1, source_target_pairs={{0,16},{8,24},{16,0},{24,8},{1,17},{9,25},{17,1},{25,9},{2,18},{10... | collective-permute-start | bytes 417800 | tf_op jit(solution)/shard_map/ppermute | solution.py:321
  25.4 5.1 %collective-permute-start.10 = (bf16[544,128]{1,0:T(8,128)(2,1)S(1)}, bf16[544,128]{1,0:T(8,128)(2,1)S(1)}, u32[]{:S(2)}, u32[]{:S(2)}) collective-permute-start(bf16[544,128]{1,0:T(8,128)(2,1)S(1)} %pad_maximum_fusion.refs_5_), channel_id=1, source_target_pairs={{0,8},{8,0},{16,24},{24,16},{1,9},{9,1},{17,25},{25,17},{2,10},{10... | collective-permute-start | bytes 417800 | tf_op jit(solution)/shard_map/ppermute | solution.py:321
  26.9 3.6 %collective-permute-start.8 = (bf16[544,128]{1,0:T(8,128)(2,1)S(1)}, bf16[544,128]{1,0:T(8,128)(2,1)S(1)}, u32[]{:S(2)}, u32[]{:S(2)}) collective-permute-start(bf16[544,128]{1,0:T(8,128)(2,1)S(1)} %pad_maximum_fusion.refs_5_), channel_id=1, source_target_pairs={{0,1},{1,0},{2,3},{3,2},{4,5},{5,4},{6,7},{7,6},{8,9},{9,8},{10,11... | collective-permute-start | bytes 417800 | tf_op jit(solution)/shard_map/ppermute | solution.py:321
  26.9 3.6 %collective-permute-start.6 = (bf16[544,128]{1,0:T(8,128)(2,1)S(1)}, bf16[544,128]{1,0:T(8,128)(2,1)S(1)}, u32[]{:S(2)}, u32[]{:S(2)}) collective-permute-start(bf16[544,128]{1,0:T(8,128)(2,1)S(1)} %collective-permute-done.1.refs_1_), channel_id=1, source_target_pairs={{0,1},{1,0},{2,3},{3,2},{4,5},{5,4},{6,7},{7,6},{8,9},{9,8},{10,11... | collective-permute-start | bytes 417800 | tf_op jit(solution)/shard_map/ppermute | solution.py:321
  29.0 1.5 %collective-permute-start.9 = (bf16[544,128]{1,0:T(8,128)(2,1)S(1)}, bf16[544,128]{1,0:T(8,128)(2,1)S(1)}, u32[]{:S(2)}, u32[]{:S(2)}) collective-permute-start(bf16[544,128]{1,0:T(8,128)(2,1)S(1)} %collective-permute-done.7.refs_6_), channel_id=1, source_target_pairs={{0,1},{1,0},{2,3},{3,2},{4,5},{5,4},{6,7},{7,6},{8,9},{9,8},{10,11... | collective-permute-start | bytes 417800 | tf_op jit(solution)/shard_map/ppermute | solution.py:321
  31.2 6.9 %collective-permute-start.11 = (bf16[64,512]{1,0:T(8,128)(2,1)S(1)}, bf16[64,512]{1,0:T(8,128)(2,1)S(1)}, u32[]{:S(2)}, u32[]{:S(2)}) collective-permute-start(bf16[64,512]{1,0:T(8,128)(2,1)S(1)} %get-tuple-element.26), channel_id=1, source_target_pairs={{0,6},{1,7},{2,4},{3,5},{4,2},{5,3},{6,0},{7,1},{8,14},{9,15},{10,... | collective-permute-start | bytes 196616 | tf_op jit(solution)/shard_map/ppermute | solution.py:321
  34.7 5.6 %collective-permute-start.12 = (bf16[64,512]{1,0:T(8,128)(2,1)S(1)}, bf16[64,512]{1,0:T(8,128)(2,1)S(1)}, u32[]{:S(2)}, u32[]{:S(2)}) collective-permute-start(bf16[64,512]{1,0:T(8,128)(2,1)S(1)} %get-tuple-element.27), channel_id=1, source_target_pairs={{0,4},{1,5},{2,6},{3,7},{4,0},{5,1},{6,2},{7,3},{8,12},{9,13},{10,... | collective-permute-start | bytes 196616 | tf_op jit(solution)/shard_map/ppermute | solution.py:321
  34.7 5.7 %collective-permute-start.13 = (bf16[64,512]{1,0:T(8,128)(2,1)S(1)}, bf16[64,512]{1,0:T(8,128)(2,1)S(1)}, u32[]{:S(2)}, u32[]{:S(2)}) collective-permute-start(bf16[64,512]{1,0:T(8,128)(2,1)S(1)} %get-tuple-element.28), channel_id=1, source_target_pairs={{0,2},{1,3},{2,0},{3,1},{4,6},{5,7},{6,4},{7,5},{8,10},{9,11},{10,... | collective-permute-start | bytes 196616 | tf_op jit(solution)/shard_map/ppermute | solution.py:321
  40.4 4.0 %collective-permute-start.14 = (bf16[32,512]{1,0:T(8,128)(2,1)S(1)}, bf16[32,512]{1,0:T(8,128)(2,1)S(1)}, u32[]{:S(2)}, u32[]{:S(2)}) collective-permute-start(bf16[32,512]{1,0:T(8,128)(2,1)S(1)} %get-tuple-element.30), channel_id=1, source_target_pairs={{0,8},{8,0},{16,24},{24,16},{1,9},{9,1},{17,25},{25,17},{2,10},{10... | collective-permute-start | bytes 98312 | tf_op jit(solution)/shard_map/ppermute | solution.py:321

commit v4 on v3

--- a/solution.py
+++ b/solution.py
@@ -88,31 +88,35 @@
     for copy in weights:
         copy.wait()
 
-    def project(index):
+    def project(index, beside):
         rng = pl.ds(index * half_rows, half_rows)
         act_copy, grad_copy = half_copies(index)
         act_copy.wait()
         act_proj[rng] = dot_nt(pin[...], act[rng]).T.astype(jnp.bfloat16)
+        for step in beside[0::2]:
+            rotate(step)
         grad_copy.wait()
         grad_proj[:, rng] = dot_nt(pout[...], grad[rng]).astype(jnp.bfloat16)
+        for step in beside[1::2]:
+            rotate(step)
 
     def rotate(step):
-        rng = pl.ds(pl.multiple_of(step * step_rows, step_rows), step_rows)
+        rng = pl.ds(step * step_rows, step_rows)
         act_part, grad_part = act_proj[rng], grad_proj[:, rng]
         act_hi, act_lo = split_two(dot_nn(act_part, bin_hi) + dot_nn(act_part, bin_lo))
         grad_hi, grad_lo = split_two(dot_nn(bout_hi, grad_part) + dot_nn(bout_lo, grad_part))
-        gt_ref[0] = grad_hi.astype(jnp.float32)
-        gt_ref[1] = grad_lo.astype(jnp.float32)
+        gt_ref[step, 0] = grad_hi.astype(jnp.float32)
+        gt_ref[step, 1] = grad_lo.astype(jnp.float32)
         spread_hi, spread_lo = [
             jnp.concatenate([
-                jnp.where(own_token, jnp.broadcast_to(gt_ref[part, pl.ds(u, 1)], (batch, step_rows)), 0.0)
+                jnp.where(own_token, jnp.broadcast_to(gt_ref[step, part, pl.ds(u, 1)], (batch, step_rows)), 0.0)
                 for u in range(rank)
             ], axis=0).astype(jnp.bfloat16)
             for part in range(2)
         ]
         wide = dot_nn(spread_hi, jnp.concatenate([act_hi, act_lo], axis=1))
         rotated = wide[:, :2 * rank] + wide[:, 2 * rank:] + dot_nn(spread_lo, act_hi)
-        start = pl.multiple_of(step * batch, batch)
+        start = step * batch
         for u in range(half):
             value = jnp.where(
                 first_lanes,
@@ -122,12 +126,13 @@
             feat[u, pl.ds(start, batch)] = value
 
     each = steps // halves
-    project(0)
-    for index in range(1, halves):
-        project(index)
-        for step in range((index - 1) * each, index * each):
-            rotate(step)
-    lax.fori_loop(steps - each, steps, lambda step, carry: (rotate(step), carry)[1], 0)
+    for index in range(halves + 1):
+        beside = list(range(max(index - 1, 0) * each, index * each))
+        if index < halves:
+            project(index, beside)
+        else:
+            for step in beside:
+                rotate(step)
     depth = half // slices
     me = lax.axis_index("mem") // cores
     for index in range(slices):
@@ -162,7 +167,7 @@
             pltpu.VMEM((1, examples), jnp.int32),
             pltpu.VMEM((rows, rank), jnp.bfloat16),
             pltpu.VMEM((rank, rows), jnp.bfloat16),
-            pltpu.VMEM((2, rank, batch * tokens), jnp.float32),
+            pltpu.VMEM((examples // batch, 2, rank, batch * tokens), jnp.float32),
             pltpu.VMEM((half, examples, 2 * rank), jnp.float32),
             pltpu.SemaphoreType.DMA((halves,)),
             pltpu.SemaphoreType.DMA((halves,)),

time: 45.2 us -> 44.9 us (level)
  no operation moved by 1% of the time
where the time goes in v4:
time: 44.9 us; the launch traced here: 44.7 us
  starting transfers between devices  18.2 us (41%)
  Pallas kernels  12.8 us (29%)
  waiting for transfers between devices  12.8 us (29%)
  local copies, waits for them, and re-layouts  0.9 us (2%)
    ppermute x15, starting transfers between devices, swap(): lax.ppermute(value, axis, [(place, place ^ distance) for place in range(s...  18.2 us
    ppermute x15, waiting for transfers between devices, swap(): lax.ppermute(value, axis, [(place, place ^ distance) for place in range(s...  12.8 us
    pallas_call x1, Pallas kernels, features(): pl.pallas_call(functools.partial(feature_kernel, tokens, slices), out_sha...  11.4 us
  transfers between devices with their start and end apart: 15, of which 8 were waited for; matrix products, arithmetic and copies ran while one was open for 2% of the time, Pallas kernels for 0%

profile of v4, /device:TPU:0, one launch (start us, length us, event | category | flops | bytes accessed | tf_op | source)
XLA Modules:
  0.0 44.7 jit_solution(938790322037684686)
XLA Ops:
  0.0 11.4 %features.1 = (bf16[272,128]{1,0:T(8,128)(2,1)}, bf16[272,128]{1,0:T(8,128)(2,1)}, bf16[272,128]{1,0:T(8,128)(2,1)}, bf16[272,128]{1,0:T(8,128)(2,1)}) custom-call(bf16[1024,4096]{1,0:T(8,128)(2,1)} %bitcast.5, bf16[1024,4096]{1,0:T(8,128)(2,1)} %bitcast.6, bf16[64,4096]{1,0:T(8,128)(2,1)} %bitcast.7, bf16[64,4096]{1,0:T(8,128)(2,1)} %bitcast.8, ...), custom_call_target="tpu_custom_call" | custom-call | flops 1073741824 | bytes 16777216 | tf_op jit(solution)/shard_map/features/pallas_call | solution.py:152
  11.4 3.1 %collective-permute-start = (bf16[272,128]{1,0:T(8,128)(2,1)}, bf16[272,128]{1,0:T(8,128)(2,1)S(1)}, u32[]{:S(2)}, u32[]{:S(2)}) collective-permute-start(bf16[272,128]{1,0:T(8,128)(2,1)} %get-tuple-element.19), channel_id=1, source_target_pairs={{0,2},{1,3},{2,0},{3,1},{4,6},{5,7},{6,4},{7,5},{8,10},{9,11},{10,... | collective-permute-start | bytes 208904 | tf_op jit(solution)/shard_map/ppermute | solution.py:326
  14.5 2.6 %collective-permute-start.2 = (bf16[272,128]{1,0:T(8,128)(2,1)}, bf16[272,128]{1,0:T(8,128)(2,1)S(1)}, u32[]{:S(2)}, u32[]{:S(2)}) collective-permute-start(bf16[272,128]{1,0:T(8,128)(2,1)} %get-tuple-element.20), channel_id=1, source_target_pairs={{0,4},{1,5},{2,6},{3,7},{4,0},{5,1},{6,2},{7,3},{8,12},{9,13},{10,... | collective-permute-start | bytes 208904 | tf_op jit(solution)/shard_map/ppermute | solution.py:326
  17.0 0.9 %constant_dynamic-update-slice_fusion.1 = bf16[544,128]{1,0:T(8,128)(2,1)S(1)} fusion(bf16[272,128]{1,0:T(8,128)(2,1)} %get-tuple-element.18), kind=kLoop, calls=%fused_computation.2 | loop fusion | bytes 139264
  18.0 0.1 collective-permute-start.4
  18.0 1.8 %collective-permute-start.5 = (bf16[544,128]{1,0:T(8,128)(2,1)S(1)}, bf16[544,128]{1,0:T(8,128)(2,1)S(1)}, u32[]{:S(2)}, u32[]{:S(2)}) collective-permute-start(bf16[544,128]{1,0:T(8,128)(2,1)S(1)} %constant_dynamic-update-slice_fusion.refs_0_), channel_id=1, source_target_pairs={{0,8},{8,0},{16,24},{24,16},{1,9},{9,1},{17,25},{25,17},{2,10},{10... | collective-permute-start | bytes 417800 | tf_op jit(solution)/shard_map/ppermute | solution.py:326
  19.8 1.5 %collective-permute-start.1 = (bf16[544,128]{1,0:T(8,128)(2,1)S(1)}, bf16[544,128]{1,0:T(8,128)(2,1)S(1)}, u32[]{:S(2)}, u32[]{:S(2)}) collective-permute-start(bf16[544,128]{1,0:T(8,128)(2,1)S(1)} %constant_dynamic-update-slice_fusion.refs_0_), channel_id=1, source_target_pairs={{0,16},{8,24},{16,0},{24,8},{1,17},{9,25},{17,1},{25,9},{2,18},{10... | collective-permute-start | bytes 417800 | tf_op jit(solution)/shard_map/ppermute | solution.py:326
  21.3 0.9 %collective-permute-done.2 = bf16[272,128]{1,0:T(8,128)(2,1)S(1)} collective-permute-done((bf16[272,128]{1,0:T(8,128)(2,1)}, bf16[272,128]{1,0:T(8,128)(2,1)S(1)}, u32[]{:S(2)}, u32[]{:S(2)}) %collective-permute-start.2) | collective-permute-done | bytes 69664 | tf_op jit(solution)/shard_map/ppermute | solution.py:326
  22.2 1.3 %collective-permute-done.3 = bf16[272,128]{1,0:T(8,128)(2,1)S(1)} collective-permute-done((bf16[272,128]{1,0:T(8,128)(2,1)}, bf16[272,128]{1,0:T(8,128)(2,1)S(1)}, u32[]{:S(2)}, u32[]{:S(2)}) %collective-permute-start.3) | collective-permute-done | bytes 69664 | tf_op jit(solution)/shard_map/ppermute | solution.py:326
  23.5 1.6 %collective-permute-start.7 = (bf16[544,128]{1,0:T(8,128)(2,1)S(1)}, bf16[544,128]{1,0:T(8,128)(2,1)S(1)}, u32[]{:S(2)}, u32[]{:S(2)}) collective-permute-start(bf16[544,128]{1,0:T(8,128)(2,1)S(1)} %pad_maximum_fusion.refs_5_), channel_id=1, source_target_pairs={{0,16},{8,24},{16,0},{24,8},{1,17},{9,25},{17,1},{25,9},{2,18},{10... | collective-permute-start | bytes 417800 | tf_op jit(solution)/shard_map/ppermute | solution.py:326
  25.1 1.5 %collective-permute-start.10 = (bf16[544,128]{1,0:T(8,128)(2,1)S(1)}, bf16[544,128]{1,0:T(8,128)(2,1)S(1)}, u32[]{:S(2)}, u32[]{:S(2)}) collective-permute-start(bf16[544,128]{1,0:T(8,128)(2,1)S(1)} %pad_maximum_fusion.refs_5_), channel_id=1, source_target_pairs={{0,8},{8,0},{16,24},{24,16},{1,9},{9,1},{17,25},{25,17},{2,10},{10... | collective-permute-start | bytes 417800 | tf_op jit(solution)/shard_map/ppermute | solution.py:326
  26.6 0.0 collective-permute-start.8
  26.6 0.5 %collective-permute-start.6 = (bf16[544,128]{1,0:T(8,128)(2,1)S(1)}, bf16[544,128]{1,0:T(8,128)(2,1)S(1)}, u32[]{:S(2)}, u32[]{:S(2)}) collective-permute-start(bf16[544,128]{1,0:T(8,128)(2,1)S(1)} %collective-permute-done.1.refs_1_), channel_id=1, source_target_pairs={{0,1},{1,0},{2,3},{3,2},{4,5},{5,4},{6,7},{7,6},{8,9},{9,8},{10,11... | collective-permute-start | bytes 417800 | tf_op jit(solution)/shard_map/ppermute | solution.py:326
  27.1 1.5 %collective-permute-done.7.refs_6_ = bf16[544,128]{1,0:T(8,128)(2,1)S(1)} collective-permute-done((bf16[544,128]{1,0:T(8,128)(2,1)S(1)}, bf16[544,128]{1,0:T(8,128)(2,1)S(1)}, u32[]{:S(2)}, u32[]{:S(2)}) %collective-permute-start.7) | collective-permute-done | bytes 139296 | tf_op jit(solution)/shard_map/ppermute | solution.py:326
  28.6 1.5 %collective-permute-done.10.refs_9_ = bf16[544,128]{1,0:T(8,128)(2,1)S(1)} collective-permute-done((bf16[544,128]{1,0:T(8,128)(2,1)S(1)}, bf16[544,128]{1,0:T(8,128)(2,1)S(1)}, u32[]{:S(2)}, u32[]{:S(2)}) %collective-permute-start.10) | collective-permute-done | bytes 139296 | tf_op jit(solution)/shard_map/ppermute | solution.py:326
  30.1 0.7 %products.1 = (bf16[64,512]{1,0:T(8,128)(2,1)S(1)}, bf16[64,512]{1,0:T(8,128)(2,1)S(1)}, bf16[64,512]{1,0:T(8,128)(2,1)S(1)}, bf16[64,512]{1,0:T(8,128)(2,1)S(1)}) custom-call(bf16[544,128]{1,0:T(8,128)(2,1)S(1)} %constant_dynamic-update-slice_fusion.refs_0_, bf16[544,128]{1,0:T(8,128)(2,1)S(1)} %collective-permute-done.1.refs_1_, ...), custom_call_target="tpu_custom_call" | custom-call | flops 268435456 | bytes 524288 | tf_op jit(solution)/shard_map/products/pallas_call | solution.py:251
  30.9 3.4 %collective-permute-start.11 = (bf16[64,512]{1,0:T(8,128)(2,1)S(1)}, bf16[64,512]{1,0:T(8,128)(2,1)S(1)}, u32[]{:S(2)}, u32[]{:S(2)}) collective-permute-start(bf16[64,512]{1,0:T(8,128)(2,1)S(1)} %get-tuple-element.26), channel_id=1, source_target_pairs={{0,6},{1,7},{2,4},{3,5},{4,2},{5,3},{6,0},{7,1},{8,14},{9,15},{10,... | collective-permute-start | bytes 196616 | tf_op jit(solution)/shard_map/ppermute | solution.py:326
  34.3 1.0 %collective-permute-start.13 = (bf16[64,512]{1,0:T(8,128)(2,1)S(1)}, bf16[64,512]{1,0:T(8,128)(2,1)S(1)}, u32[]{:S(2)}, u32[]{:S(2)}) collective-permute-start(bf16[64,512]{1,0:T(8,128)(2,1)S(1)} %get-tuple-element.28), channel_id=1, source_target_pairs={{0,2},{1,3},{2,0},{3,1},{4,6},{5,7},{6,4},{7,5},{8,10},{9,11},{10,... | collective-permute-start | bytes 196616 | tf_op jit(solution)/shard_map/ppermute | solution.py:326
  35.3 2.4 %collective-permute-done.11.refs_1_ = bf16[64,512]{1,0:T(8,128)(2,1)S(1)} collective-permute-done((bf16[64,512]{1,0:T(8,128)(2,1)S(1)}, bf16[64,512]{1,0:T(8,128)(2,1)S(1)}, u32[]{:S(2)}, u32[]{:S(2)}) %collective-permute-start.11) | collective-permute-done | bytes 65568 | tf_op jit(solution)/shard_map/ppermute | solution.py:326
  37.7 2.1 %collective-permute-done.12.refs_2_ = bf16[64,512]{1,0:T(8,128)(2,1)S(1)} collective-permute-done((bf16[64,512]{1,0:T(8,128)(2,1)S(1)}, bf16[64,512]{1,0:T(8,128)(2,1)S(1)}, u32[]{:S(2)}, u32[]{:S(2)}) %collective-permute-start.12) | collective-permute-done | bytes 65568 | tf_op jit(solution)/shard_map/ppermute | solution.py:326
  39.9 0.2 collective-permute-done.13.refs_3_
  40.1 1.1 %collective-permute-start.14 = (bf16[32,512]{1,0:T(8,128)(2,1)S(1)}, bf16[32,512]{1,0:T(8,128)(2,1)S(1)}, u32[]{:S(2)}, u32[]{:S(2)}) collective-permute-start(bf16[32,512]{1,0:T(8,128)(2,1)S(1)} %get-tuple-element.30), channel_id=1, source_target_pairs={{0,8},{8,0},{16,24},{24,16},{1,9},{9,1},{17,25},{25,17},{2,10},{10... | collective-permute-start | bytes 98312 | tf_op jit(solution)/shard_map/ppermute | solution.py:326
  41.2 2.9 %collective-permute-done.14.refs_1_ = bf16[32,512]{1,0:T(8,128)(2,1)S(1)} collective-permute-done((bf16[32,512]{1,0:T(8,128)(2,1)S(1)}, bf16[32,512]{1,0:T(8,128)(2,1)S(1)}, u32[]{:S(2)}, u32[]{:S(2)}) %collective-permute-start.14) | collective-permute-done | bytes 32800 | tf_op jit(solution)/shard_map/ppermute | solution.py:326
  44.1 0.7 %finish.1 = f32[32,1024]{1,0:T(8,128)} custom-call(f32[32,512]{1,0:T(8,128)S(1)} %get-tuple-element.29.refs_0_, bf16[32,512]{1,0:T(8,128)(2,1)S(1)} %collective-permute-done.14.refs_1_), custom_call_target="tpu_custom_call" | custom-call | flops 131072 | bytes 262144 | tf_op jit(solution)/shard_map/finish/pallas_call | solution.py:311
  (13 shorter events, 0.1 us)
Async XLA Ops:
  11.4 6.6 %collective-permute-start = (bf16[272,128]{1,0:T(8,128)(2,1)}, bf16[272,128]{1,0:T(8,128)(2,1)S(1)}, u32[]{:S(2)}, u32[]{:S(2)}) collective-permute-start(bf16[272,128]{1,0:T(8,128)(2,1)} %get-tuple-element.19), channel_id=1, source_target_pairs={{0,2},{1,3},{2,0},{3,1},{4,6},{5,7},{6,4},{7,5},{8,10},{9,11},{10,... | collective-permute-start | bytes 208904 | tf_op jit(solution)/shard_map/ppermute | solution.py:326
  14.5 7.7 %collective-permute-start.2 = (bf16[272,128]{1,0:T(8,128)(2,1)}, bf16[272,128]{1,0:T(8,128)(2,1)S(1)}, u32[]{:S(2)}, u32[]{:S(2)}) collective-permute-start(bf16[272,128]{1,0:T(8,128)(2,1)} %get-tuple-element.20), channel_id=1, source_target_pairs={{0,4},{1,5},{2,6},{3,7},{4,0},{5,1},{6,2},{7,3},{8,12},{9,13},{10,... | collective-permute-start | bytes 208904 | tf_op jit(solution)/shard_map/ppermute | solution.py:326
  17.0 6.4 %collective-permute-start.3 = (bf16[272,128]{1,0:T(8,128)(2,1)}, bf16[272,128]{1,0:T(8,128)(2,1)S(1)}, u32[]{:S(2)}, u32[]{:S(2)}) collective-permute-start(bf16[272,128]{1,0:T(8,128)(2,1)} %get-tuple-element.21), channel_id=1, source_target_pairs={{0,6},{1,7},{2,4},{3,5},{4,2},{5,3},{6,0},{7,1},{8,14},{9,15},{10,... | collective-permute-start | bytes 208904 | tf_op jit(solution)/shard_map/ppermute | solution.py:326
  18.0 5.5 %collective-permute-start.4 = (bf16[544,128]{1,0:T(8,128)(2,1)S(1)}, bf16[544,128]{1,0:T(8,128)(2,1)S(1)}, u32[]{:S(2)}, u32[]{:S(2)}) collective-permute-start(bf16[544,128]{1,0:T(8,128)(2,1)S(1)} %constant_dynamic-update-slice_fusion.refs_0_), channel_id=1, source_target_pairs={{0,1},{1,0},{2,3},{3,2},{4,5},{5,4},{6,7},{7,6},{8,9},{9,8},{10,11... | collective-permute-start | bytes 417800 | tf_op jit(solution)/shard_map/ppermute | solution.py:326
  18.0 8.5 %collective-permute-start.5 = (bf16[544,128]{1,0:T(8,128)(2,1)S(1)}, bf16[544,128]{1,0:T(8,128)(2,1)S(1)}, u32[]{:S(2)}, u32[]{:S(2)}) collective-permute-start(bf16[544,128]{1,0:T(8,128)(2,1)S(1)} %constant_dynamic-update-slice_fusion.refs_0_), channel_id=1, source_target_pairs={{0,8},{8,0},{16,24},{24,16},{1,9},{9,1},{17,25},{25,17},{2,10},{10... | collective-permute-start | bytes 417800 | tf_op jit(solution)/shard_map/ppermute | solution.py:326
  19.8 6.8 %collective-permute-start.1 = (bf16[544,128]{1,0:T(8,128)(2,1)S(1)}, bf16[544,128]{1,0:T(8,128)(2,1)S(1)}, u32[]{:S(2)}, u32[]{:S(2)}) collective-permute-start(bf16[544,128]{1,0:T(8,128)(2,1)S(1)} %constant_dynamic-update-slice_fusion.refs_0_), channel_id=1, source_target_pairs={{0,16},{8,24},{16,0},{24,8},{1,17},{9,25},{17,1},{25,9},{2,18},{10... | collective-permute-start | bytes 417800 | tf_op jit(solution)/shard_map/ppermute | solution.py:326
  23.5 5.1 %collective-permute-start.7 = (bf16[544,128]{1,0:T(8,128)(2,1)S(1)}, bf16[544,128]{1,0:T(8,128)(2,1)S(1)}, u32[]{:S(2)}, u32[]{:S(2)}) collective-permute-start(bf16[544,128]{1,0:T(8,128)(2,1)S(1)} %pad_maximum_fusion.refs_5_), channel_id=1, source_target_pairs={{0,16},{8,24},{16,0},{24,8},{1,17},{9,25},{17,1},{25,9},{2,18},{10... | collective-permute-start | bytes 417800 | tf_op jit(solution)/shard_map/ppermute | solution.py:326
  25.1 5.1 %collective-permute-start.10 = (bf16[544,128]{1,0:T(8,128)(2,1)S(1)}, bf16[544,128]{1,0:T(8,128)(2,1)S(1)}, u32[]{:S(2)}, u32[]{:S(2)}) collective-permute-start(bf16[544,128]{1,0:T(8,128)(2,1)S(1)} %pad_maximum_fusion.refs_5_), channel_id=1, source_target_pairs={{0,8},{8,0},{16,24},{24,16},{1,9},{9,1},{17,25},{25,17},{2,10},{10... | collective-permute-start | bytes 417800 | tf_op jit(solution)/shard_map/ppermute | solution.py:326
  26.6 3.6 %collective-permute-start.8 = (bf16[544,128]{1,0:T(8,128)(2,1)S(1)}, bf16[544,128]{1,0:T(8,128)(2,1)S(1)}, u32[]{:S(2)}, u32[]{:S(2)}) collective-permute-start(bf16[544,128]{1,0:T(8,128)(2,1)S(1)} %pad_maximum_fusion.refs_5_), channel_id=1, source_target_pairs={{0,1},{1,0},{2,3},{3,2},{4,5},{5,4},{6,7},{7,6},{8,9},{9,8},{10,11... | collective-permute-start | bytes 417800 | tf_op jit(solution)/shard_map/ppermute | solution.py:326
  26.6 3.6 %collective-permute-start.6 = (bf16[544,128]{1,0:T(8,128)(2,1)S(1)}, bf16[544,128]{1,0:T(8,128)(2,1)S(1)}, u32[]{:S(2)}, u32[]{:S(2)}) collective-permute-start(bf16[544,128]{1,0:T(8,128)(2,1)S(1)} %collective-permute-done.1.refs_1_), channel_id=1, source_target_pairs={{0,1},{1,0},{2,3},{3,2},{4,5},{5,4},{6,7},{7,6},{8,9},{9,8},{10,11... | collective-permute-start | bytes 417800 | tf_op jit(solution)/shard_map/ppermute | solution.py:326
  28.6 1.5 %collective-permute-start.9 = (bf16[544,128]{1,0:T(8,128)(2,1)S(1)}, bf16[544,128]{1,0:T(8,128)(2,1)S(1)}, u32[]{:S(2)}, u32[]{:S(2)}) collective-permute-start(bf16[544,128]{1,0:T(8,128)(2,1)S(1)} %collective-permute-done.7.refs_6_), channel_id=1, source_target_pairs={{0,1},{1,0},{2,3},{3,2},{4,5},{5,4},{6,7},{7,6},{8,9},{9,8},{10,11... | collective-permute-start | bytes 417800 | tf_op jit(solution)/shard_map/ppermute | solution.py:326
  30.9 6.9 %collective-permute-start.11 = (bf16[64,512]{1,0:T(8,128)(2,1)S(1)}, bf16[64,512]{1,0:T(8,128)(2,1)S(1)}, u32[]{:S(2)}, u32[]{:S(2)}) collective-permute-start(bf16[64,512]{1,0:T(8,128)(2,1)S(1)} %get-tuple-element.26), channel_id=1, source_target_pairs={{0,6},{1,7},{2,4},{3,5},{4,2},{5,3},{6,0},{7,1},{8,14},{9,15},{10,... | collective-permute-start | bytes 196616 | tf_op jit(solution)/shard_map/ppermute | solution.py:326
  34.3 5.6 %collective-permute-start.12 = (bf16[64,512]{1,0:T(8,128)(2,1)S(1)}, bf16[64,512]{1,0:T(8,128)(2,1)S(1)}, u32[]{:S(2)}, u32[]{:S(2)}) collective-permute-start(bf16[64,512]{1,0:T(8,128)(2,1)S(1)} %get-tuple-element.27), channel_id=1, source_target_pairs={{0,4},{1,5},{2,6},{3,7},{4,0},{5,1},{6,2},{7,3},{8,12},{9,13},{10,... | collective-permute-start | bytes 196616 | tf_op jit(solution)/shard_map/ppermute | solution.py:326
  34.3 5.7 %collective-permute-start.13 = (bf16[64,512]{1,0:T(8,128)(2,1)S(1)}, bf16[64,512]{1,0:T(8,128)(2,1)S(1)}, u32[]{:S(2)}, u32[]{:S(2)}) collective-permute-start(bf16[64,512]{1,0:T(8,128)(2,1)S(1)} %get-tuple-element.28), channel_id=1, source_target_pairs={{0,2},{1,3},{2,0},{3,1},{4,6},{5,7},{6,4},{7,5},{8,10},{9,11},{10,... | collective-permute-start | bytes 196616 | tf_op jit(solution)/shard_map/ppermute | solution.py:326
  40.1 4.0 %collective-permute-start.14 = (bf16[32,512]{1,0:T(8,128)(2,1)S(1)}, bf16[32,512]{1,0:T(8,128)(2,1)S(1)}, u32[]{:S(2)}, u32[]{:S(2)}) collective-permute-start(bf16[32,512]{1,0:T(8,128)(2,1)S(1)} %get-tuple-element.30), channel_id=1, source_target_pairs={{0,8},{8,0},{16,24},{24,16},{1,9},{9,1},{17,25},{25,17},{2,10},{10... | collective-permute-start | bytes 98312 | tf_op jit(solution)/shard_map/ppermute | solution.py:326

commit v5 on v4

--- a/solution.py
+++ b/solution.py
@@ -152,7 +152,7 @@
     return pl.pallas_call(
         functools.partial(feature_kernel, tokens, slices),
         out_shape=[
-            jax.ShapeDtypeStruct((half // slices * examples + id_rows, 2 * rank), jnp.bfloat16)
+            pltpu.VMEM((half // slices * examples + id_rows, 2 * rank), jnp.bfloat16)
         ] * slices,
         in_specs=[hbm] * 8,
         out_specs=[vmem] * slices,

time: 44.9 us -> 44 us (0.980)
  local copies, waits for them, and re-layouts: 0.9 us -> 0.02 us
  Pallas kernels: 12.8 us -> 12.1 us
  waiting for transfers between devices: 12.8 us -> 13.4 us
    unnamed x1, local copies, waits for them, and re-layouts: 0.89 us -> 0.01 us
    pallas_call x1, Pallas kernels: 11.4 us -> 10.7 us  [features(): pl.pallas_call(functools.partial(feature_kernel, tokens, slices), out_sha...]
    ppermute x15, waiting for transfers between devices: 12.8 us -> 13.4 us  [swap(): lax.ppermute(value, axis, [(place, place ^ distance) for place in range(s...]
  transfers between devices with their start and end apart: 15 -> 15, of which waited for: 8 -> 8; matrix products, arithmetic and copies ran while one was open for 2% -> 0% of each run, Pallas kernels for 0% -> 0%
where the time goes in v5:
time: 44 us; the launch traced here: 43.8 us
  starting transfers between devices  18.2 us (41%)
  waiting for transfers between devices  13.4 us (30%)
  Pallas kernels  12.1 us (28%)
    ppermute x15, starting transfers between devices, swap(): lax.ppermute(value, axis, [(place, place ^ distance) for place in range(s...  18.2 us
    ppermute x15, waiting for transfers between devices, swap(): lax.ppermute(value, axis, [(place, place ^ distance) for place in range(s...  13.4 us
    pallas_call x1, Pallas kernels, features(): pl.pallas_call(functools.partial(feature_kernel, tokens, slices), out_sha...  10.7 us
  transfers between devices with their start and end apart: 15, of which 8 were waited for; matrix products, arithmetic and copies ran while one was open for 0% of the time, Pallas kernels for 0%

profile of v5, /device:TPU:0, one launch (start us, length us, event | category | flops | bytes accessed | tf_op | source)
XLA Modules:
  0.0 43.8 jit_solution(8131323602657186634)
XLA Ops:
  0.0 10.7 %features.1 = (bf16[272,128]{1,0:T(8,128)(2,1)S(1)}, bf16[272,128]{1,0:T(8,128)(2,1)S(1)}, bf16[272,128]{1,0:T(8,128)(2,1)S(1)}, bf16[272,128]{1,0:T(8,128)(2,1)S(1)}) custom-call(bf16[1024,4096]{1,0:T(8,128)(2,1)} %bitcast.5, bf16[1024,4096]{1,0:T(8,128)(2,1)} %bitcast.6, bf16[64,4096]{1,0:T(8,128)(2,1)} %bitcast.7, bf16[64,4096]{1,0:T(8,128)(2,1)} %bitcast.8, ...), custom_call_target="tpu_custom_call" | custom-call | flops 1073741824 | bytes 16777216 | tf_op jit(solution)/shard_map/features/pallas_call | solution.py:152
  10.7 3.1 %collective-permute-start = (bf16[272,128]{1,0:T(8,128)(2,1)S(1)}, bf16[272,128]{1,0:T(8,128)(2,1)S(1)}, u32[]{:S(2)}, u32[]{:S(2)}) collective-permute-start(bf16[272,128]{1,0:T(8,128)(2,1)S(1)} %get-tuple-element.19), channel_id=1, source_target_pairs={{0,2},{1,3},{2,0},{3,1},{4,6},{5,7},{6,4},{7,5},{8,10},{9,11},{10,... | collective-permute-start | bytes 208904 | tf_op jit(solution)/shard_map/ppermute | solution.py:326
  13.8 2.6 %collective-permute-start.2 = (bf16[272,128]{1,0:T(8,128)(2,1)S(1)}, bf16[272,128]{1,0:T(8,128)(2,1)S(1)}, u32[]{:S(2)}, u32[]{:S(2)}) collective-permute-start(bf16[272,128]{1,0:T(8,128)(2,1)S(1)} %get-tuple-element.20), channel_id=1, source_target_pairs={{0,4},{1,5},{2,6},{3,7},{4,0},{5,1},{6,2},{7,3},{8,12},{9,13},{10,... | collective-permute-start | bytes 208904 | tf_op jit(solution)/shard_map/ppermute | solution.py:326
  16.4 0.1 collective-permute-start.4
  16.5 1.8 %collective-permute-start.5 = (bf16[544,128]{1,0:T(8,128)(2,1)S(1)}, bf16[544,128]{1,0:T(8,128)(2,1)S(1)}, u32[]{:S(2)}, u32[]{:S(2)}) collective-permute-start(bf16[544,128]{1,0:T(8,128)(2,1)S(1)} %constant_dynamic-update-slice_fusion.refs_0_), channel_id=1, source_target_pairs={{0,8},{8,0},{16,24},{24,16},{1,9},{9,1},{17,25},{25,17},{2,10},{10... | collective-permute-start | bytes 417800 | tf_op jit(solution)/shard_map/ppermute | solution.py:326
  18.3 1.5 %collective-permute-start.1 = (bf16[544,128]{1,0:T(8,128)(2,1)S(1)}, bf16[544,128]{1,0:T(8,128)(2,1)S(1)}, u32[]{:S(2)}, u32[]{:S(2)}) collective-permute-start(bf16[544,128]{1,0:T(8,128)(2,1)S(1)} %constant_dynamic-update-slice_fusion.refs_0_), channel_id=1, source_target_pairs={{0,16},{8,24},{16,0},{24,8},{1,17},{9,25},{17,1},{25,9},{2,18},{10... | collective-permute-start | bytes 417800 | tf_op jit(solution)/shard_map/ppermute | solution.py:326
  19.8 1.5 %collective-permute-done.2 = bf16[272,128]{1,0:T(8,128)(2,1)S(1)} collective-permute-done((bf16[272,128]{1,0:T(8,128)(2,1)S(1)}, bf16[272,128]{1,0:T(8,128)(2,1)S(1)}, u32[]{:S(2)}, u32[]{:S(2)}) %collective-permute-start.2) | collective-permute-done | bytes 69664 | tf_op jit(solution)/shard_map/ppermute | solution.py:326
  21.3 1.3 %collective-permute-done.3 = bf16[272,128]{1,0:T(8,128)(2,1)S(1)} collective-permute-done((bf16[272,128]{1,0:T(8,128)(2,1)S(1)}, bf16[272,128]{1,0:T(8,128)(2,1)S(1)}, u32[]{:S(2)}, u32[]{:S(2)}) %collective-permute-start.3) | collective-permute-done | bytes 69664 | tf_op jit(solution)/shard_map/ppermute | solution.py:326
  22.6 0.0 collective-permute-done.4.refs_2_
  22.6 1.6 %collective-permute-start.7 = (bf16[544,128]{1,0:T(8,128)(2,1)S(1)}, bf16[544,128]{1,0:T(8,128)(2,1)S(1)}, u32[]{:S(2)}, u32[]{:S(2)}) collective-permute-start(bf16[544,128]{1,0:T(8,128)(2,1)S(1)} %pad_maximum_fusion.refs_5_), channel_id=1, source_target_pairs={{0,16},{8,24},{16,0},{24,8},{1,17},{9,25},{17,1},{25,9},{2,18},{10... | collective-permute-start | bytes 417800 | tf_op jit(solution)/shard_map/ppermute | solution.py:326
  24.2 1.5 %collective-permute-start.10 = (bf16[544,128]{1,0:T(8,128)(2,1)S(1)}, bf16[544,128]{1,0:T(8,128)(2,1)S(1)}, u32[]{:S(2)}, u32[]{:S(2)}) collective-permute-start(bf16[544,128]{1,0:T(8,128)(2,1)S(1)} %pad_maximum_fusion.refs_5_), channel_id=1, source_target_pairs={{0,8},{8,0},{16,24},{24,16},{1,9},{9,1},{17,25},{25,17},{2,10},{10... | collective-permute-start | bytes 417800 | tf_op jit(solution)/shard_map/ppermute | solution.py:326
  25.7 0.5 %collective-permute-start.6 = (bf16[544,128]{1,0:T(8,128)(2,1)S(1)}, bf16[544,128]{1,0:T(8,128)(2,1)S(1)}, u32[]{:S(2)}, u32[]{:S(2)}) collective-permute-start(bf16[544,128]{1,0:T(8,128)(2,1)S(1)} %collective-permute-done.1.refs_1_), channel_id=1, source_target_pairs={{0,1},{1,0},{2,3},{3,2},{4,5},{5,4},{6,7},{7,6},{8,9},{9,8},{10,11... | collective-permute-start | bytes 417800 | tf_op jit(solution)/shard_map/ppermute | solution.py:326
  26.2 1.5 %collective-permute-done.7.refs_6_ = bf16[544,128]{1,0:T(8,128)(2,1)S(1)} collective-permute-done((bf16[544,128]{1,0:T(8,128)(2,1)S(1)}, bf16[544,128]{1,0:T(8,128)(2,1)S(1)}, u32[]{:S(2)}, u32[]{:S(2)}) %collective-permute-start.7) | collective-permute-done | bytes 139296 | tf_op jit(solution)/shard_map/ppermute | solution.py:326
  27.7 1.5 %collective-permute-done.10.refs_9_ = bf16[544,128]{1,0:T(8,128)(2,1)S(1)} collective-permute-done((bf16[544,128]{1,0:T(8,128)(2,1)S(1)}, bf16[544,128]{1,0:T(8,128)(2,1)S(1)}, u32[]{:S(2)}, u32[]{:S(2)}) %collective-permute-start.10) | collective-permute-done | bytes 139296 | tf_op jit(solution)/shard_map/ppermute | solution.py:326
  29.3 0.0 collective-permute-done.8.refs_7_
  29.3 0.7 %products.1 = (bf16[64,512]{1,0:T(8,128)(2,1)S(1)}, bf16[64,512]{1,0:T(8,128)(2,1)S(1)}, bf16[64,512]{1,0:T(8,128)(2,1)S(1)}, bf16[64,512]{1,0:T(8,128)(2,1)S(1)}) custom-call(bf16[544,128]{1,0:T(8,128)(2,1)S(1)} %constant_dynamic-update-slice_fusion.refs_0_, bf16[544,128]{1,0:T(8,128)(2,1)S(1)} %collective-permute-done.1.refs_1_, ...), custom_call_target="tpu_custom_call" | custom-call | flops 268435456 | bytes 524288 | tf_op jit(solution)/shard_map/products/pallas_call | solution.py:251
  30.0 3.3 %collective-permute-start.11 = (bf16[64,512]{1,0:T(8,128)(2,1)S(1)}, bf16[64,512]{1,0:T(8,128)(2,1)S(1)}, u32[]{:S(2)}, u32[]{:S(2)}) collective-permute-start(bf16[64,512]{1,0:T(8,128)(2,1)S(1)} %get-tuple-element.26), channel_id=1, source_target_pairs={{0,6},{1,7},{2,4},{3,5},{4,2},{5,3},{6,0},{7,1},{8,14},{9,15},{10,... | collective-permute-start | bytes 196616 | tf_op jit(solution)/shard_map/ppermute | solution.py:326
  33.3 1.1 %collective-permute-start.13 = (bf16[64,512]{1,0:T(8,128)(2,1)S(1)}, bf16[64,512]{1,0:T(8,128)(2,1)S(1)}, u32[]{:S(2)}, u32[]{:S(2)}) collective-permute-start(bf16[64,512]{1,0:T(8,128)(2,1)S(1)} %get-tuple-element.28), channel_id=1, source_target_pairs={{0,2},{1,3},{2,0},{3,1},{4,6},{5,7},{6,4},{7,5},{8,10},{9,11},{10,... | collective-permute-start | bytes 196616 | tf_op jit(solution)/shard_map/ppermute | solution.py:326
  34.5 2.4 %collective-permute-done.11.refs_1_ = bf16[64,512]{1,0:T(8,128)(2,1)S(1)} collective-permute-done((bf16[64,512]{1,0:T(8,128)(2,1)S(1)}, bf16[64,512]{1,0:T(8,128)(2,1)S(1)}, u32[]{:S(2)}, u32[]{:S(2)}) %collective-permute-start.11) | collective-permute-done | bytes 65568 | tf_op jit(solution)/shard_map/ppermute | solution.py:326
  36.9 2.1 %collective-permute-done.12.refs_2_ = bf16[64,512]{1,0:T(8,128)(2,1)S(1)} collective-permute-done((bf16[64,512]{1,0:T(8,128)(2,1)S(1)}, bf16[64,512]{1,0:T(8,128)(2,1)S(1)}, u32[]{:S(2)}, u32[]{:S(2)}) %collective-permute-start.12) | collective-permute-done | bytes 65568 | tf_op jit(solution)/shard_map/ppermute | solution.py:326
  39.0 0.1 collective-permute-done.13.refs_3_
  39.2 1.1 %collective-permute-start.14 = (bf16[32,512]{1,0:T(8,128)(2,1)S(1)}, bf16[32,512]{1,0:T(8,128)(2,1)S(1)}, u32[]{:S(2)}, u32[]{:S(2)}) collective-permute-start(bf16[32,512]{1,0:T(8,128)(2,1)S(1)} %get-tuple-element.30), channel_id=1, source_target_pairs={{0,8},{8,0},{16,24},{24,16},{1,9},{9,1},{17,25},{25,17},{2,10},{10... | collective-permute-start | bytes 98312 | tf_op jit(solution)/shard_map/ppermute | solution.py:326
  40.3 2.8 %collective-permute-done.14.refs_1_ = bf16[32,512]{1,0:T(8,128)(2,1)S(1)} collective-permute-done((bf16[32,512]{1,0:T(8,128)(2,1)S(1)}, bf16[32,512]{1,0:T(8,128)(2,1)S(1)}, u32[]{:S(2)}, u32[]{:S(2)}) %collective-permute-start.14) | collective-permute-done | bytes 32800 | tf_op jit(solution)/shard_map/ppermute | solution.py:326
  43.1 0.7 %finish.1 = f32[32,1024]{1,0:T(8,128)} custom-call(f32[32,512]{1,0:T(8,128)S(1)} %get-tuple-element.29.refs_0_, bf16[32,512]{1,0:T(8,128)(2,1)S(1)} %collective-permute-done.14.refs_1_), custom_call_target="tpu_custom_call" | custom-call | flops 131072 | bytes 262144 | tf_op jit(solution)/shard_map/finish/pallas_call | solution.py:311
  (13 shorter events, 0.1 us)
Async XLA Ops:
  10.7 5.7 %collective-permute-start = (bf16[272,128]{1,0:T(8,128)(2,1)S(1)}, bf16[272,128]{1,0:T(8,128)(2,1)S(1)}, u32[]{:S(2)}, u32[]{:S(2)}) collective-permute-start(bf16[272,128]{1,0:T(8,128)(2,1)S(1)} %get-tuple-element.19), channel_id=1, source_target_pairs={{0,2},{1,3},{2,0},{3,1},{4,6},{5,7},{6,4},{7,5},{8,10},{9,11},{10,... | collective-permute-start | bytes 208904 | tf_op jit(solution)/shard_map/ppermute | solution.py:326
  13.8 7.5 %collective-permute-start.2 = (bf16[272,128]{1,0:T(8,128)(2,1)S(1)}, bf16[272,128]{1,0:T(8,128)(2,1)S(1)}, u32[]{:S(2)}, u32[]{:S(2)}) collective-permute-start(bf16[272,128]{1,0:T(8,128)(2,1)S(1)} %get-tuple-element.20), channel_id=1, source_target_pairs={{0,4},{1,5},{2,6},{3,7},{4,0},{5,1},{6,2},{7,3},{8,12},{9,13},{10,... | collective-permute-start | bytes 208904 | tf_op jit(solution)/shard_map/ppermute | solution.py:326
  16.4 6.2 %collective-permute-start.3 = (bf16[272,128]{1,0:T(8,128)(2,1)S(1)}, bf16[272,128]{1,0:T(8,128)(2,1)S(1)}, u32[]{:S(2)}, u32[]{:S(2)}) collective-permute-start(bf16[272,128]{1,0:T(8,128)(2,1)S(1)} %get-tuple-element.21), channel_id=1, source_target_pairs={{0,6},{1,7},{2,4},{3,5},{4,2},{5,3},{6,0},{7,1},{8,14},{9,15},{10,... | collective-permute-start | bytes 208904 | tf_op jit(solution)/shard_map/ppermute | solution.py:326
  16.4 6.2 %collective-permute-start.4 = (bf16[544,128]{1,0:T(8,128)(2,1)S(1)}, bf16[544,128]{1,0:T(8,128)(2,1)S(1)}, u32[]{:S(2)}, u32[]{:S(2)}) collective-permute-start(bf16[544,128]{1,0:T(8,128)(2,1)S(1)} %constant_dynamic-update-slice_fusion.refs_0_), channel_id=1, source_target_pairs={{0,1},{1,0},{2,3},{3,2},{4,5},{5,4},{6,7},{7,6},{8,9},{9,8},{10,11... | collective-permute-start | bytes 417800 | tf_op jit(solution)/shard_map/ppermute | solution.py:326
  16.5 9.2 %collective-permute-start.5 = (bf16[544,128]{1,0:T(8,128)(2,1)S(1)}, bf16[544,128]{1,0:T(8,128)(2,1)S(1)}, u32[]{:S(2)}, u32[]{:S(2)}) collective-permute-start(bf16[544,128]{1,0:T(8,128)(2,1)S(1)} %constant_dynamic-update-slice_fusion.refs_0_), channel_id=1, source_target_pairs={{0,8},{8,0},{16,24},{24,16},{1,9},{9,1},{17,25},{25,17},{2,10},{10... | collective-permute-start | bytes 417800 | tf_op jit(solution)/shard_map/ppermute | solution.py:326
  18.3 7.4 %collective-permute-start.1 = (bf16[544,128]{1,0:T(8,128)(2,1)S(1)}, bf16[544,128]{1,0:T(8,128)(2,1)S(1)}, u32[]{:S(2)}, u32[]{:S(2)}) collective-permute-start(bf16[544,128]{1,0:T(8,128)(2,1)S(1)} %constant_dynamic-update-slice_fusion.refs_0_), channel_id=1, source_target_pairs={{0,16},{8,24},{16,0},{24,8},{1,17},{9,25},{17,1},{25,9},{2,18},{10... | collective-permute-start | bytes 417800 | tf_op jit(solution)/shard_map/ppermute | solution.py:326
  22.6 5.1 %collective-permute-start.7 = (bf16[544,128]{1,0:T(8,128)(2,1)S(1)}, bf16[544,128]{1,0:T(8,128)(2,1)S(1)}, u32[]{:S(2)}, u32[]{:S(2)}) collective-permute-start(bf16[544,128]{1,0:T(8,128)(2,1)S(1)} %pad_maximum_fusion.refs_5_), channel_id=1, source_target_pairs={{0,16},{8,24},{16,0},{24,8},{1,17},{9,25},{17,1},{25,9},{2,18},{10... | collective-permute-start | bytes 417800 | tf_op jit(solution)/shard_map/ppermute | solution.py:326
  24.2 5.1 %collective-permute-start.10 = (bf16[544,128]{1,0:T(8,128)(2,1)S(1)}, bf16[544,128]{1,0:T(8,128)(2,1)S(1)}, u32[]{:S(2)}, u32[]{:S(2)}) collective-permute-start(bf16[544,128]{1,0:T(8,128)(2,1)S(1)} %pad_maximum_fusion.refs_5_), channel_id=1, source_target_pairs={{0,8},{8,0},{16,24},{24,16},{1,9},{9,1},{17,25},{25,17},{2,10},{10... | collective-permute-start | bytes 417800 | tf_op jit(solution)/shard_map/ppermute | solution.py:326
  25.7 3.6 %collective-permute-start.8 = (bf16[544,128]{1,0:T(8,128)(2,1)S(1)}, bf16[544,128]{1,0:T(8,128)(2,1)S(1)}, u32[]{:S(2)}, u32[]{:S(2)}) collective-permute-start(bf16[544,128]{1,0:T(8,128)(2,1)S(1)} %pad_maximum_fusion.refs_5_), channel_id=1, source_target_pairs={{0,1},{1,0},{2,3},{3,2},{4,5},{5,4},{6,7},{7,6},{8,9},{9,8},{10,11... | collective-permute-start | bytes 417800 | tf_op jit(solution)/shard_map/ppermute | solution.py:326
  25.7 3.6 %collective-permute-start.6 = (bf16[544,128]{1,0:T(8,128)(2,1)S(1)}, bf16[544,128]{1,0:T(8,128)(2,1)S(1)}, u32[]{:S(2)}, u32[]{:S(2)}) collective-permute-start(bf16[544,128]{1,0:T(8,128)(2,1)S(1)} %collective-permute-done.1.refs_1_), channel_id=1, source_target_pairs={{0,1},{1,0},{2,3},{3,2},{4,5},{5,4},{6,7},{7,6},{8,9},{9,8},{10,11... | collective-permute-start | bytes 417800 | tf_op jit(solution)/shard_map/ppermute | solution.py:326
  27.7 1.5 %collective-permute-start.9 = (bf16[544,128]{1,0:T(8,128)(2,1)S(1)}, bf16[544,128]{1,0:T(8,128)(2,1)S(1)}, u32[]{:S(2)}, u32[]{:S(2)}) collective-permute-start(bf16[544,128]{1,0:T(8,128)(2,1)S(1)} %collective-permute-done.7.refs_6_), channel_id=1, source_target_pairs={{0,1},{1,0},{2,3},{3,2},{4,5},{5,4},{6,7},{7,6},{8,9},{9,8},{10,11... | collective-permute-start | bytes 417800 | tf_op jit(solution)/shard_map/ppermute | solution.py:326
  30.0 6.9 %collective-permute-start.11 = (bf16[64,512]{1,0:T(8,128)(2,1)S(1)}, bf16[64,512]{1,0:T(8,128)(2,1)S(1)}, u32[]{:S(2)}, u32[]{:S(2)}) collective-permute-start(bf16[64,512]{1,0:T(8,128)(2,1)S(1)} %get-tuple-element.26), channel_id=1, source_target_pairs={{0,6},{1,7},{2,4},{3,5},{4,2},{5,3},{6,0},{7,1},{8,14},{9,15},{10,... | collective-permute-start | bytes 196616 | tf_op jit(solution)/shard_map/ppermute | solution.py:326
  33.3 5.6 %collective-permute-start.12 = (bf16[64,512]{1,0:T(8,128)(2,1)S(1)}, bf16[64,512]{1,0:T(8,128)(2,1)S(1)}, u32[]{:S(2)}, u32[]{:S(2)}) collective-permute-start(bf16[64,512]{1,0:T(8,128)(2,1)S(1)} %get-tuple-element.27), channel_id=1, source_target_pairs={{0,4},{1,5},{2,6},{3,7},{4,0},{5,1},{6,2},{7,3},{8,12},{9,13},{10,... | collective-permute-start | bytes 196616 | tf_op jit(solution)/shard_map/ppermute | solution.py:326
  33.3 5.8 %collective-permute-start.13 = (bf16[64,512]{1,0:T(8,128)(2,1)S(1)}, bf16[64,512]{1,0:T(8,128)(2,1)S(1)}, u32[]{:S(2)}, u32[]{:S(2)}) collective-permute-start(bf16[64,512]{1,0:T(8,128)(2,1)S(1)} %get-tuple-element.28), channel_id=1, source_target_pairs={{0,2},{1,3},{2,0},{3,1},{4,6},{5,7},{6,4},{7,5},{8,10},{9,11},{10,... | collective-permute-start | bytes 196616 | tf_op jit(solution)/shard_map/ppermute | solution.py:326
  39.2 4.0 %collective-permute-start.14 = (bf16[32,512]{1,0:T(8,128)(2,1)S(1)}, bf16[32,512]{1,0:T(8,128)(2,1)S(1)}, u32[]{:S(2)}, u32[]{:S(2)}) collective-permute-start(bf16[32,512]{1,0:T(8,128)(2,1)S(1)} %get-tuple-element.30), channel_id=1, source_target_pairs={{0,8},{8,0},{16,24},{24,16},{1,9},{9,1},{17,25},{25,17},{2,10},{10... | collective-permute-start | bytes 98312 | tf_op jit(solution)/shard_map/ppermute | solution.py:326

commit v6 on v5

--- a/solution.py
+++ b/solution.py
@@ -62,8 +62,8 @@
         for index, (source, target) in enumerate((
             (bin_hbm, bin_ref), (bout_hbm, bout_ref), (eigen_hbm, eigen_ref), (ids_hbm, ids_ref)))
     ]
-    for copy in weights:
-        copy.start()
+    for priority, copy in enumerate(weights):
+        copy.start(priority=priority)
     start_half(0)
     for copy in small:
         copy.start()
@@ -92,7 +92,9 @@
         rng = pl.ds(index * half_rows, half_rows)
         act_copy, grad_copy = half_copies(index)
         act_copy.wait()
-        act_proj[rng] = dot_nt(pin[...], act[rng]).T.astype(jnp.bfloat16)
+        act_part = dot_nt(pin[...], act[rng]).T.astype(jnp.bfloat16)
+        act_hi, act_lo = split_two(dot_nn(act_part, bin_hi) + dot_nn(act_part, bin_lo))
+        act_proj[rng] = jnp.concatenate([act_hi, act_lo], axis=1)
         for step in beside[0::2]:
             rotate(step)
         grad_copy.wait()
@@ -103,7 +105,6 @@
     def rotate(step):
         rng = pl.ds(step * step_rows, step_rows)
         act_part, grad_part = act_proj[rng], grad_proj[:, rng]
-        act_hi, act_lo = split_two(dot_nn(act_part, bin_hi) + dot_nn(act_part, bin_lo))
         grad_hi, grad_lo = split_two(dot_nn(bout_hi, grad_part) + dot_nn(bout_lo, grad_part))
         gt_ref[step, 0] = grad_hi.astype(jnp.float32)
         gt_ref[step, 1] = grad_lo.astype(jnp.float32)
@@ -114,8 +115,8 @@
             ], axis=0).astype(jnp.bfloat16)
             for part in range(2)
         ]
-        wide = dot_nn(spread_hi, jnp.concatenate([act_hi, act_lo], axis=1))
-        rotated = wide[:, :2 * rank] + wide[:, 2 * rank:] + dot_nn(spread_lo, act_hi)
+        wide = dot_nn(spread_hi, act_part)
+        rotated = wide[:, :2 * rank] + wide[:, 2 * rank:] + dot_nn(spread_lo, act_part[:, :2 * rank])
         start = step * batch
         for u in range(half):
             value = jnp.where(
@@ -165,7 +166,7 @@
             pltpu.VMEM((rank, rank), jnp.float32),
             pltpu.VMEM((rank, rank), jnp.float32),
             pltpu.VMEM((1, examples), jnp.int32),
-            pltpu.VMEM((rows, rank), jnp.bfloat16),
+            pltpu.VMEM((rows, 4 * rank), jnp.bfloat16),
             pltpu.VMEM((rank, rows), jnp.bfloat16),
             pltpu.VMEM((examples // batch, 2, rank, batch * tokens), jnp.float32),
             pltpu.VMEM((half, examples, 2 * rank), jnp.float32),

time: 44 us -> 45.6 us (1.036)
  Pallas kernels: 12.1 us -> 13.8 us
    pallas_call x1, Pallas kernels: 10.7 us -> 12.4 us  [features(): pl.pallas_call(functools.partial(feature_kernel, tokens, slices), out_sha...]
where the time goes in v6:
time: 45.6 us; the launch traced here: 45.5 us
  starting transfers between devices  18.2 us (40%)
  Pallas kernels  13.8 us (30%)
  waiting for transfers between devices  13.3 us (29%)
    ppermute x15, starting transfers between devices, swap(): lax.ppermute(value, axis, [(place, place ^ distance) for place in range(s...  18.2 us
    ppermute x15, waiting for transfers between devices, swap(): lax.ppermute(value, axis, [(place, place ^ distance) for place in range(s...  13.3 us
    pallas_call x1, Pallas kernels, features(): pl.pallas_call(functools.partial(feature_kernel, tokens, slices), out_sha...  12.4 us
  transfers between devices with their start and end apart: 15, of which 8 were waited for; matrix products, arithmetic and copies ran while one was open for 0% of the time, Pallas kernels for 0%

profile of v6, /device:TPU:0, one launch (start us, length us, event | category | flops | bytes accessed | tf_op | source)
XLA Modules:
  0.0 45.5 jit_solution(11855665537811534561)
XLA Ops:
  0.0 12.4 %features.1 = (bf16[272,128]{1,0:T(8,128)(2,1)S(1)}, bf16[272,128]{1,0:T(8,128)(2,1)S(1)}, bf16[272,128]{1,0:T(8,128)(2,1)S(1)}, bf16[272,128]{1,0:T(8,128)(2,1)S(1)}) custom-call(bf16[1024,4096]{1,0:T(8,128)(2,1)} %bitcast.5, bf16[1024,4096]{1,0:T(8,128)(2,1)} %bitcast.6, bf16[64,4096]{1,0:T(8,128)(2,1)} %bitcast.7, bf16[64,4096]{1,0:T(8,128)(2,1)} %bitcast.8, ...), custom_call_target="tpu_custom_call" | custom-call | flops 1073741824 | bytes 16777216 | tf_op jit(solution)/shard_map/features/pallas_call | solution.py:153
  12.4 3.1 %collective-permute-start = (bf16[272,128]{1,0:T(8,128)(2,1)S(1)}, bf16[272,128]{1,0:T(8,128)(2,1)S(1)}, u32[]{:S(2)}, u32[]{:S(2)}) collective-permute-start(bf16[272,128]{1,0:T(8,128)(2,1)S(1)} %get-tuple-element.19), channel_id=1, source_target_pairs={{0,2},{1,3},{2,0},{3,1},{4,6},{5,7},{6,4},{7,5},{8,10},{9,11},{10,... | collective-permute-start | bytes 208904 | tf_op jit(solution)/shard_map/ppermute | solution.py:327
  15.5 2.6 %collective-permute-start.2 = (bf16[272,128]{1,0:T(8,128)(2,1)S(1)}, bf16[272,128]{1,0:T(8,128)(2,1)S(1)}, u32[]{:S(2)}, u32[]{:S(2)}) collective-permute-start(bf16[272,128]{1,0:T(8,128)(2,1)S(1)} %get-tuple-element.20), channel_id=1, source_target_pairs={{0,4},{1,5},{2,6},{3,7},{4,0},{5,1},{6,2},{7,3},{8,12},{9,13},{10,... | collective-permute-start | bytes 208904 | tf_op jit(solution)/shard_map/ppermute | solution.py:327
  18.1 0.0 collective-permute-start.3
  18.1 0.0 collective-permute-done
  18.1 0.1 collective-permute-start.4
  18.2 1.8 %collective-permute-start.5 = (bf16[544,128]{1,0:T(8,128)(2,1)S(1)}, bf16[544,128]{1,0:T(8,128)(2,1)S(1)}, u32[]{:S(2)}, u32[]{:S(2)}) collective-permute-start(bf16[544,128]{1,0:T(8,128)(2,1)S(1)} %constant_dynamic-update-slice_fusion.refs_0_), channel_id=1, source_target_pairs={{0,8},{8,0},{16,24},{24,16},{1,9},{9,1},{17,25},{25,17},{2,10},{10... | collective-permute-start | bytes 417800 | tf_op jit(solution)/shard_map/ppermute | solution.py:327
  19.9 1.5 %collective-permute-start.1 = (bf16[544,128]{1,0:T(8,128)(2,1)S(1)}, bf16[544,128]{1,0:T(8,128)(2,1)S(1)}, u32[]{:S(2)}, u32[]{:S(2)}) collective-permute-start(bf16[544,128]{1,0:T(8,128)(2,1)S(1)} %constant_dynamic-update-slice_fusion.refs_0_), channel_id=1, source_target_pairs={{0,16},{8,24},{16,0},{24,8},{1,17},{9,25},{17,1},{25,9},{2,18},{10... | collective-permute-start | bytes 417800 | tf_op jit(solution)/shard_map/ppermute | solution.py:327
  21.5 1.5 %collective-permute-done.2 = bf16[272,128]{1,0:T(8,128)(2,1)S(1)} collective-permute-done((bf16[272,128]{1,0:T(8,128)(2,1)S(1)}, bf16[272,128]{1,0:T(8,128)(2,1)S(1)}, u32[]{:S(2)}, u32[]{:S(2)}) %collective-permute-start.2) | collective-permute-done | bytes 69664 | tf_op jit(solution)/shard_map/ppermute | solution.py:327
  23.0 1.3 %collective-permute-done.3 = bf16[272,128]{1,0:T(8,128)(2,1)S(1)} collective-permute-done((bf16[272,128]{1,0:T(8,128)(2,1)S(1)}, bf16[272,128]{1,0:T(8,128)(2,1)S(1)}, u32[]{:S(2)}, u32[]{:S(2)}) %collective-permute-start.3) | collective-permute-done | bytes 69664 | tf_op jit(solution)/shard_map/ppermute | solution.py:327
  24.3 1.6 %collective-permute-start.7 = (bf16[544,128]{1,0:T(8,128)(2,1)S(1)}, bf16[544,128]{1,0:T(8,128)(2,1)S(1)}, u32[]{:S(2)}, u32[]{:S(2)}) collective-permute-start(bf16[544,128]{1,0:T(8,128)(2,1)S(1)} %pad_maximum_fusion.refs_5_), channel_id=1, source_target_pairs={{0,16},{8,24},{16,0},{24,8},{1,17},{9,25},{17,1},{25,9},{2,18},{10... | collective-permute-start | bytes 417800 | tf_op jit(solution)/shard_map/ppermute | solution.py:327
  25.9 1.5 %collective-permute-start.10 = (bf16[544,128]{1,0:T(8,128)(2,1)S(1)}, bf16[544,128]{1,0:T(8,128)(2,1)S(1)}, u32[]{:S(2)}, u32[]{:S(2)}) collective-permute-start(bf16[544,128]{1,0:T(8,128)(2,1)S(1)} %pad_maximum_fusion.refs_5_), channel_id=1, source_target_pairs={{0,8},{8,0},{16,24},{24,16},{1,9},{9,1},{17,25},{25,17},{2,10},{10... | collective-permute-start | bytes 417800 | tf_op jit(solution)/shard_map/ppermute | solution.py:327
  27.4 0.5 %collective-permute-start.6 = (bf16[544,128]{1,0:T(8,128)(2,1)S(1)}, bf16[544,128]{1,0:T(8,128)(2,1)S(1)}, u32[]{:S(2)}, u32[]{:S(2)}) collective-permute-start(bf16[544,128]{1,0:T(8,128)(2,1)S(1)} %collective-permute-done.1.refs_1_), channel_id=1, source_target_pairs={{0,1},{1,0},{2,3},{3,2},{4,5},{5,4},{6,7},{7,6},{8,9},{9,8},{10,11... | collective-permute-start | bytes 417800 | tf_op jit(solution)/shard_map/ppermute | solution.py:327
  27.9 1.5 %collective-permute-done.7.refs_6_ = bf16[544,128]{1,0:T(8,128)(2,1)S(1)} collective-permute-done((bf16[544,128]{1,0:T(8,128)(2,1)S(1)}, bf16[544,128]{1,0:T(8,128)(2,1)S(1)}, u32[]{:S(2)}, u32[]{:S(2)}) %collective-permute-start.7) | collective-permute-done | bytes 139296 | tf_op jit(solution)/shard_map/ppermute | solution.py:327
  29.4 1.5 %collective-permute-done.10.refs_9_ = bf16[544,128]{1,0:T(8,128)(2,1)S(1)} collective-permute-done((bf16[544,128]{1,0:T(8,128)(2,1)S(1)}, bf16[544,128]{1,0:T(8,128)(2,1)S(1)}, u32[]{:S(2)}, u32[]{:S(2)}) %collective-permute-start.10) | collective-permute-done | bytes 139296 | tf_op jit(solution)/shard_map/ppermute | solution.py:327
  30.9 0.7 %products.1 = (bf16[64,512]{1,0:T(8,128)(2,1)S(1)}, bf16[64,512]{1,0:T(8,128)(2,1)S(1)}, bf16[64,512]{1,0:T(8,128)(2,1)S(1)}, bf16[64,512]{1,0:T(8,128)(2,1)S(1)}) custom-call(bf16[544,128]{1,0:T(8,128)(2,1)S(1)} %constant_dynamic-update-slice_fusion.refs_0_, bf16[544,128]{1,0:T(8,128)(2,1)S(1)} %collective-permute-done.1.refs_1_, ...), custom_call_target="tpu_custom_call" | custom-call | flops 268435456 | bytes 524288 | tf_op jit(solution)/shard_map/products/pallas_call | solution.py:252
  31.7 3.3 %collective-permute-start.11 = (bf16[64,512]{1,0:T(8,128)(2,1)S(1)}, bf16[64,512]{1,0:T(8,128)(2,1)S(1)}, u32[]{:S(2)}, u32[]{:S(2)}) collective-permute-start(bf16[64,512]{1,0:T(8,128)(2,1)S(1)} %get-tuple-element.26), channel_id=1, source_target_pairs={{0,6},{1,7},{2,4},{3,5},{4,2},{5,3},{6,0},{7,1},{8,14},{9,15},{10,... | collective-permute-start | bytes 196616 | tf_op jit(solution)/shard_map/ppermute | solution.py:327
  35.0 1.1 %collective-permute-start.13 = (bf16[64,512]{1,0:T(8,128)(2,1)S(1)}, bf16[64,512]{1,0:T(8,128)(2,1)S(1)}, u32[]{:S(2)}, u32[]{:S(2)}) collective-permute-start(bf16[64,512]{1,0:T(8,128)(2,1)S(1)} %get-tuple-element.28), channel_id=1, source_target_pairs={{0,2},{1,3},{2,0},{3,1},{4,6},{5,7},{6,4},{7,5},{8,10},{9,11},{10,... | collective-permute-start | bytes 196616 | tf_op jit(solution)/shard_map/ppermute | solution.py:327
  36.1 2.4 %collective-permute-done.11.refs_1_ = bf16[64,512]{1,0:T(8,128)(2,1)S(1)} collective-permute-done((bf16[64,512]{1,0:T(8,128)(2,1)S(1)}, bf16[64,512]{1,0:T(8,128)(2,1)S(1)}, u32[]{:S(2)}, u32[]{:S(2)}) %collective-permute-start.11) | collective-permute-done | bytes 65568 | tf_op jit(solution)/shard_map/ppermute | solution.py:327
  38.5 2.1 %collective-permute-done.12.refs_2_ = bf16[64,512]{1,0:T(8,128)(2,1)S(1)} collective-permute-done((bf16[64,512]{1,0:T(8,128)(2,1)S(1)}, bf16[64,512]{1,0:T(8,128)(2,1)S(1)}, u32[]{:S(2)}, u32[]{:S(2)}) %collective-permute-start.12) | collective-permute-done | bytes 65568 | tf_op jit(solution)/shard_map/ppermute | solution.py:327
  40.7 0.1 collective-permute-done.13.refs_3_
  40.8 1.2 %collective-permute-start.14 = (bf16[32,512]{1,0:T(8,128)(2,1)S(1)}, bf16[32,512]{1,0:T(8,128)(2,1)S(1)}, u32[]{:S(2)}, u32[]{:S(2)}) collective-permute-start(bf16[32,512]{1,0:T(8,128)(2,1)S(1)} %get-tuple-element.30), channel_id=1, source_target_pairs={{0,8},{8,0},{16,24},{24,16},{1,9},{9,1},{17,25},{25,17},{2,10},{10... | collective-permute-start | bytes 98312 | tf_op jit(solution)/shard_map/ppermute | solution.py:327
  42.0 2.8 %collective-permute-done.14.refs_1_ = bf16[32,512]{1,0:T(8,128)(2,1)S(1)} collective-permute-done((bf16[32,512]{1,0:T(8,128)(2,1)S(1)}, bf16[32,512]{1,0:T(8,128)(2,1)S(1)}, u32[]{:S(2)}, u32[]{:S(2)}) %collective-permute-start.14) | collective-permute-done | bytes 32800 | tf_op jit(solution)/shard_map/ppermute | solution.py:327
  44.8 0.7 %finish.1 = f32[32,1024]{1,0:T(8,128)} custom-call(f32[32,512]{1,0:T(8,128)S(1)} %get-tuple-element.29.refs_0_, bf16[32,512]{1,0:T(8,128)(2,1)S(1)} %collective-permute-done.14.refs_1_), custom_call_target="tpu_custom_call" | custom-call | flops 131072 | bytes 262144 | tf_op jit(solution)/shard_map/finish/pallas_call | solution.py:312
  (13 shorter events, 0.1 us)
Async XLA Ops:
  12.4 5.7 %collective-permute-start = (bf16[272,128]{1,0:T(8,128)(2,1)S(1)}, bf16[272,128]{1,0:T(8,128)(2,1)S(1)}, u32[]{:S(2)}, u32[]{:S(2)}) collective-permute-start(bf16[272,128]{1,0:T(8,128)(2,1)S(1)} %get-tuple-element.19), channel_id=1, source_target_pairs={{0,2},{1,3},{2,0},{3,1},{4,6},{5,7},{6,4},{7,5},{8,10},{9,11},{10,... | collective-permute-start | bytes 208904 | tf_op jit(solution)/shard_map/ppermute | solution.py:327
  15.5 7.5 %collective-permute-start.2 = (bf16[272,128]{1,0:T(8,128)(2,1)S(1)}, bf16[272,128]{1,0:T(8,128)(2,1)S(1)}, u32[]{:S(2)}, u32[]{:S(2)}) collective-permute-start(bf16[272,128]{1,0:T(8,128)(2,1)S(1)} %get-tuple-element.20), channel_id=1, source_target_pairs={{0,4},{1,5},{2,6},{3,7},{4,0},{5,1},{6,2},{7,3},{8,12},{9,13},{10,... | collective-permute-start | bytes 208904 | tf_op jit(solution)/shard_map/ppermute | solution.py:327
  18.1 6.2 %collective-permute-start.3 = (bf16[272,128]{1,0:T(8,128)(2,1)S(1)}, bf16[272,128]{1,0:T(8,128)(2,1)S(1)}, u32[]{:S(2)}, u32[]{:S(2)}) collective-permute-start(bf16[272,128]{1,0:T(8,128)(2,1)S(1)} %get-tuple-element.21), channel_id=1, source_target_pairs={{0,6},{1,7},{2,4},{3,5},{4,2},{5,3},{6,0},{7,1},{8,14},{9,15},{10,... | collective-permute-start | bytes 208904 | tf_op jit(solution)/shard_map/ppermute | solution.py:327
  18.1 6.2 %collective-permute-start.4 = (bf16[544,128]{1,0:T(8,128)(2,1)S(1)}, bf16[544,128]{1,0:T(8,128)(2,1)S(1)}, u32[]{:S(2)}, u32[]{:S(2)}) collective-permute-start(bf16[544,128]{1,0:T(8,128)(2,1)S(1)} %constant_dynamic-update-slice_fusion.refs_0_), channel_id=1, source_target_pairs={{0,1},{1,0},{2,3},{3,2},{4,5},{5,4},{6,7},{7,6},{8,9},{9,8},{10,11... | collective-permute-start | bytes 417800 | tf_op jit(solution)/shard_map/ppermute | solution.py:327
  18.2 9.2 %collective-permute-start.5 = (bf16[544,128]{1,0:T(8,128)(2,1)S(1)}, bf16[544,128]{1,0:T(8,128)(2,1)S(1)}, u32[]{:S(2)}, u32[]{:S(2)}) collective-permute-start(bf16[544,128]{1,0:T(8,128)(2,1)S(1)} %constant_dynamic-update-slice_fusion.refs_0_), channel_id=1, source_target_pairs={{0,8},{8,0},{16,24},{24,16},{1,9},{9,1},{17,25},{25,17},{2,10},{10... | collective-permute-start | bytes 417800 | tf_op jit(solution)/shard_map/ppermute | solution.py:327
  19.9 7.4 %collective-permute-start.1 = (bf16[544,128]{1,0:T(8,128)(2,1)S(1)}, bf16[544,128]{1,0:T(8,128)(2,1)S(1)}, u32[]{:S(2)}, u32[]{:S(2)}) collective-permute-start(bf16[544,128]{1,0:T(8,128)(2,1)S(1)} %constant_dynamic-update-slice_fusion.refs_0_), channel_id=1, source_target_pairs={{0,16},{8,24},{16,0},{24,8},{1,17},{9,25},{17,1},{25,9},{2,18},{10... | collective-permute-start | bytes 417800 | tf_op jit(solution)/shard_map/ppermute | solution.py:327
  24.3 5.1 %collective-permute-start.7 = (bf16[544,128]{1,0:T(8,128)(2,1)S(1)}, bf16[544,128]{1,0:T(8,128)(2,1)S(1)}, u32[]{:S(2)}, u32[]{:S(2)}) collective-permute-start(bf16[544,128]{1,0:T(8,128)(2,1)S(1)} %pad_maximum_fusion.refs_5_), channel_id=1, source_target_pairs={{0,16},{8,24},{16,0},{24,8},{1,17},{9,25},{17,1},{25,9},{2,18},{10... | collective-permute-start | bytes 417800 | tf_op jit(solution)/shard_map/ppermute | solution.py:327
  25.9 5.1 %collective-permute-start.10 = (bf16[544,128]{1,0:T(8,128)(2,1)S(1)}, bf16[544,128]{1,0:T(8,128)(2,1)S(1)}, u32[]{:S(2)}, u32[]{:S(2)}) collective-permute-start(bf16[544,128]{1,0:T(8,128)(2,1)S(1)} %pad_maximum_fusion.refs_5_), channel_id=1, source_target_pairs={{0,8},{8,0},{16,24},{24,16},{1,9},{9,1},{17,25},{25,17},{2,10},{10... | collective-permute-start | bytes 417800 | tf_op jit(solution)/shard_map/ppermute | solution.py:327
  27.4 3.6 %collective-permute-start.8 = (bf16[544,128]{1,0:T(8,128)(2,1)S(1)}, bf16[544,128]{1,0:T(8,128)(2,1)S(1)}, u32[]{:S(2)}, u32[]{:S(2)}) collective-permute-start(bf16[544,128]{1,0:T(8,128)(2,1)S(1)} %pad_maximum_fusion.refs_5_), channel_id=1, source_target_pairs={{0,1},{1,0},{2,3},{3,2},{4,5},{5,4},{6,7},{7,6},{8,9},{9,8},{10,11... | collective-permute-start | bytes 417800 | tf_op jit(solution)/shard_map/ppermute | solution.py:327
  27.4 3.6 %collective-permute-start.6 = (bf16[544,128]{1,0:T(8,128)(2,1)S(1)}, bf16[544,128]{1,0:T(8,128)(2,1)S(1)}, u32[]{:S(2)}, u32[]{:S(2)}) collective-permute-start(bf16[544,128]{1,0:T(8,128)(2,1)S(1)} %collective-permute-done.1.refs_1_), channel_id=1, source_target_pairs={{0,1},{1,0},{2,3},{3,2},{4,5},{5,4},{6,7},{7,6},{8,9},{9,8},{10,11... | collective-permute-start | bytes 417800 | tf_op jit(solution)/shard_map/ppermute | solution.py:327
  29.4 1.5 %collective-permute-start.9 = (bf16[544,128]{1,0:T(8,128)(2,1)S(1)}, bf16[544,128]{1,0:T(8,128)(2,1)S(1)}, u32[]{:S(2)}, u32[]{:S(2)}) collective-permute-start(bf16[544,128]{1,0:T(8,128)(2,1)S(1)} %collective-permute-done.7.refs_6_), channel_id=1, source_target_pairs={{0,1},{1,0},{2,3},{3,2},{4,5},{5,4},{6,7},{7,6},{8,9},{9,8},{10,11... | collective-permute-start | bytes 417800 | tf_op jit(solution)/shard_map/ppermute | solution.py:327
  31.7 6.9 %collective-permute-start.11 = (bf16[64,512]{1,0:T(8,128)(2,1)S(1)}, bf16[64,512]{1,0:T(8,128)(2,1)S(1)}, u32[]{:S(2)}, u32[]{:S(2)}) collective-permute-start(bf16[64,512]{1,0:T(8,128)(2,1)S(1)} %get-tuple-element.26), channel_id=1, source_target_pairs={{0,6},{1,7},{2,4},{3,5},{4,2},{5,3},{6,0},{7,1},{8,14},{9,15},{10,... | collective-permute-start | bytes 196616 | tf_op jit(solution)/shard_map/ppermute | solution.py:327
  35.0 5.6 %collective-permute-start.12 = (bf16[64,512]{1,0:T(8,128)(2,1)S(1)}, bf16[64,512]{1,0:T(8,128)(2,1)S(1)}, u32[]{:S(2)}, u32[]{:S(2)}) collective-permute-start(bf16[64,512]{1,0:T(8,128)(2,1)S(1)} %get-tuple-element.27), channel_id=1, source_target_pairs={{0,4},{1,5},{2,6},{3,7},{4,0},{5,1},{6,2},{7,3},{8,12},{9,13},{10,... | collective-permute-start | bytes 196616 | tf_op jit(solution)/shard_map/ppermute | solution.py:327
  35.0 5.8 %collective-permute-start.13 = (bf16[64,512]{1,0:T(8,128)(2,1)S(1)}, bf16[64,512]{1,0:T(8,128)(2,1)S(1)}, u32[]{:S(2)}, u32[]{:S(2)}) collective-permute-start(bf16[64,512]{1,0:T(8,128)(2,1)S(1)} %get-tuple-element.28), channel_id=1, source_target_pairs={{0,2},{1,3},{2,0},{3,1},{4,6},{5,7},{6,4},{7,5},{8,10},{9,11},{10,... | collective-permute-start | bytes 196616 | tf_op jit(solution)/shard_map/ppermute | solution.py:327
  40.8 4.0 %collective-permute-start.14 = (bf16[32,512]{1,0:T(8,128)(2,1)S(1)}, bf16[32,512]{1,0:T(8,128)(2,1)S(1)}, u32[]{:S(2)}, u32[]{:S(2)}) collective-permute-start(bf16[32,512]{1,0:T(8,128)(2,1)S(1)} %get-tuple-element.30), channel_id=1, source_target_pairs={{0,8},{8,0},{16,24},{24,16},{1,9},{9,1},{17,25},{25,17},{2,10},{10... | collective-permute-start | bytes 98312 | tf_op jit(solution)/shard_map/ppermute | solution.py:327

commit v7 on v5

--- a/solution.py
+++ b/solution.py
@@ -351,7 +351,8 @@
         slabs += columns + others + rows
     partial = products(slabs, slices, pieces, examples, row_groups, column_groups)
     parts = [partial[0]] + [
-        swap(partial[index], "mem", members, cores * index) for index in reversed(range(1, slices))]
+        swap(partial[index], "mem", members, cores * index)
+        for index in (*range(slices // 2, slices), *reversed(range(1, slices // 2)))]
     sums = totals(parts, examples)
     sums = [swap(value, "grp", groups, step) for step, value in enumerate(sums)]
     return finish(sums, column_groups, factor)

time: 44 us -> 44.1 us (level)
  waiting for transfers between devices: 13.4 us -> 14 us
  starting transfers between devices: 18.2 us -> 17.7 us
    ppermute x15, waiting for transfers between devices: 13.4 us -> 14 us  [swap(): lax.ppermute(value, axis, [(place, place ^ distance) for place in range(s...]
    ppermute x15, starting transfers between devices: 18.2 us -> 17.7 us  [swap(): lax.ppermute(value, axis, [(place, place ^ distance) for place in range(s...]
  transfers between devices with their start and end apart: 15 -> 15, of which waited for: 8 -> 7; matrix products, arithmetic and copies ran while one was open for 0% -> 0% of each run, Pallas kernels for 0% -> 0%
where the time goes in v7:
time: 44.1 us; the launch traced here: 44 us
  starting transfers between devices  17.7 us (40%)
  waiting for transfers between devices  14 us (32%)
  Pallas kernels  12.1 us (27%)
    ppermute x15, starting transfers between devices, swap(): lax.ppermute(value, axis, [(place, place ^ distance) for place in range(s...  17.7 us
    ppermute x15, waiting for transfers between devices, swap(): lax.ppermute(value, axis, [(place, place ^ distance) for place in range(s...  14 us
    pallas_call x1, Pallas kernels, features(): pl.pallas_call(functools.partial(feature_kernel, tokens, slices), out_sha...  10.7 us
  transfers between devices with their start and end apart: 15, of which 7 were waited for; matrix products, arithmetic and copies ran while one was open for 0% of the time, Pallas kernels for 0%

profile of v7, /device:TPU:0, one launch (start us, length us, event | category | flops | bytes accessed | tf_op | source)
XLA Modules:
  0.0 44.0 jit_solution(7801045998233191458)
XLA Ops:
  0.0 10.7 %features.1 = (bf16[272,128]{1,0:T(8,128)(2,1)S(1)}, bf16[272,128]{1,0:T(8,128)(2,1)S(1)}, bf16[272,128]{1,0:T(8,128)(2,1)S(1)}, bf16[272,128]{1,0:T(8,128)(2,1)S(1)}) custom-call(bf16[1024,4096]{1,0:T(8,128)(2,1)} %bitcast.5, bf16[1024,4096]{1,0:T(8,128)(2,1)} %bitcast.6, bf16[64,4096]{1,0:T(8,128)(2,1)} %bitcast.7, bf16[64,4096]{1,0:T(8,128)(2,1)} %bitcast.8, ...), custom_call_target="tpu_custom_call" | custom-call | flops 1073741824 | bytes 16777216 | tf_op jit(solution)/shard_map/features/pallas_call | solution.py:152
  10.7 3.1 %collective-permute-start = (bf16[272,128]{1,0:T(8,128)(2,1)S(1)}, bf16[272,128]{1,0:T(8,128)(2,1)S(1)}, u32[]{:S(2)}, u32[]{:S(2)}) collective-permute-start(bf16[272,128]{1,0:T(8,128)(2,1)S(1)} %get-tuple-element.19), channel_id=1, source_target_pairs={{0,2},{1,3},{2,0},{3,1},{4,6},{5,7},{6,4},{7,5},{8,10},{9,11},{10,... | collective-permute-start | bytes 208904 | tf_op jit(solution)/shard_map/ppermute | solution.py:326
  13.8 2.6 %collective-permute-start.2 = (bf16[272,128]{1,0:T(8,128)(2,1)S(1)}, bf16[272,128]{1,0:T(8,128)(2,1)S(1)}, u32[]{:S(2)}, u32[]{:S(2)}) collective-permute-start(bf16[272,128]{1,0:T(8,128)(2,1)S(1)} %get-tuple-element.20), channel_id=1, source_target_pairs={{0,4},{1,5},{2,6},{3,7},{4,0},{5,1},{6,2},{7,3},{8,12},{9,13},{10,... | collective-permute-start | bytes 208904 | tf_op jit(solution)/shard_map/ppermute | solution.py:326
  16.4 0.0 collective-permute-done
  16.4 0.1 collective-permute-start.4
  16.5 1.8 %collective-permute-start.5 = (bf16[544,128]{1,0:T(8,128)(2,1)S(1)}, bf16[544,128]{1,0:T(8,128)(2,1)S(1)}, u32[]{:S(2)}, u32[]{:S(2)}) collective-permute-start(bf16[544,128]{1,0:T(8,128)(2,1)S(1)} %constant_dynamic-update-slice_fusion.refs_0_), channel_id=1, source_target_pairs={{0,8},{8,0},{16,24},{24,16},{1,9},{9,1},{17,25},{25,17},{2,10},{10... | collective-permute-start | bytes 417800 | tf_op jit(solution)/shard_map/ppermute | solution.py:326
  18.3 1.5 %collective-permute-start.1 = (bf16[544,128]{1,0:T(8,128)(2,1)S(1)}, bf16[544,128]{1,0:T(8,128)(2,1)S(1)}, u32[]{:S(2)}, u32[]{:S(2)}) collective-permute-start(bf16[544,128]{1,0:T(8,128)(2,1)S(1)} %constant_dynamic-update-slice_fusion.refs_0_), channel_id=1, source_target_pairs={{0,16},{8,24},{16,0},{24,8},{1,17},{9,25},{17,1},{25,9},{2,18},{10... | collective-permute-start | bytes 417800 | tf_op jit(solution)/shard_map/ppermute | solution.py:326
  19.8 1.5 %collective-permute-done.2 = bf16[272,128]{1,0:T(8,128)(2,1)S(1)} collective-permute-done((bf16[272,128]{1,0:T(8,128)(2,1)S(1)}, bf16[272,128]{1,0:T(8,128)(2,1)S(1)}, u32[]{:S(2)}, u32[]{:S(2)}) %collective-permute-start.2) | collective-permute-done | bytes 69664 | tf_op jit(solution)/shard_map/ppermute | solution.py:326
  21.3 1.3 %collective-permute-done.3 = bf16[272,128]{1,0:T(8,128)(2,1)S(1)} collective-permute-done((bf16[272,128]{1,0:T(8,128)(2,1)S(1)}, bf16[272,128]{1,0:T(8,128)(2,1)S(1)}, u32[]{:S(2)}, u32[]{:S(2)}) %collective-permute-start.3) | collective-permute-done | bytes 69664 | tf_op jit(solution)/shard_map/ppermute | solution.py:326
  22.6 1.6 %collective-permute-start.7 = (bf16[544,128]{1,0:T(8,128)(2,1)S(1)}, bf16[544,128]{1,0:T(8,128)(2,1)S(1)}, u32[]{:S(2)}, u32[]{:S(2)}) collective-permute-start(bf16[544,128]{1,0:T(8,128)(2,1)S(1)} %pad_maximum_fusion.refs_5_), channel_id=1, source_target_pairs={{0,16},{8,24},{16,0},{24,8},{1,17},{9,25},{17,1},{25,9},{2,18},{10... | collective-permute-start | bytes 417800 | tf_op jit(solution)/shard_map/ppermute | solution.py:326
  24.2 1.5 %collective-permute-start.10 = (bf16[544,128]{1,0:T(8,128)(2,1)S(1)}, bf16[544,128]{1,0:T(8,128)(2,1)S(1)}, u32[]{:S(2)}, u32[]{:S(2)}) collective-permute-start(bf16[544,128]{1,0:T(8,128)(2,1)S(1)} %pad_maximum_fusion.refs_5_), channel_id=1, source_target_pairs={{0,8},{8,0},{16,24},{24,16},{1,9},{9,1},{17,25},{25,17},{2,10},{10... | collective-permute-start | bytes 417800 | tf_op jit(solution)/shard_map/ppermute | solution.py:326
  25.7 0.0 collective-permute-start.8
  25.7 0.5 %collective-permute-start.6 = (bf16[544,128]{1,0:T(8,128)(2,1)S(1)}, bf16[544,128]{1,0:T(8,128)(2,1)S(1)}, u32[]{:S(2)}, u32[]{:S(2)}) collective-permute-start(bf16[544,128]{1,0:T(8,128)(2,1)S(1)} %collective-permute-done.1.refs_1_), channel_id=1, source_target_pairs={{0,1},{1,0},{2,3},{3,2},{4,5},{5,4},{6,7},{7,6},{8,9},{9,8},{10,11... | collective-permute-start | bytes 417800 | tf_op jit(solution)/shard_map/ppermute | solution.py:326
  26.2 1.5 %collective-permute-done.7.refs_6_ = bf16[544,128]{1,0:T(8,128)(2,1)S(1)} collective-permute-done((bf16[544,128]{1,0:T(8,128)(2,1)S(1)}, bf16[544,128]{1,0:T(8,128)(2,1)S(1)}, u32[]{:S(2)}, u32[]{:S(2)}) %collective-permute-start.7) | collective-permute-done | bytes 139296 | tf_op jit(solution)/shard_map/ppermute | solution.py:326
  27.7 1.5 %collective-permute-done.10.refs_9_ = bf16[544,128]{1,0:T(8,128)(2,1)S(1)} collective-permute-done((bf16[544,128]{1,0:T(8,128)(2,1)S(1)}, bf16[544,128]{1,0:T(8,128)(2,1)S(1)}, u32[]{:S(2)}, u32[]{:S(2)}) %collective-permute-start.10) | collective-permute-done | bytes 139296 | tf_op jit(solution)/shard_map/ppermute | solution.py:326
  29.3 0.7 %products.1 = (bf16[64,512]{1,0:T(8,128)(2,1)S(1)}, bf16[64,512]{1,0:T(8,128)(2,1)S(1)}, bf16[64,512]{1,0:T(8,128)(2,1)S(1)}, bf16[64,512]{1,0:T(8,128)(2,1)S(1)}) custom-call(bf16[544,128]{1,0:T(8,128)(2,1)S(1)} %constant_dynamic-update-slice_fusion.refs_0_, bf16[544,128]{1,0:T(8,128)(2,1)S(1)} %collective-permute-done.1.refs_1_, ...), custom_call_target="tpu_custom_call" | custom-call | flops 268435456 | bytes 524288 | tf_op jit(solution)/shard_map/products/pallas_call | solution.py:251
  30.0 2.0 %collective-permute-start.11 = (bf16[64,512]{1,0:T(8,128)(2,1)S(1)}, bf16[64,512]{1,0:T(8,128)(2,1)S(1)}, u32[]{:S(2)}, u32[]{:S(2)}) collective-permute-start(bf16[64,512]{1,0:T(8,128)(2,1)S(1)} %get-tuple-element.26), channel_id=1, source_target_pairs={{0,4},{1,5},{2,6},{3,7},{4,0},{5,1},{6,2},{7,3},{8,12},{9,13},{10,... | collective-permute-start | bytes 196616 | tf_op jit(solution)/shard_map/ppermute | solution.py:326
  32.0 1.4 %collective-permute-start.12 = (bf16[64,512]{1,0:T(8,128)(2,1)S(1)}, bf16[64,512]{1,0:T(8,128)(2,1)S(1)}, u32[]{:S(2)}, u32[]{:S(2)}) collective-permute-start(bf16[64,512]{1,0:T(8,128)(2,1)S(1)} %get-tuple-element.27), channel_id=1, source_target_pairs={{0,6},{1,7},{2,4},{3,5},{4,2},{5,3},{6,0},{7,1},{8,14},{9,15},{10,... | collective-permute-start | bytes 196616 | tf_op jit(solution)/shard_map/ppermute | solution.py:326
  33.4 0.5 %collective-permute-start.13 = (bf16[64,512]{1,0:T(8,128)(2,1)S(1)}, bf16[64,512]{1,0:T(8,128)(2,1)S(1)}, u32[]{:S(2)}, u32[]{:S(2)}) collective-permute-start(bf16[64,512]{1,0:T(8,128)(2,1)S(1)} %get-tuple-element.28), channel_id=1, source_target_pairs={{0,2},{1,3},{2,0},{3,1},{4,6},{5,7},{6,4},{7,5},{8,10},{9,11},{10,... | collective-permute-start | bytes 196616 | tf_op jit(solution)/shard_map/ppermute | solution.py:326
  33.9 4.5 %collective-permute-done.11.refs_1_ = bf16[64,512]{1,0:T(8,128)(2,1)S(1)} collective-permute-done((bf16[64,512]{1,0:T(8,128)(2,1)S(1)}, bf16[64,512]{1,0:T(8,128)(2,1)S(1)}, u32[]{:S(2)}, u32[]{:S(2)}) %collective-permute-start.11) | collective-permute-done | bytes 65568 | tf_op jit(solution)/shard_map/ppermute | solution.py:326
  38.5 0.8 %collective-permute-done.13.refs_3_ = bf16[64,512]{1,0:T(8,128)(2,1)S(1)} collective-permute-done((bf16[64,512]{1,0:T(8,128)(2,1)S(1)}, bf16[64,512]{1,0:T(8,128)(2,1)S(1)}, u32[]{:S(2)}, u32[]{:S(2)}) %collective-permute-start.13) | collective-permute-done | bytes 65568 | tf_op jit(solution)/shard_map/ppermute | solution.py:326
  39.3 1.2 %collective-permute-start.14 = (bf16[32,512]{1,0:T(8,128)(2,1)S(1)}, bf16[32,512]{1,0:T(8,128)(2,1)S(1)}, u32[]{:S(2)}, u32[]{:S(2)}) collective-permute-start(bf16[32,512]{1,0:T(8,128)(2,1)S(1)} %get-tuple-element.30), channel_id=1, source_target_pairs={{0,8},{8,0},{16,24},{24,16},{1,9},{9,1},{17,25},{25,17},{2,10},{10... | collective-permute-start | bytes 98312 | tf_op jit(solution)/shard_map/ppermute | solution.py:326
  40.5 2.8 %collective-permute-done.14.refs_1_ = bf16[32,512]{1,0:T(8,128)(2,1)S(1)} collective-permute-done((bf16[32,512]{1,0:T(8,128)(2,1)S(1)}, bf16[32,512]{1,0:T(8,128)(2,1)S(1)}, u32[]{:S(2)}, u32[]{:S(2)}) %collective-permute-start.14) | collective-permute-done | bytes 32800 | tf_op jit(solution)/shard_map/ppermute | solution.py:326
  43.3 0.7 %finish.1 = f32[32,1024]{1,0:T(8,128)} custom-call(f32[32,512]{1,0:T(8,128)S(1)} %get-tuple-element.29.refs_0_, bf16[32,512]{1,0:T(8,128)(2,1)S(1)} %collective-permute-done.14.refs_1_), custom_call_target="tpu_custom_call" | custom-call | flops 131072 | bytes 262144 | tf_op jit(solution)/shard_map/finish/pallas_call | solution.py:311
  (13 shorter events, 0.1 us)
Async XLA Ops:
  10.7 5.7 %collective-permute-start = (bf16[272,128]{1,0:T(8,128)(2,1)S(1)}, bf16[272,128]{1,0:T(8,128)(2,1)S(1)}, u32[]{:S(2)}, u32[]{:S(2)}) collective-permute-start(bf16[272,128]{1,0:T(8,128)(2,1)S(1)} %get-tuple-element.19), channel_id=1, source_target_pairs={{0,2},{1,3},{2,0},{3,1},{4,6},{5,7},{6,4},{7,5},{8,10},{9,11},{10,... | collective-permute-start | bytes 208904 | tf_op jit(solution)/shard_map/ppermute | solution.py:326
  13.8 7.5 %collective-permute-start.2 = (bf16[272,128]{1,0:T(8,128)(2,1)S(1)}, bf16[272,128]{1,0:T(8,128)(2,1)S(1)}, u32[]{:S(2)}, u32[]{:S(2)}) collective-permute-start(bf16[272,128]{1,0:T(8,128)(2,1)S(1)} %get-tuple-element.20), channel_id=1, source_target_pairs={{0,4},{1,5},{2,6},{3,7},{4,0},{5,1},{6,2},{7,3},{8,12},{9,13},{10,... | collective-permute-start | bytes 208904 | tf_op jit(solution)/shard_map/ppermute | solution.py:326
  16.4 6.2 %collective-permute-start.3 = (bf16[272,128]{1,0:T(8,128)(2,1)S(1)}, bf16[272,128]{1,0:T(8,128)(2,1)S(1)}, u32[]{:S(2)}, u32[]{:S(2)}) collective-permute-start(bf16[272,128]{1,0:T(8,128)(2,1)S(1)} %get-tuple-element.21), channel_id=1, source_target_pairs={{0,6},{1,7},{2,4},{3,5},{4,2},{5,3},{6,0},{7,1},{8,14},{9,15},{10,... | collective-permute-start | bytes 208904 | tf_op jit(solution)/shard_map/ppermute | solution.py:326
  16.4 6.2 %collective-permute-start.4 = (bf16[544,128]{1,0:T(8,128)(2,1)S(1)}, bf16[544,128]{1,0:T(8,128)(2,1)S(1)}, u32[]{:S(2)}, u32[]{:S(2)}) collective-permute-start(bf16[544,128]{1,0:T(8,128)(2,1)S(1)} %constant_dynamic-update-slice_fusion.refs_0_), channel_id=1, source_target_pairs={{0,1},{1,0},{2,3},{3,2},{4,5},{5,4},{6,7},{7,6},{8,9},{9,8},{10,11... | collective-permute-start | bytes 417800 | tf_op jit(solution)/shard_map/ppermute | solution.py:326
  16.5 9.2 %collective-permute-start.5 = (bf16[544,128]{1,0:T(8,128)(2,1)S(1)}, bf16[544,128]{1,0:T(8,128)(2,1)S(1)}, u32[]{:S(2)}, u32[]{:S(2)}) collective-permute-start(bf16[544,128]{1,0:T(8,128)(2,1)S(1)} %constant_dynamic-update-slice_fusion.refs_0_), channel_id=1, source_target_pairs={{0,8},{8,0},{16,24},{24,16},{1,9},{9,1},{17,25},{25,17},{2,10},{10... | collective-permute-start | bytes 417800 | tf_op jit(solution)/shard_map/ppermute | solution.py:326
  18.3 7.4 %collective-permute-start.1 = (bf16[544,128]{1,0:T(8,128)(2,1)S(1)}, bf16[544,128]{1,0:T(8,128)(2,1)S(1)}, u32[]{:S(2)}, u32[]{:S(2)}) collective-permute-start(bf16[544,128]{1,0:T(8,128)(2,1)S(1)} %constant_dynamic-update-slice_fusion.refs_0_), channel_id=1, source_target_pairs={{0,16},{8,24},{16,0},{24,8},{1,17},{9,25},{17,1},{25,9},{2,18},{10... | collective-permute-start | bytes 417800 | tf_op jit(solution)/shard_map/ppermute | solution.py:326
  22.6 5.1 %collective-permute-start.7 = (bf16[544,128]{1,0:T(8,128)(2,1)S(1)}, bf16[544,128]{1,0:T(8,128)(2,1)S(1)}, u32[]{:S(2)}, u32[]{:S(2)}) collective-permute-start(bf16[544,128]{1,0:T(8,128)(2,1)S(1)} %pad_maximum_fusion.refs_5_), channel_id=1, source_target_pairs={{0,16},{8,24},{16,0},{24,8},{1,17},{9,25},{17,1},{25,9},{2,18},{10... | collective-permute-start | bytes 417800 | tf_op jit(solution)/shard_map/ppermute | solution.py:326
  24.2 5.1 %collective-permute-start.10 = (bf16[544,128]{1,0:T(8,128)(2,1)S(1)}, bf16[544,128]{1,0:T(8,128)(2,1)S(1)}, u32[]{:S(2)}, u32[]{:S(2)}) collective-permute-start(bf16[544,128]{1,0:T(8,128)(2,1)S(1)} %pad_maximum_fusion.refs_5_), channel_id=1, source_target_pairs={{0,8},{8,0},{16,24},{24,16},{1,9},{9,1},{17,25},{25,17},{2,10},{10... | collective-permute-start | bytes 417800 | tf_op jit(solution)/shard_map/ppermute | solution.py:326
  25.7 3.6 %collective-permute-start.8 = (bf16[544,128]{1,0:T(8,128)(2,1)S(1)}, bf16[544,128]{1,0:T(8,128)(2,1)S(1)}, u32[]{:S(2)}, u32[]{:S(2)}) collective-permute-start(bf16[544,128]{1,0:T(8,128)(2,1)S(1)} %pad_maximum_fusion.refs_5_), channel_id=1, source_target_pairs={{0,1},{1,0},{2,3},{3,2},{4,5},{5,4},{6,7},{7,6},{8,9},{9,8},{10,11... | collective-permute-start | bytes 417800 | tf_op jit(solution)/shard_map/ppermute | solution.py:326
  25.7 3.6 %collective-permute-start.6 = (bf16[544,128]{1,0:T(8,128)(2,1)S(1)}, bf16[544,128]{1,0:T(8,128)(2,1)S(1)}, u32[]{:S(2)}, u32[]{:S(2)}) collective-permute-start(bf16[544,128]{1,0:T(8,128)(2,1)S(1)} %collective-permute-done.1.refs_1_), channel_id=1, source_target_pairs={{0,1},{1,0},{2,3},{3,2},{4,5},{5,4},{6,7},{7,6},{8,9},{9,8},{10,11... | collective-permute-start | bytes 417800 | tf_op jit(solution)/shard_map/ppermute | solution.py:326
  27.7 1.5 %collective-permute-start.9 = (bf16[544,128]{1,0:T(8,128)(2,1)S(1)}, bf16[544,128]{1,0:T(8,128)(2,1)S(1)}, u32[]{:S(2)}, u32[]{:S(2)}) collective-permute-start(bf16[544,128]{1,0:T(8,128)(2,1)S(1)} %collective-permute-done.7.refs_6_), channel_id=1, source_target_pairs={{0,1},{1,0},{2,3},{3,2},{4,5},{5,4},{6,7},{7,6},{8,9},{9,8},{10,11... | collective-permute-start | bytes 417800 | tf_op jit(solution)/shard_map/ppermute | solution.py:326
  30.0 8.5 %collective-permute-start.11 = (bf16[64,512]{1,0:T(8,128)(2,1)S(1)}, bf16[64,512]{1,0:T(8,128)(2,1)S(1)}, u32[]{:S(2)}, u32[]{:S(2)}) collective-permute-start(bf16[64,512]{1,0:T(8,128)(2,1)S(1)} %get-tuple-element.26), channel_id=1, source_target_pairs={{0,4},{1,5},{2,6},{3,7},{4,0},{5,1},{6,2},{7,3},{8,12},{9,13},{10,... | collective-permute-start | bytes 196616 | tf_op jit(solution)/shard_map/ppermute | solution.py:326
  32.0 6.5 %collective-permute-start.12 = (bf16[64,512]{1,0:T(8,128)(2,1)S(1)}, bf16[64,512]{1,0:T(8,128)(2,1)S(1)}, u32[]{:S(2)}, u32[]{:S(2)}) collective-permute-start(bf16[64,512]{1,0:T(8,128)(2,1)S(1)} %get-tuple-element.27), channel_id=1, source_target_pairs={{0,6},{1,7},{2,4},{3,5},{4,2},{5,3},{6,0},{7,1},{8,14},{9,15},{10,... | collective-permute-start | bytes 196616 | tf_op jit(solution)/shard_map/ppermute | solution.py:326
  33.4 5.9 %collective-permute-start.13 = (bf16[64,512]{1,0:T(8,128)(2,1)S(1)}, bf16[64,512]{1,0:T(8,128)(2,1)S(1)}, u32[]{:S(2)}, u32[]{:S(2)}) collective-permute-start(bf16[64,512]{1,0:T(8,128)(2,1)S(1)} %get-tuple-element.28), channel_id=1, source_target_pairs={{0,2},{1,3},{2,0},{3,1},{4,6},{5,7},{6,4},{7,5},{8,10},{9,11},{10,... | collective-permute-start | bytes 196616 | tf_op jit(solution)/shard_map/ppermute | solution.py:326
  39.3 4.0 %collective-permute-start.14 = (bf16[32,512]{1,0:T(8,128)(2,1)S(1)}, bf16[32,512]{1,0:T(8,128)(2,1)S(1)}, u32[]{:S(2)}, u32[]{:S(2)}) collective-permute-start(bf16[32,512]{1,0:T(8,128)(2,1)S(1)} %get-tuple-element.30), channel_id=1, source_target_pairs={{0,8},{8,0},{16,24},{24,16},{1,9},{9,1},{17,25},{25,17},{2,10},{10... | collective-permute-start | bytes 98312 | tf_op jit(solution)/shard_map/ppermute | solution.py:326

commit v8 on v5

--- a/solution.py
+++ b/solution.py
@@ -62,9 +62,10 @@
         for index, (source, target) in enumerate((
             (bin_hbm, bin_ref), (bout_hbm, bout_ref), (eigen_hbm, eigen_ref), (ids_hbm, ids_ref)))
     ]
-    for copy in weights:
-        copy.start()
-    start_half(0)
+    weights[0].start()
+    half_copies(0)[0].start(priority=0)
+    weights[1].start()
+    half_copies(0)[1].start(priority=1)
     for copy in small:
         copy.start()
     for index in range(1, halves):
@@ -85,8 +86,7 @@
     place = lax.broadcasted_iota(jnp.int32, (id_rows, 2 * rank), 0) % 4
     digits = (jnp.broadcast_to(ids, (id_rows, 2 * rank)) >> (place * 8)) & 255
     digits = digits.astype(jnp.float32).astype(jnp.bfloat16)
-    for copy in weights:
-        copy.wait()
+    weights[0].wait()
 
     def project(index, beside):
         rng = pl.ds(index * half_rows, half_rows)
@@ -95,6 +95,8 @@
         act_proj[rng] = dot_nt(pin[...], act[rng]).T.astype(jnp.bfloat16)
         for step in beside[0::2]:
             rotate(step)
+        if index == 0:
+            weights[1].wait()
         grad_copy.wait()
         grad_proj[:, rng] = dot_nt(pout[...], grad[rng]).astype(jnp.bfloat16)
         for step in beside[1::2]:

time: 44 us -> 44 us (level)
  no operation moved by 1% of the time
where the time goes in v8:
time: 44 us; the launch traced here: 43.8 us
  starting transfers between devices  18.2 us (41%)
  waiting for transfers between devices  13.4 us (30%)
  Pallas kernels  12.1 us (28%)
    ppermute x15, starting transfers between devices, swap(): lax.ppermute(value, axis, [(place, place ^ distance) for place in range(s...  18.2 us
    ppermute x15, waiting for transfers between devices, swap(): lax.ppermute(value, axis, [(place, place ^ distance) for place in range(s...  13.4 us
    pallas_call x1, Pallas kernels, features(): pl.pallas_call(functools.partial(feature_kernel, tokens, slices), out_sha...  10.7 us
  transfers between devices with their start and end apart: 15, of which 8 were waited for; matrix products, arithmetic and copies ran while one was open for 0% of the time, Pallas kernels for 0%

profile of v8, /device:TPU:0, one launch (start us, length us, event | category | flops | bytes accessed | tf_op | source)
XLA Modules:
  0.0 43.8 jit_solution(11969684651958076561)
XLA Ops:
  0.0 10.7 %features.1 = (bf16[272,128]{1,0:T(8,128)(2,1)S(1)}, bf16[272,128]{1,0:T(8,128)(2,1)S(1)}, bf16[272,128]{1,0:T(8,128)(2,1)S(1)}, bf16[272,128]{1,0:T(8,128)(2,1)S(1)}) custom-call(bf16[1024,4096]{1,0:T(8,128)(2,1)} %bitcast.5, bf16[1024,4096]{1,0:T(8,128)(2,1)} %bitcast.6, bf16[64,4096]{1,0:T(8,128)(2,1)} %bitcast.7, bf16[64,4096]{1,0:T(8,128)(2,1)} %bitcast.8, ...), custom_call_target="tpu_custom_call" | custom-call | flops 1073741824 | bytes 16777216 | tf_op jit(solution)/shard_map/features/pallas_call | solution.py:154
  10.7 3.1 %collective-permute-start = (bf16[272,128]{1,0:T(8,128)(2,1)S(1)}, bf16[272,128]{1,0:T(8,128)(2,1)S(1)}, u32[]{:S(2)}, u32[]{:S(2)}) collective-permute-start(bf16[272,128]{1,0:T(8,128)(2,1)S(1)} %get-tuple-element.19), channel_id=1, source_target_pairs={{0,2},{1,3},{2,0},{3,1},{4,6},{5,7},{6,4},{7,5},{8,10},{9,11},{10,... | collective-permute-start | bytes 208904 | tf_op jit(solution)/shard_map/ppermute | solution.py:328
  13.8 2.6 %collective-permute-start.2 = (bf16[272,128]{1,0:T(8,128)(2,1)S(1)}, bf16[272,128]{1,0:T(8,128)(2,1)S(1)}, u32[]{:S(2)}, u32[]{:S(2)}) collective-permute-start(bf16[272,128]{1,0:T(8,128)(2,1)S(1)} %get-tuple-element.20), channel_id=1, source_target_pairs={{0,4},{1,5},{2,6},{3,7},{4,0},{5,1},{6,2},{7,3},{8,12},{9,13},{10,... | collective-permute-start | bytes 208904 | tf_op jit(solution)/shard_map/ppermute | solution.py:328
  16.4 0.1 collective-permute-start.4
  16.5 1.8 %collective-permute-start.5 = (bf16[544,128]{1,0:T(8,128)(2,1)S(1)}, bf16[544,128]{1,0:T(8,128)(2,1)S(1)}, u32[]{:S(2)}, u32[]{:S(2)}) collective-permute-start(bf16[544,128]{1,0:T(8,128)(2,1)S(1)} %constant_dynamic-update-slice_fusion.refs_0_), channel_id=1, source_target_pairs={{0,8},{8,0},{16,24},{24,16},{1,9},{9,1},{17,25},{25,17},{2,10},{10... | collective-permute-start | bytes 417800 | tf_op jit(solution)/shard_map/ppermute | solution.py:328
  18.3 1.5 %collective-permute-start.1 = (bf16[544,128]{1,0:T(8,128)(2,1)S(1)}, bf16[544,128]{1,0:T(8,128)(2,1)S(1)}, u32[]{:S(2)}, u32[]{:S(2)}) collective-permute-start(bf16[544,128]{1,0:T(8,128)(2,1)S(1)} %constant_dynamic-update-slice_fusion.refs_0_), channel_id=1, source_target_pairs={{0,16},{8,24},{16,0},{24,8},{1,17},{9,25},{17,1},{25,9},{2,18},{10... | collective-permute-start | bytes 417800 | tf_op jit(solution)/shard_map/ppermute | solution.py:328
  19.8 1.5 %collective-permute-done.2 = bf16[272,128]{1,0:T(8,128)(2,1)S(1)} collective-permute-done((bf16[272,128]{1,0:T(8,128)(2,1)S(1)}, bf16[272,128]{1,0:T(8,128)(2,1)S(1)}, u32[]{:S(2)}, u32[]{:S(2)}) %collective-permute-start.2) | collective-permute-done | bytes 69664 | tf_op jit(solution)/shard_map/ppermute | solution.py:328
  21.3 1.3 %collective-permute-done.3 = bf16[272,128]{1,0:T(8,128)(2,1)S(1)} collective-permute-done((bf16[272,128]{1,0:T(8,128)(2,1)S(1)}, bf16[272,128]{1,0:T(8,128)(2,1)S(1)}, u32[]{:S(2)}, u32[]{:S(2)}) %collective-permute-start.3) | collective-permute-done | bytes 69664 | tf_op jit(solution)/shard_map/ppermute | solution.py:328
  22.6 0.0 collective-permute-done.4.refs_2_
  22.6 1.6 %collective-permute-start.7 = (bf16[544,128]{1,0:T(8,128)(2,1)S(1)}, bf16[544,128]{1,0:T(8,128)(2,1)S(1)}, u32[]{:S(2)}, u32[]{:S(2)}) collective-permute-start(bf16[544,128]{1,0:T(8,128)(2,1)S(1)} %pad_maximum_fusion.refs_5_), channel_id=1, source_target_pairs={{0,16},{8,24},{16,0},{24,8},{1,17},{9,25},{17,1},{25,9},{2,18},{10... | collective-permute-start | bytes 417800 | tf_op jit(solution)/shard_map/ppermute | solution.py:328
  24.2 1.5 %collective-permute-start.10 = (bf16[544,128]{1,0:T(8,128)(2,1)S(1)}, bf16[544,128]{1,0:T(8,128)(2,1)S(1)}, u32[]{:S(2)}, u32[]{:S(2)}) collective-permute-start(bf16[544,128]{1,0:T(8,128)(2,1)S(1)} %pad_maximum_fusion.refs_5_), channel_id=1, source_target_pairs={{0,8},{8,0},{16,24},{24,16},{1,9},{9,1},{17,25},{25,17},{2,10},{10... | collective-permute-start | bytes 417800 | tf_op jit(solution)/shard_map/ppermute | solution.py:328
  25.7 0.5 %collective-permute-start.6 = (bf16[544,128]{1,0:T(8,128)(2,1)S(1)}, bf16[544,128]{1,0:T(8,128)(2,1)S(1)}, u32[]{:S(2)}, u32[]{:S(2)}) collective-permute-start(bf16[544,128]{1,0:T(8,128)(2,1)S(1)} %collective-permute-done.1.refs_1_), channel_id=1, source_target_pairs={{0,1},{1,0},{2,3},{3,2},{4,5},{5,4},{6,7},{7,6},{8,9},{9,8},{10,11... | collective-permute-start | bytes 417800 | tf_op jit(solution)/shard_map/ppermute | solution.py:328
  26.2 1.5 %collective-permute-done.7.refs_6_ = bf16[544,128]{1,0:T(8,128)(2,1)S(1)} collective-permute-done((bf16[544,128]{1,0:T(8,128)(2,1)S(1)}, bf16[544,128]{1,0:T(8,128)(2,1)S(1)}, u32[]{:S(2)}, u32[]{:S(2)}) %collective-permute-start.7) | collective-permute-done | bytes 139296 | tf_op jit(solution)/shard_map/ppermute | solution.py:328
  27.7 1.5 %collective-permute-done.10.refs_9_ = bf16[544,128]{1,0:T(8,128)(2,1)S(1)} collective-permute-done((bf16[544,128]{1,0:T(8,128)(2,1)S(1)}, bf16[544,128]{1,0:T(8,128)(2,1)S(1)}, u32[]{:S(2)}, u32[]{:S(2)}) %collective-permute-start.10) | collective-permute-done | bytes 139296 | tf_op jit(solution)/shard_map/ppermute | solution.py:328
  29.3 0.0 collective-permute-done.8.refs_7_
  29.3 0.7 %products.1 = (bf16[64,512]{1,0:T(8,128)(2,1)S(1)}, bf16[64,512]{1,0:T(8,128)(2,1)S(1)}, bf16[64,512]{1,0:T(8,128)(2,1)S(1)}, bf16[64,512]{1,0:T(8,128)(2,1)S(1)}) custom-call(bf16[544,128]{1,0:T(8,128)(2,1)S(1)} %constant_dynamic-update-slice_fusion.refs_0_, bf16[544,128]{1,0:T(8,128)(2,1)S(1)} %collective-permute-done.1.refs_1_, ...), custom_call_target="tpu_custom_call" | custom-call | flops 268435456 | bytes 524288 | tf_op jit(solution)/shard_map/products/pallas_call | solution.py:253
  30.0 3.3 %collective-permute-start.11 = (bf16[64,512]{1,0:T(8,128)(2,1)S(1)}, bf16[64,512]{1,0:T(8,128)(2,1)S(1)}, u32[]{:S(2)}, u32[]{:S(2)}) collective-permute-start(bf16[64,512]{1,0:T(8,128)(2,1)S(1)} %get-tuple-element.26), channel_id=1, source_target_pairs={{0,6},{1,7},{2,4},{3,5},{4,2},{5,3},{6,0},{7,1},{8,14},{9,15},{10,... | collective-permute-start | bytes 196616 | tf_op jit(solution)/shard_map/ppermute | solution.py:328
  33.3 1.1 %collective-permute-start.13 = (bf16[64,512]{1,0:T(8,128)(2,1)S(1)}, bf16[64,512]{1,0:T(8,128)(2,1)S(1)}, u32[]{:S(2)}, u32[]{:S(2)}) collective-permute-start(bf16[64,512]{1,0:T(8,128)(2,1)S(1)} %get-tuple-element.28), channel_id=1, source_target_pairs={{0,2},{1,3},{2,0},{3,1},{4,6},{5,7},{6,4},{7,5},{8,10},{9,11},{10,... | collective-permute-start | bytes 196616 | tf_op jit(solution)/shard_map/ppermute | solution.py:328
  34.5 2.4 %collective-permute-done.11.refs_1_ = bf16[64,512]{1,0:T(8,128)(2,1)S(1)} collective-permute-done((bf16[64,512]{1,0:T(8,128)(2,1)S(1)}, bf16[64,512]{1,0:T(8,128)(2,1)S(1)}, u32[]{:S(2)}, u32[]{:S(2)}) %collective-permute-start.11) | collective-permute-done | bytes 65568 | tf_op jit(solution)/shard_map/ppermute | solution.py:328
  36.9 2.1 %collective-permute-done.12.refs_2_ = bf16[64,512]{1,0:T(8,128)(2,1)S(1)} collective-permute-done((bf16[64,512]{1,0:T(8,128)(2,1)S(1)}, bf16[64,512]{1,0:T(8,128)(2,1)S(1)}, u32[]{:S(2)}, u32[]{:S(2)}) %collective-permute-start.12) | collective-permute-done | bytes 65568 | tf_op jit(solution)/shard_map/ppermute | solution.py:328
  39.0 0.1 collective-permute-done.13.refs_3_
  39.2 1.1 %collective-permute-start.14 = (bf16[32,512]{1,0:T(8,128)(2,1)S(1)}, bf16[32,512]{1,0:T(8,128)(2,1)S(1)}, u32[]{:S(2)}, u32[]{:S(2)}) collective-permute-start(bf16[32,512]{1,0:T(8,128)(2,1)S(1)} %get-tuple-element.30), channel_id=1, source_target_pairs={{0,8},{8,0},{16,24},{24,16},{1,9},{9,1},{17,25},{25,17},{2,10},{10... | collective-permute-start | bytes 98312 | tf_op jit(solution)/shard_map/ppermute | solution.py:328
  40.3 2.8 %collective-permute-done.14.refs_1_ = bf16[32,512]{1,0:T(8,128)(2,1)S(1)} collective-permute-done((bf16[32,512]{1,0:T(8,128)(2,1)S(1)}, bf16[32,512]{1,0:T(8,128)(2,1)S(1)}, u32[]{:S(2)}, u32[]{:S(2)}) %collective-permute-start.14) | collective-permute-done | bytes 32800 | tf_op jit(solution)/shard_map/ppermute | solution.py:328
  43.1 0.7 %finish.1 = f32[32,1024]{1,0:T(8,128)} custom-call(f32[32,512]{1,0:T(8,128)S(1)} %get-tuple-element.29.refs_0_, bf16[32,512]{1,0:T(8,128)(2,1)S(1)} %collective-permute-done.14.refs_1_), custom_call_target="tpu_custom_call" | custom-call | flops 131072 | bytes 262144 | tf_op jit(solution)/shard_map/finish/pallas_call | solution.py:313
  (13 shorter events, 0.1 us)
Async XLA Ops:
  10.7 5.7 %collective-permute-start = (bf16[272,128]{1,0:T(8,128)(2,1)S(1)}, bf16[272,128]{1,0:T(8,128)(2,1)S(1)}, u32[]{:S(2)}, u32[]{:S(2)}) collective-permute-start(bf16[272,128]{1,0:T(8,128)(2,1)S(1)} %get-tuple-element.19), channel_id=1, source_target_pairs={{0,2},{1,3},{2,0},{3,1},{4,6},{5,7},{6,4},{7,5},{8,10},{9,11},{10,... | collective-permute-start | bytes 208904 | tf_op jit(solution)/shard_map/ppermute | solution.py:328
  13.8 7.5 %collective-permute-start.2 = (bf16[272,128]{1,0:T(8,128)(2,1)S(1)}, bf16[272,128]{1,0:T(8,128)(2,1)S(1)}, u32[]{:S(2)}, u32[]{:S(2)}) collective-permute-start(bf16[272,128]{1,0:T(8,128)(2,1)S(1)} %get-tuple-element.20), channel_id=1, source_target_pairs={{0,4},{1,5},{2,6},{3,7},{4,0},{5,1},{6,2},{7,3},{8,12},{9,13},{10,... | collective-permute-start | bytes 208904 | tf_op jit(solution)/shard_map/ppermute | solution.py:328
  16.4 6.2 %collective-permute-start.3 = (bf16[272,128]{1,0:T(8,128)(2,1)S(1)}, bf16[272,128]{1,0:T(8,128)(2,1)S(1)}, u32[]{:S(2)}, u32[]{:S(2)}) collective-permute-start(bf16[272,128]{1,0:T(8,128)(2,1)S(1)} %get-tuple-element.21), channel_id=1, source_target_pairs={{0,6},{1,7},{2,4},{3,5},{4,2},{5,3},{6,0},{7,1},{8,14},{9,15},{10,... | collective-permute-start | bytes 208904 | tf_op jit(solution)/shard_map/ppermute | solution.py:328
  16.4 6.2 %collective-permute-start.4 = (bf16[544,128]{1,0:T(8,128)(2,1)S(1)}, bf16[544,128]{1,0:T(8,128)(2,1)S(1)}, u32[]{:S(2)}, u32[]{:S(2)}) collective-permute-start(bf16[544,128]{1,0:T(8,128)(2,1)S(1)} %constant_dynamic-update-slice_fusion.refs_0_), channel_id=1, source_target_pairs={{0,1},{1,0},{2,3},{3,2},{4,5},{5,4},{6,7},{7,6},{8,9},{9,8},{10,11... | collective-permute-start | bytes 417800 | tf_op jit(solution)/shard_map/ppermute | solution.py:328
  16.5 9.2 %collective-permute-start.5 = (bf16[544,128]{1,0:T(8,128)(2,1)S(1)}, bf16[544,128]{1,0:T(8,128)(2,1)S(1)}, u32[]{:S(2)}, u32[]{:S(2)}) collective-permute-start(bf16[544,128]{1,0:T(8,128)(2,1)S(1)} %constant_dynamic-update-slice_fusion.refs_0_), channel_id=1, source_target_pairs={{0,8},{8,0},{16,24},{24,16},{1,9},{9,1},{17,25},{25,17},{2,10},{10... | collective-permute-start | bytes 417800 | tf_op jit(solution)/shard_map/ppermute | solution.py:328
  18.3 7.4 %collective-permute-start.1 = (bf16[544,128]{1,0:T(8,128)(2,1)S(1)}, bf16[544,128]{1,0:T(8,128)(2,1)S(1)}, u32[]{:S(2)}, u32[]{:S(2)}) collective-permute-start(bf16[544,128]{1,0:T(8,128)(2,1)S(1)} %constant_dynamic-update-slice_fusion.refs_0_), channel_id=1, source_target_pairs={{0,16},{8,24},{16,0},{24,8},{1,17},{9,25},{17,1},{25,9},{2,18},{10... | collective-permute-start | bytes 417800 | tf_op jit(solution)/shard_map/ppermute | solution.py:328
  22.6 5.1 %collective-permute-start.7 = (bf16[544,128]{1,0:T(8,128)(2,1)S(1)}, bf16[544,128]{1,0:T(8,128)(2,1)S(1)}, u32[]{:S(2)}, u32[]{:S(2)}) collective-permute-start(bf16[544,128]{1,0:T(8,128)(2,1)S(1)} %pad_maximum_fusion.refs_5_), channel_id=1, source_target_pairs={{0,16},{8,24},{16,0},{24,8},{1,17},{9,25},{17,1},{25,9},{2,18},{10... | collective-permute-start | bytes 417800 | tf_op jit(solution)/shard_map/ppermute | solution.py:328
  24.2 5.1 %collective-permute-start.10 = (bf16[544,128]{1,0:T(8,128)(2,1)S(1)}, bf16[544,128]{1,0:T(8,128)(2,1)S(1)}, u32[]{:S(2)}, u32[]{:S(2)}) collective-permute-start(bf16[544,128]{1,0:T(8,128)(2,1)S(1)} %pad_maximum_fusion.refs_5_), channel_id=1, source_target_pairs={{0,8},{8,0},{16,24},{24,16},{1,9},{9,1},{17,25},{25,17},{2,10},{10... | collective-permute-start | bytes 417800 | tf_op jit(solution)/shard_map/ppermute | solution.py:328
  25.7 3.6 %collective-permute-start.8 = (bf16[544,128]{1,0:T(8,128)(2,1)S(1)}, bf16[544,128]{1,0:T(8,128)(2,1)S(1)}, u32[]{:S(2)}, u32[]{:S(2)}) collective-permute-start(bf16[544,128]{1,0:T(8,128)(2,1)S(1)} %pad_maximum_fusion.refs_5_), channel_id=1, source_target_pairs={{0,1},{1,0},{2,3},{3,2},{4,5},{5,4},{6,7},{7,6},{8,9},{9,8},{10,11... | collective-permute-start | bytes 417800 | tf_op jit(solution)/shard_map/ppermute | solution.py:328
  25.7 3.6 %collective-permute-start.6 = (bf16[544,128]{1,0:T(8,128)(2,1)S(1)}, bf16[544,128]{1,0:T(8,128)(2,1)S(1)}, u32[]{:S(2)}, u32[]{:S(2)}) collective-permute-start(bf16[544,128]{1,0:T(8,128)(2,1)S(1)} %collective-permute-done.1.refs_1_), channel_id=1, source_target_pairs={{0,1},{1,0},{2,3},{3,2},{4,5},{5,4},{6,7},{7,6},{8,9},{9,8},{10,11... | collective-permute-start | bytes 417800 | tf_op jit(solution)/shard_map/ppermute | solution.py:328
  27.7 1.5 %collective-permute-start.9 = (bf16[544,128]{1,0:T(8,128)(2,1)S(1)}, bf16[544,128]{1,0:T(8,128)(2,1)S(1)}, u32[]{:S(2)}, u32[]{:S(2)}) collective-permute-start(bf16[544,128]{1,0:T(8,128)(2,1)S(1)} %collective-permute-done.7.refs_6_), channel_id=1, source_target_pairs={{0,1},{1,0},{2,3},{3,2},{4,5},{5,4},{6,7},{7,6},{8,9},{9,8},{10,11... | collective-permute-start | bytes 417800 | tf_op jit(solution)/shard_map/ppermute | solution.py:328
  30.0 6.9 %collective-permute-start.11 = (bf16[64,512]{1,0:T(8,128)(2,1)S(1)}, bf16[64,512]{1,0:T(8,128)(2,1)S(1)}, u32[]{:S(2)}, u32[]{:S(2)}) collective-permute-start(bf16[64,512]{1,0:T(8,128)(2,1)S(1)} %get-tuple-element.26), channel_id=1, source_target_pairs={{0,6},{1,7},{2,4},{3,5},{4,2},{5,3},{6,0},{7,1},{8,14},{9,15},{10,... | collective-permute-start | bytes 196616 | tf_op jit(solution)/shard_map/ppermute | solution.py:328
  33.3 5.6 %collective-permute-start.12 = (bf16[64,512]{1,0:T(8,128)(2,1)S(1)}, bf16[64,512]{1,0:T(8,128)(2,1)S(1)}, u32[]{:S(2)}, u32[]{:S(2)}) collective-permute-start(bf16[64,512]{1,0:T(8,128)(2,1)S(1)} %get-tuple-element.27), channel_id=1, source_target_pairs={{0,4},{1,5},{2,6},{3,7},{4,0},{5,1},{6,2},{7,3},{8,12},{9,13},{10,... | collective-permute-start | bytes 196616 | tf_op jit(solution)/shard_map/ppermute | solution.py:328
  33.3 5.8 %collective-permute-start.13 = (bf16[64,512]{1,0:T(8,128)(2,1)S(1)}, bf16[64,512]{1,0:T(8,128)(2,1)S(1)}, u32[]{:S(2)}, u32[]{:S(2)}) collective-permute-start(bf16[64,512]{1,0:T(8,128)(2,1)S(1)} %get-tuple-element.28), channel_id=1, source_target_pairs={{0,2},{1,3},{2,0},{3,1},{4,6},{5,7},{6,4},{7,5},{8,10},{9,11},{10,... | collective-permute-start | bytes 196616 | tf_op jit(solution)/shard_map/ppermute | solution.py:328
  39.2 4.0 %collective-permute-start.14 = (bf16[32,512]{1,0:T(8,128)(2,1)S(1)}, bf16[32,512]{1,0:T(8,128)(2,1)S(1)}, u32[]{:S(2)}, u32[]{:S(2)}) collective-permute-start(bf16[32,512]{1,0:T(8,128)(2,1)S(1)} %get-tuple-element.30), channel_id=1, source_target_pairs={{0,8},{8,0},{16,24},{24,16},{1,9},{9,1},{17,25},{25,17},{2,10},{10... | collective-permute-start | bytes 98312 | tf_op jit(solution)/shard_map/ppermute | solution.py:328
